TPU v7x, 32 devices: a whole 2x2x4 slice. The times are simulated.
32 devices in a mesh: dp: 8 (over y, x, core), mp: 4 (over z).
Axes of the slice: x: 2, y: 2, z: 4, core: 2. Of those that a mesh axis runs over, the one named last changes fastest.
Arguments:
- tokens: bfloat16 [8, 2048, 1024], P(None, ('mp', 'dp')), may hold values from -6 to 6
- out_grad: bfloat16 [8, 2048, 1024], P(None, ('mp', 'dp')), may hold values from -6 to 6
- seq_lengths: int32 [8], replicated, may hold values from 1024 to 2048, as said below
- mix_gain: float32 [1024], replicated, may hold values from 0.1 to 1.9
- w_query: bfloat16 [1024, 1024], P('dp', 'mp'), may hold values from -0.1875 to 0.1875
- w_key: bfloat16 [1024, 1024], P('dp', 'mp'), may hold values from -0.1875 to 0.1875
- w_value: bfloat16 [1024, 2048], P('dp', 'mp'), may hold values from -0.1875 to 0.1875
- w_outgate: bfloat16 [1024, 2048], P('dp', 'mp'), may hold values from -0.1875 to 0.1875
- w_decay: bfloat16 [1024, 8], P('dp', 'mp'), may hold values from -0.1875 to 0.1875
- w_beta: bfloat16 [1024, 8], P('dp', 'mp'), may hold values from -0.1875 to 0.1875
- conv_weight: float32 [4, 4096], replicated, may hold values from -2.5 to 2.5
- rate_log: float32 [8], replicated, may hold values from 0 to 2.77
- step_bias: float32 [8], replicated, may hold values from -14 to -2.3
- head_gain: float32 [256], replicated, may hold values from 0.1 to 1.9
- w_out: bfloat16 [1024, 2048], P('dp', 'mp'), may hold values from -0.1875 to 0.1875
- ffn_gain: float32 [1024], replicated, may hold values from 0.1 to 1.9
- w_ffn_gate: bfloat16 [1024, 2816], P('dp', 'mp'), may hold values from -0.1875 to 0.1875
- w_ffn_up: bfloat16 [1024, 2816], P('dp', 'mp'), may hold values from -0.1875 to 0.1875
- w_ffn_down: bfloat16 [1024, 2816], P('dp', 'mp'), may hold values from -0.15625 to 0.15625
Outputs:
- block_out: bfloat16 [8, 2048, 1024], P(None, ('mp', 'dp'))
- input_grad: bfloat16 [8, 2048, 1024], P(None, ('mp', 'dp'))
- mix_gain_grad: float32 [1024], replicated
- w_query_grad: float32 [1024, 1024], P('dp', 'mp')
- w_key_grad: float32 [1024, 1024], P('dp', 'mp')
- w_value_grad: float32 [1024, 2048], P('dp', 'mp')
- w_outgate_grad: float32 [1024, 2048], P('dp', 'mp')
- w_decay_grad: float32 [1024, 8], P('dp', 'mp')
- w_beta_grad: float32 [1024, 8], P('dp', 'mp')
- conv_weight_grad: float32 [4, 4096], replicated
- rate_log_grad: float32 [8], replicated
- step_bias_grad: float32 [8], replicated
- head_gain_grad: float32 [256], replicated
- w_out_grad: float32 [1024, 2048], P('dp', 'mp')
- ffn_gain_grad: float32 [1024], replicated
- w_ffn_gate_grad: float32 [1024, 2816], P('dp', 'mp')
- w_ffn_up_grad: float32 [1024, 2816], P('dp', 'mp')
- w_ffn_down_grad: float32 [1024, 2816], P('dp', 'mp')
Inputs may be any that keep to these rules, and one draw needn't show every extreme that they name: `seq_lengths`: one length per sequence; positions from the length on are padding; some sequence has length 2048 and some 1024.
All inputs are finite; a program needn't handle non-finite values.
Results may differ from a plain program's by a relative error of at most 0.015.
The roundings to bfloat16 on the way count: a program that leaves them out, or rounds other values in their place, can miss the bound.
Values may be sent and summed in bfloat16 or wider, within the bound.
A program may use at most 320 MiB of HBM per device.

v0:
```python
from functools import partial

import jax
import jax.numpy as jnp
from jax import lax
from jax.sharding import PartitionSpec as P

H = 8
DK = 128
SPAN = 64


def rms_scale(value_vectors, gain):
    return (
        value_vectors
        * lax.rsqrt(jnp.mean(value_vectors * value_vectors, axis=-1, keepdims=True) + 1e-05)
        * gain
    )


def short_conv(raw_input, weights):
    tap_count = weights.shape[0]
    length = raw_input.shape[1]
    padded = jnp.pad(raw_input, ((0, 0), (tap_count - 1, 0), (0, 0)))
    summed = weights[0] * padded[:, 0:length]
    for offset in range(1, tap_count):
        summed = summed + weights[offset] * padded[:, offset : offset + length]
    return summed


def spanned_rule(query_vectors, key_vectors, value_vectors, write_strength, log_decay, block_size):
    seq_count, length, head_count, key_size = query_vectors.shape
    value_size = value_vectors.shape[-1]
    blocks = length // block_size

    def blocked(source):
        shaped = source.reshape((seq_count, blocks, block_size, head_count) + source.shape[3:])
        return jnp.moveaxis(shaped, 3, 1)

    query_b = blocked(query_vectors)
    keyed_b = blocked(key_vectors)
    value_b = blocked(value_vectors)
    beta_b = blocked(write_strength)
    cumulative = jnp.cumsum(blocked(log_decay), axis=-1)
    row_ids = lax.broadcasted_iota(jnp.int32, (block_size, block_size), 0)
    col_ids = lax.broadcasted_iota(jnp.int32, (block_size, block_size), 1)
    strict = row_ids > col_ids
    inclusive = row_ids >= col_ids
    spread = cumulative[..., :, None] - cumulative[..., None, :]
    fade_strict = jnp.where(strict, jnp.exp(jnp.where(strict, spread, 0.0)), 0.0)
    fade_incl = jnp.where(inclusive, jnp.exp(jnp.where(inclusive, spread, 0.0)), 0.0)
    key_gram = jnp.einsum("shncd,shnmd->shncm", keyed_b, keyed_b, precision=lax.Precision.HIGHEST)
    lower = jnp.eye(block_size, dtype=jnp.float32) + beta_b[..., :, None] * key_gram * fade_strict
    growth = jnp.exp(cumulative)
    rhs_side = jnp.concatenate(
        [(beta_b * growth)[..., None] * keyed_b, beta_b[..., None] * value_b], axis=-1
    )
    solved = jax.scipy.linalg.solve_triangular(lower, rhs_side, lower=True, unit_diagonal=True)
    w_block = solved[..., :key_size]
    u_block = solved[..., key_size:]
    scores = (
        jnp.einsum("shncd,shnmd->shncm", query_b, keyed_b, precision=lax.Precision.HIGHEST)
        * fade_incl
    )
    query_g = query_b * growth[..., None]
    last_sum = cumulative[..., -1:]
    keyed_g = keyed_b * jnp.exp(last_sum - cumulative)[..., None]

    def advance(state, item):
        w_part, u_part, score_part, query_part, keyed_part, last_part = item
        fresh = u_part - jnp.einsum(
            "shcd,shde->shce", w_part, state, precision=lax.Precision.HIGHEST
        )
        result = jnp.einsum("shcd,shde->shce", query_part, state, precision=lax.Precision.HIGHEST)
        result = result + jnp.einsum(
            "shcm,shme->shce", score_part, fresh, precision=lax.Precision.HIGHEST
        )
        state = jnp.exp(last_part)[..., None] * state
        state = state + jnp.einsum(
            "shcd,shce->shde", keyed_part, fresh, precision=lax.Precision.HIGHEST
        )
        return (state, result)

    items = tuple(
        (
            jnp.moveaxis(member, 2, 0)
            for member in (w_block, u_block, scores, query_g, keyed_g, last_sum)
        )
    )
    start_state = jnp.zeros((seq_count, head_count, key_size, value_size), jnp.float32)
    final_state, results = lax.scan(advance, start_state, items)
    ordered = jnp.transpose(results, (1, 0, 3, 2, 4))
    return ordered.reshape(seq_count, length, head_count, value_size)


def mixer_core(
    projected_rows,
    conv_query,
    conv_keyed,
    conv_value,
    rate_local,
    bias_local,
    gain_head,
    block_size,
):
    key_cols = conv_query.shape[1]
    value_cols = conv_value.shape[1]
    head_count = rate_local.shape[0]
    seq_count = projected_rows.shape[0]
    length = projected_rows.shape[1]
    key_size = key_cols // head_count
    value_size = value_cols // head_count
    start_gate = 2 * key_cols + value_cols
    start_decay = start_gate + value_cols
    query_raw = projected_rows[..., :key_cols]
    keyed_raw = projected_rows[..., key_cols : 2 * key_cols]
    value_raw = projected_rows[..., 2 * key_cols : start_gate]
    gate_raw = projected_rows[..., start_gate:start_decay]
    decay_raw = projected_rows[..., start_decay : start_decay + head_count]
    beta_raw = projected_rows[..., start_decay + head_count : start_decay + 2 * head_count]
    query_vectors = jax.nn.silu(short_conv(query_raw, conv_query)).reshape(
        seq_count, length, head_count, key_size
    )
    key_vectors = jax.nn.silu(short_conv(keyed_raw, conv_keyed)).reshape(
        seq_count, length, head_count, key_size
    )
    value_vectors = jax.nn.silu(short_conv(value_raw, conv_value)).reshape(
        seq_count, length, head_count, value_size
    )
    query_vectors = (
        query_vectors
        * lax.rsqrt(jnp.sum(query_vectors * query_vectors, axis=-1, keepdims=True) + 1e-06)
        * key_size ** (-0.5)
    )
    key_vectors = key_vectors * lax.rsqrt(
        jnp.sum(key_vectors * key_vectors, axis=-1, keepdims=True) + 1e-06
    )
    write_strength = jax.nn.sigmoid(beta_raw)
    log_decay = -jnp.exp(rate_local) * jax.nn.softplus(decay_raw + bias_local)
    mixed = spanned_rule(
        query_vectors, key_vectors, value_vectors, write_strength, log_decay, block_size
    )
    gated = rms_scale(mixed, gain_head) * jax.nn.silu(
        gate_raw.reshape(seq_count, length, head_count, value_size)
    )
    return gated.reshape(seq_count, length, value_cols)


def per_device(
    tokens,
    out_grad,
    seq_lengths,
    mix_gain,
    w_query,
    w_key,
    w_value,
    w_outgate,
    w_decay,
    w_beta,
    conv_weight,
    rate_log,
    step_bias,
    head_gain,
    w_out,
    ffn_gain,
    w_ffn_gate,
    w_ffn_up,
    w_ffn_down,
):
    groups = lax.axis_size("dp")
    group_index = lax.axis_index("dp")
    share_index = lax.axis_index("mp")
    seq_count = seq_lengths.shape[0]
    per_group = seq_count // groups
    ranked = jnp.argsort(-seq_lengths, stable=True)
    rank_ids = jnp.arange(seq_count, dtype=jnp.int32)
    rounds = rank_ids // groups
    column = rank_ids % groups
    target = jnp.where(rounds % 2 == 0, column, groups - 1 - column)
    slot_of = target * per_group + rounds
    dealt_order = jnp.zeros((seq_count,), jnp.int32).at[slot_of].set(ranked)
    inverse = jnp.zeros((seq_count,), jnp.int32).at[dealt_order].set(rank_ids)
    local_tokens, local_grad = (
        lax.all_to_all(
            jnp.take(tokens, dealt_order, axis=0), "dp", split_axis=0, concat_axis=1, tiled=True
        ),
        lax.all_to_all(
            jnp.take(out_grad, dealt_order, axis=0), "dp", split_axis=0, concat_axis=1, tiled=True
        ),
    )
    mine = lax.dynamic_slice_in_dim(dealt_order, group_index * per_group, per_group)
    my_lengths = jnp.take(seq_lengths, mine)
    part_len = local_tokens.shape[1]
    positions = share_index * part_len + jnp.arange(part_len, dtype=jnp.int32)
    live_part = (positions[None, :] < my_lengths[:, None]).astype(jnp.float32)[..., None]
    residual = local_tokens.astype(jnp.float32)
    upstream = live_part * local_grad.astype(jnp.float32)
    (
        g_query,
        g_key,
        g_value,
        g_outgate,
        g_decay,
        g_beta,
        output_weight_gradient,
        gate_weight_gradient,
        up_weight_gradient,
        down_weight_gradient,
    ) = (
        lax.all_gather(w_query, "dp", axis=0, tiled=True),
        lax.all_gather(w_key, "dp", axis=0, tiled=True),
        lax.all_gather(w_value, "dp", axis=0, tiled=True),
        lax.all_gather(w_outgate, "dp", axis=0, tiled=True),
        lax.all_gather(w_decay, "dp", axis=0, tiled=True),
        lax.all_gather(w_beta, "dp", axis=0, tiled=True),
        lax.all_gather(w_out, "dp", axis=0, tiled=True),
        lax.all_gather(w_ffn_gate, "dp", axis=0, tiled=True),
        lax.all_gather(w_ffn_up, "dp", axis=0, tiled=True),
        lax.all_gather(w_ffn_down, "dp", axis=0, tiled=True),
    )
    key_cols = g_query.shape[1]
    value_cols = g_value.shape[1]
    heads_local = g_decay.shape[1]
    normed_one, norm_one_back = jax.vjp(rms_scale, residual, mix_gain)
    mixer_input, layer_output_gradient = (
        lax.all_gather(normed_one.astype(jnp.bfloat16), "mp", axis=1, tiled=True),
        lax.all_gather(upstream.astype(jnp.bfloat16), "mp", axis=1, tiled=True),
    )
    joined_weight = jnp.concatenate([g_query, g_key, g_value, g_outgate, g_decay, g_beta], axis=1)
    projected_rows = jnp.einsum(
        "tjx,xq->tjq", mixer_input, joined_weight, preferred_element_type=jnp.float32
    )
    conv_query = lax.dynamic_slice_in_dim(conv_weight, share_index * key_cols, key_cols, 1)
    conv_keyed = lax.dynamic_slice_in_dim(conv_weight, H * DK + share_index * key_cols, key_cols, 1)
    conv_value = lax.dynamic_slice_in_dim(
        conv_weight, 2 * H * DK + share_index * value_cols, value_cols, 1
    )
    rate_local = lax.dynamic_slice_in_dim(rate_log, share_index * heads_local, heads_local)
    bias_local = lax.dynamic_slice_in_dim(step_bias, share_index * heads_local, heads_local)
    core = partial(mixer_core, block_size=SPAN)
    head_out, core_back = jax.vjp(
        core, projected_rows, conv_query, conv_keyed, conv_value, rate_local, bias_local, head_gain
    )
    head_lower_precision = head_out.astype(jnp.bfloat16)
    mixer_pieces = jnp.einsum(
        "gez,mz->gem",
        head_lower_precision,
        output_weight_gradient,
        preferred_element_type=jnp.float32,
    )
    mixed = lax.psum_scatter(mixer_pieces, "mp", scatter_dimension=1, tiled=True)
    after_mix = residual + mixed
    normed_two, norm_two_back = jax.vjp(rms_scale, after_mix, ffn_gain)
    feedforward_input = lax.all_gather(normed_two.astype(jnp.bfloat16), "mp", axis=1, tiled=True)
    gate_activation = jnp.einsum(
        "vhr,rw->vhw", feedforward_input, gate_weight_gradient, preferred_element_type=jnp.float32
    )
    up_activation = jnp.einsum(
        "vhr,rw->vhw", feedforward_input, up_weight_gradient, preferred_element_type=jnp.float32
    )
    sigmoid_gate = jax.nn.sigmoid(gate_activation)
    silu_activation = (gate_activation * sigmoid_gate * up_activation).astype(jnp.bfloat16)
    feedforward_pieces = jnp.einsum(
        "omw,cw->omc", silu_activation, down_weight_gradient, preferred_element_type=jnp.float32
    )
    ffn_result = lax.psum_scatter(
        feedforward_pieces.astype(jnp.bfloat16), "mp", scatter_dimension=1, tiled=True
    ).astype(jnp.float32)
    block_output = (live_part * (after_mix + ffn_result)).astype(jnp.bfloat16)
    activation_gradient = jnp.einsum(
        "vhr,rw->vhw",
        layer_output_gradient,
        down_weight_gradient,
        preferred_element_type=jnp.float32,
    )
    grad_down = jnp.einsum(
        "itg,ity->gy", layer_output_gradient, silu_activation, preferred_element_type=jnp.float32
    )
    gate_gradient = (
        activation_gradient
        * up_activation
        * sigmoid_gate
        * (1.0 + gate_activation * (1.0 - sigmoid_gate))
    ).astype(jnp.bfloat16)
    up_gradient = (activation_gradient * gate_activation * sigmoid_gate).astype(jnp.bfloat16)
    gate_input_gradient = jnp.einsum(
        "itg,ity->gy", feedforward_input, gate_gradient, preferred_element_type=jnp.float32
    )
    up_input_gradient = jnp.einsum(
        "itg,ity->gy", feedforward_input, up_gradient, preferred_element_type=jnp.float32
    )
    backward_pieces = jnp.einsum(
        "omw,cw->omc", gate_gradient, gate_weight_gradient, preferred_element_type=jnp.float32
    )
    backward_pieces = backward_pieces + jnp.einsum(
        "omw,cw->omc", up_gradient, up_weight_gradient, preferred_element_type=jnp.float32
    )
    d_normed_two = lax.psum_scatter(backward_pieces, "mp", scatter_dimension=1, tiled=True)
    d_after, d_ffn_gain = norm_two_back(d_normed_two)
    d_after = d_after + upstream
    mixer_output_gradient = lax.all_gather(d_after.astype(jnp.bfloat16), "mp", axis=1, tiled=True)
    head_gradient = jnp.einsum(
        "tjx,xq->tjq",
        mixer_output_gradient,
        output_weight_gradient,
        preferred_element_type=jnp.float32,
    )
    grad_out = jnp.einsum(
        "wzi,wzt->it",
        mixer_output_gradient,
        head_lower_precision,
        preferred_element_type=jnp.float32,
    )
    d_projected, d_conv_query, d_conv_keyed, d_conv_value, d_rate, d_bias, d_head_gain = core_back(
        head_gradient
    )
    projection_gradient_lower = d_projected.astype(jnp.bfloat16)
    input_pieces = jnp.einsum(
        "gez,mz->gem", projection_gradient_lower, joined_weight, preferred_element_type=jnp.float32
    )
    grad_joined = jnp.einsum(
        "wzi,wzt->it", mixer_input, projection_gradient_lower, preferred_element_type=jnp.float32
    )
    d_normed_one = lax.psum_scatter(
        input_pieces.astype(jnp.bfloat16), "mp", scatter_dimension=1, tiled=True
    ).astype(jnp.float32)
    d_input, d_mix_gain = norm_one_back(d_normed_one)
    d_input = d_input + d_after
    start_gate = 2 * key_cols + value_cols
    start_decay = start_gate + value_cols
    grad_query = grad_joined[:, :key_cols]
    grad_key = grad_joined[:, key_cols : 2 * key_cols]
    grad_value = grad_joined[:, 2 * key_cols : start_gate]
    grad_outgate = grad_joined[:, start_gate:start_decay]
    grad_decay = grad_joined[:, start_decay : start_decay + heads_local]
    grad_beta = grad_joined[:, start_decay + heads_local : start_decay + 2 * heads_local]
    weight_summed = (
        lax.psum_scatter(grad_query, "dp", scatter_dimension=0, tiled=True),
        lax.psum_scatter(grad_key, "dp", scatter_dimension=0, tiled=True),
        lax.psum_scatter(grad_value, "dp", scatter_dimension=0, tiled=True),
        lax.psum_scatter(grad_outgate, "dp", scatter_dimension=0, tiled=True),
        lax.psum_scatter(grad_decay, "dp", scatter_dimension=0, tiled=True),
        lax.psum_scatter(grad_beta, "dp", scatter_dimension=0, tiled=True),
        lax.psum_scatter(grad_out, "dp", scatter_dimension=0, tiled=True),
        lax.psum_scatter(gate_input_gradient, "dp", scatter_dimension=0, tiled=True),
        lax.psum_scatter(up_input_gradient, "dp", scatter_dimension=0, tiled=True),
        lax.psum_scatter(grad_down, "dp", scatter_dimension=0, tiled=True),
    )
    conv_full = jnp.zeros(conv_weight.shape, jnp.float32)
    conv_full = lax.dynamic_update_slice_in_dim(conv_full, d_conv_query, share_index * key_cols, 1)
    conv_full = lax.dynamic_update_slice_in_dim(
        conv_full, d_conv_keyed, H * DK + share_index * key_cols, 1
    )
    conv_full = lax.dynamic_update_slice_in_dim(
        conv_full, d_conv_value, 2 * H * DK + share_index * value_cols, 1
    )
    rate_full = lax.dynamic_update_slice_in_dim(
        jnp.zeros(rate_log.shape, jnp.float32), d_rate, share_index * heads_local, 0
    )
    bias_full = lax.dynamic_update_slice_in_dim(
        jnp.zeros(step_bias.shape, jnp.float32), d_bias, share_index * heads_local, 0
    )
    sum_mix_gain, sum_ffn_gain, sum_head_gain, sum_conv, sum_rate, sum_bias = lax.psum(
        (d_mix_gain, d_ffn_gain, d_head_gain, conv_full, rate_full, bias_full), ("dp", "mp")
    )
    returned_out, returned_grad = (
        lax.all_to_all(block_output, "dp", split_axis=1, concat_axis=0, tiled=True),
        lax.all_to_all(d_input.astype(jnp.bfloat16), "dp", split_axis=1, concat_axis=0, tiled=True),
    )
    final_out = jnp.take(returned_out, inverse, axis=0)
    final_grad = jnp.take(returned_grad, inverse, axis=0)
    (
        sum_query,
        sum_key,
        sum_value,
        sum_outgate,
        sum_decay,
        sum_beta,
        sum_out,
        sum_gate,
        sum_up,
        sum_down,
    ) = weight_summed
    return (
        final_out,
        final_grad,
        sum_mix_gain,
        sum_query,
        sum_key,
        sum_value,
        sum_outgate,
        sum_decay,
        sum_beta,
        sum_conv,
        sum_rate,
        sum_bias,
        sum_head_gain,
        sum_out,
        sum_ffn_gain,
        sum_gate,
        sum_up,
        sum_down,
    )


def solution(mesh):
    return jax.shard_map(
        per_device,
        mesh=mesh,
        in_specs=(
            P(None, ("mp", "dp"), None),
            P(None, ("mp", "dp"), None),
            P(),
            P(),
            P("dp", "mp"),
            P("dp", "mp"),
            P("dp", "mp"),
            P("dp", "mp"),
            P("dp", "mp"),
            P("dp", "mp"),
            P(),
            P(),
            P(),
            P(),
            P("dp", "mp"),
            P(),
            P("dp", "mp"),
            P("dp", "mp"),
            P("dp", "mp"),
        ),
        out_specs=(
            P(None, ("mp", "dp"), None),
            P(None, ("mp", "dp"), None),
            P(),
            P("dp", "mp"),
            P("dp", "mp"),
            P("dp", "mp"),
            P("dp", "mp"),
            P("dp", "mp"),
            P("dp", "mp"),
            P(),
            P(),
            P(),
            P(),
            P("dp", "mp"),
            P(),
            P("dp", "mp"),
            P("dp", "mp"),
            P("dp", "mp"),
        ),
        check_vma=False,
    )
```

profile of v0, /device:TPU:0, one launch (start us, length us, event | category | flops | bytes accessed | tf_op | source)
XLA Modules:
  0.0 2776.7 jit_solution(11327948872262366101)
XLA Ops:
  14.1 21.8 all_to_all.42
  85.4 63.2 %all-gather.11.cloned.1.call-done = bf16[1,2048,1024]{2,1,0:T(8,128)(2,1)} async-done(((bf16[1,512,1024]{2,1,0:T(8,128)(2,1)}), bf16[1,2048,1024]{2,1,0:T(8,128)(2,1)}) %all-gather.11.cloned.1.call-update) | async-done | bytes 4194320 | tf_op jit(solution)/shard_map/all_gather | solution.py:226
  226.8 134.0 %custom-call.10 = f32[2,32,1,64,64]{1,3,4,2,0:T(8,128)} custom-call(f32[2,32,1,64,64]{1,4,3,2,0:T(8,128)} %get-tuple-element.940), custom_call_target="InvertDiagBlocksLowerTriangular" | custom-call | tf_op jit(solution)/shard_map/jvp(jit(_solve_triangular))/vmap(vmap())/triangular_solve | solution.py:58
  425.0 221.8 %while.49 = (s32[]{:T(128)}, f32[1,2,128,256]{3,2,1,0:T(8,128)S(1)}, f32[32,1,2,64,256]{4,2,3,0,1:T(2,128)}, f32[32,1,2,128,256]{4,3,2,1,0:T(8,128)}, f32[32,1,2...) while((s32[]{:T(128)}, ...), condition=%wide.region_7.9_spmd.clone, body=%wide.region_6.8_spmd.clone.sunk | while | flops 176619520 | bytes 3150021 | solution.py:91
  677.6 142.5 %reduce-scatter.19.cloned.1.call-done = f32[1,512,1024]{2,1,0:T(8,128)} async-done(((f32[1,2048,1024]{2,1,0:T(8,128)}), f32[1,512,1024]{2,1,0:T(8,128)}) %reduce-scatter.19.cloned.1.call-update) | async-done | bytes 2097168 | tf_op jit(solution)/shard_map/reduce_scatter | solution.py:251
  852.6 82.9 %all-gather.19.cloned.1.call-done = bf16[1,2048,1024]{2,1,0:T(8,128)(2,1)} async-done(((bf16[1,512,1024]{2,1,0:T(8,128)(2,1)}), bf16[1,2048,1024]{2,1,0:T(8,128)(2,1)}) %all-gather.19.cloned.1.call-update) | async-done | bytes 4194320 | tf_op jit(solution)/shard_map/all_gather | solution.py:254
  943.8 17.5 all-gather.21.cloned.1.call-done
  969.6 18.9 all-gather.25.cloned.1.call-done
  988.5 82.8 %all-gather.27.cloned.1.call-done = bf16[1,2048,1024]{2,1,0:T(8,128)(2,1)} async-done(((bf16[1,512,1024]{2,1,0:T(8,128)(2,1)}), bf16[1,2048,1024]{2,1,0:T(8,128)(2,1)}) %all-gather.27.cloned.1.call-update) | async-done | bytes 4194320 | tf_op jit(solution)/shard_map/all_gather | solution.py:227
  1101.3 134.8 %reduce-scatter.23.cloned.1.call-done = f32[1,512,1024]{2,1,0:T(8,128)} async-done(((f32[1,2048,1024]{2,1,0:T(8,128)}), f32[1,512,1024]{2,1,0:T(8,128)}) %reduce-scatter.23.cloned.1.call-update) | async-done | bytes 2097168 | tf_op jit(solution)/shard_map/reduce_scatter | solution.py:298
  1238.8 76.9 %reduce-scatter.21.cloned.1.call-done = bf16[1,512,1024]{2,1,0:T(8,128)(2,1)} async-done(((bf16[1,2048,1024]{2,1,0:T(8,128)(2,1)}), bf16[1,512,1024]{2,1,0:T(8,128)(2,1)}) %reduce-scatter.21.cloned.1.call-update) | async-done | bytes 1048592 | tf_op jit(solution)/shard_map/reduce_scatter | solution.py:266
  1352.6 49.4 %all-gather.29.cloned.1.call-done = bf16[1,2048,1024]{2,1,0:T(8,128)(2,1)} async-done(((bf16[1,512,1024]{2,1,0:T(8,128)(2,1)}), bf16[1,2048,1024]{2,1,0:T(8,128)(2,1)}) %all-gather.29.cloned.1.call-update) | async-done | bytes 4194320 | tf_op jit(solution)/shard_map/all_gather | solution.py:301
  1449.1 480.7 %while.50 = (s32[]{:T(128)}, f32[1,2,128,256]{2,3,1,0:T(8,128)S(1)}, f32[32,1,2,64,128]{4,3,2,1,0:T(8,128)}, f32[32,1,2,64,256]{4,3,2,1,0:T(8,128)}, f32[32,1,2,...) while((s32[]{:T(128)}, ...), condition=%wide.region_18.20_spmd.clone, body=%wide.region_16.19_spmd.clone.sunk | while | flops 353009664 | bytes 6036753 | solution.py:91
  2064.6 18.4 multiply_reduce_fusion.3
  2247.1 35.9 %reduce-scatter.43.cloned.1.call-done = f32[128,2]{1,0:T(8,128)} async-done(((f32[1024,2]{1,0:T(8,128)}), f32[128,2]{1,0:T(8,128)}) %reduce-scatter.43.cloned.1.call-update) | async-done | bytes 1040
  2284.5 37.6 %reduce-scatter.29.cloned.1.call-done = f32[128,256]{0,1:T(8,128)} async-done(((f32[1024,256]{0,1:T(8,128)}), f32[128,256]{0,1:T(8,128)}) %reduce-scatter.29.cloned.1.call-update) | async-done | bytes 131088 | tf_op jit(solution)/shard_map/reduce_scatter | solution.py:339
  2323.8 37.4 %reduce-scatter.27.cloned.1.call-done = f32[128,256]{0,1:T(8,128)} async-done(((f32[1024,256]{0,1:T(8,128)}), f32[128,256]{0,1:T(8,128)}) %reduce-scatter.27.cloned.1.call-update) | async-done | bytes 131088 | tf_op jit(solution)/shard_map/reduce_scatter | solution.py:338
  2362.9 42.8 %reduce-scatter.33.cloned.1.call-done = f32[128,512]{0,1:T(8,128)} async-done(((f32[1024,512]{0,1:T(8,128)}), f32[128,512]{0,1:T(8,128)}) %reduce-scatter.33.cloned.1.call-update) | async-done | bytes 262160 | tf_op jit(solution)/shard_map/reduce_scatter | solution.py:341
  2407.5 43.0 %reduce-scatter.31.cloned.1.call-done = f32[128,512]{0,1:T(8,128)} async-done(((f32[1024,512]{0,1:T(8,128)}), f32[128,512]{0,1:T(8,128)}) %reduce-scatter.31.cloned.1.call-update) | async-done | bytes 262160 | tf_op jit(solution)/shard_map/reduce_scatter | solution.py:340
  2452.2 39.5 %all-reduce.36 = (f32[1024]{0:T(1024)}, f32[8]{0:T(128)}, f32[8]{0:T(128)}, f32[256]{0:T(256)}, f32[1024]{0:T(1024)}) all-reduce(f32[1024]{0:T(1024)S(1)} %get-tuple-element.804, f32[8]{0:T(128)S(1)} %multiply_dynamic-update-slice_fusion, f32[8]{0:T(128)S(1)} %dynamic_update_slice.94, ...), channel_id=1, replica_groups=mesh['dp'=8,'mp'=4] {'dp','mp'}, use_global_device_ids=true, to_apply=%region_33.35 | all-reduce | flops 2320 | bytes 18560 | tf_op jit(solution)/shard_map/psum | solution.py:363
  2501.0 47.7 %reduce-scatter.37.cloned.1.call-done = f32[128,704]{0,1:T(8,128)} async-done(((f32[1024,704]{0,1:T(8,128)}), f32[128,704]{0,1:T(8,128)}) %reduce-scatter.37.cloned.1.call-update) | async-done | bytes 360464 | tf_op jit(solution)/shard_map/reduce_scatter | solution.py:345
  2548.8 48.9 %reduce-scatter.39.cloned.1.call-done = f32[128,704]{0,1:T(8,128)} async-done(((f32[1024,704]{0,1:T(8,128)}), f32[128,704]{0,1:T(8,128)}) %reduce-scatter.39.cloned.1.call-update) | async-done | bytes 360464 | tf_op jit(solution)/shard_map/reduce_scatter | solution.py:346
  2597.6 124.5 %all-reduce.39.cloned.1.call-done = f32[4,4096]{1,0:T(4,128)} async-done(((f32[4,4096]{1,0:T(4,128)}), f32[4,4096]{1,0:T(4,128)}) %all-reduce.39.cloned.1.call-update) | async-done | bytes 65552 | tf_op jit(solution)/shard_map/psum | solution.py:363
  2722.1 46.3 %reduce-scatter.35.cloned.1.call-done = f32[128,512]{1,0:T(8,128)} async-done(((f32[1024,512]{1,0:T(8,128)}), f32[128,512]{1,0:T(8,128)}) %reduce-scatter.35.cloned.1.call-update) | async-done | bytes 262160 | tf_op jit(solution)/shard_map/reduce_scatter | solution.py:344
  (1267 shorter events, 1408.2 us)
Async XLA Ops:
  8.7 139.9 %all-gather.11.cloned.1.call-start = ((), (), s32[]{:S(2)}) async-start(), calls=%async_computation.18 | async-start | bytes 5242880 | tf_op jit(solution)/shard_map/all_gather | solution.py:226
  39.5 629.7 %all-gather.17.cloned.1.call-start = ((), (), s32[]{:S(2)}) async-start(), calls=%async_computation.21 | async-start | bytes 1179648 | tf_op jit(solution)/shard_map/all_gather | solution.py:216
  40.0 780.1 %reduce-scatter.19.cloned.1.call-start = ((), (), s32[]{:S(2)}) async-start(), calls=%async_computation.22 | async-start | bytes 10485760 | tf_op jit(solution)/shard_map/reduce_scatter | solution.py:251
  677.0 175.7 %all-gather.23.cloned.1.call-start = ((), (), s32[]{:S(2)}) async-start(), calls=%async_computation.25 | async-start | bytes 1622016 | tf_op jit(solution)/shard_map/all_gather | solution.py:218
  677.5 258.0 %all-gather.19.cloned.1.call-start = ((), (), s32[]{:S(2)}) async-start(), calls=%async_computation.23 | async-start | bytes 5242880 | tf_op jit(solution)/shard_map/all_gather | solution.py:254
  824.7 136.6 %all-gather.21.cloned.1.call-start = ((), (), s32[]{:S(2)}) async-start(), calls=%async_computation.24 | async-start | bytes 1622016 | tf_op jit(solution)/shard_map/all_gather | solution.py:217
  825.4 163.1 %all-gather.25.cloned.1.call-start = ((), (), s32[]{:S(2)}) async-start(), calls=%async_computation.26 | async-start | bytes 1622016 | tf_op jit(solution)/shard_map/all_gather | solution.py:219
  829.8 241.5 %all-gather.27.cloned.1.call-start = ((), (), s32[]{:S(2)}) async-start(), calls=%async_computation.28 | async-start | bytes 5242880 | tf_op jit(solution)/shard_map/all_gather | solution.py:227
  848.0 388.1 %reduce-scatter.23.cloned.1.call-start = ((), (), s32[]{:S(2)}) async-start(), calls=%async_computation.29 | async-start | bytes 10485760 | tf_op jit(solution)/shard_map/reduce_scatter | solution.py:298
  1093.0 222.8 %reduce-scatter.21.cloned.1.call-start = ((), (), s32[]{:S(2)}) async-start(), calls=%async_computation.27 | async-start | bytes 5242880 | tf_op jit(solution)/shard_map/reduce_scatter | solution.py:266
  1101.3 300.7 %all-gather.29.cloned.1.call-start = ((), (), s32[]{:S(2)}) async-start(), calls=%async_computation.30 | async-start | bytes 5242880 | tf_op jit(solution)/shard_map/all_gather | solution.py:301
  1320.5 884.1 %reduce-scatter.25.cloned.1.call-start = ((), (), s32[]{:S(2)}) async-start(), calls=%async_computation.31 | async-start | bytes 5242880 | tf_op jit(solution)/shard_map/reduce_scatter | solution.py:324
  2128.5 117.2 %reduce-scatter.45.cloned.1.call-start = ((), (), s32[]{:S(2)}) async-start(), calls=%async_computation.42 | async-start | bytes 589824
  2147.3 135.7 %reduce-scatter.43.cloned.1.call-start = ((), (), s32[]{:S(2)}) async-start(), calls=%async_computation.41 | async-start | bytes 589824
  2148.5 173.7 %reduce-scatter.29.cloned.1.call-start = ((), (), s32[]{:S(2)}) async-start(), calls=%async_computation.33 | async-start | bytes 1179648 | tf_op jit(solution)/shard_map/reduce_scatter | solution.py:339
  2151.8 209.5 %reduce-scatter.27.cloned.1.call-start = ((), (), s32[]{:S(2)}) async-start(), calls=%async_computation.32 | async-start | bytes 1179648 | tf_op jit(solution)/shard_map/reduce_scatter | solution.py:338
  2152.3 253.4 %reduce-scatter.33.cloned.1.call-start = ((), (), s32[]{:S(2)}) async-start(), calls=%async_computation.35 | async-start | bytes 2359296 | tf_op jit(solution)/shard_map/reduce_scatter | solution.py:341
  2157.3 293.2 %reduce-scatter.31.cloned.1.call-start = ((), (), s32[]{:S(2)}) async-start(), calls=%async_computation.34 | async-start | bytes 2359296 | tf_op jit(solution)/shard_map/reduce_scatter | solution.py:340
  2157.9 343.2 %reduce-scatter.41.cloned.1.call-start = ((), (), s32[]{:S(2)}) async-start(), calls=%async_computation.40 | async-start | bytes 3244032 | tf_op jit(solution)/shard_map/reduce_scatter | solution.py:347
  2165.7 383.1 %reduce-scatter.37.cloned.1.call-start = ((), (), s32[]{:S(2)}) async-start(), calls=%async_computation.38 | async-start | bytes 3244032 | tf_op jit(solution)/shard_map/reduce_scatter | solution.py:345
  2173.6 424.0 %reduce-scatter.39.cloned.1.call-start = ((), (), s32[]{:S(2)}) async-start(), calls=%async_computation.39 | async-start | bytes 3244032 | tf_op jit(solution)/shard_map/reduce_scatter | solution.py:346
  2181.5 540.7 %all-reduce.39.cloned.1.call-start = ((), (), s32[]{:S(2)}) async-start(), calls=%async_computation.36 | async-start | bytes 131072 | tf_op jit(solution)/shard_map/psum | solution.py:363
  2182.3 586.2 %reduce-scatter.35.cloned.1.call-start = ((), (), s32[]{:S(2)}) async-start(), calls=%async_computation.37 | async-start | bytes 2359296 | tf_op jit(solution)/shard_map/reduce_scatter | solution.py:344
  2220.0 271.7 %all-to-all-start.3 = ((bf16[8,2,32768]{2,1,0:T(2,128)(2,1)}), bf16[8,2,32768]{2,1,0:T(2,128)(2,1)}, u32[]{:S(2)}, u32[]{:S(2)}) async-start(bf16[8,2,32768]{2,1,0:T(2,128)(2,1)} %reshape.1795), calls=%async_computation.7 | async-start | bytes 2097152 | tf_op jit(solution)/shard_map/all_to_all | solution.py:368
  (141 other events, 6528.6 us)
Sparse Core Ops, SparseCore 0:
  9.9 29.9 all-gather.12
  41.8 23.7 all-gather.14
  67.8 80.7 all-gather.10
  677.1 142.9 reduce-scatter.18
  821.8 30.7 all-gather.22
  854.8 80.7 all-gather.18
  937.4 23.8 all-gather.20
  963.2 25.2 all-gather.24
  990.5 80.7 all-gather.26
  1093.1 142.9 reduce-scatter.22
  1238.2 77.4 reduce-scatter.20
  1320.7 81.2 all-gather.28
  2128.6 75.2 reduce-scatter.24
  2206.9 38.7 reduce-scatter.44
  2248.9 34.1 reduce-scatter.42
  2286.1 36.0 reduce-scatter.28
  2325.2 35.9 reduce-scatter.26
  2364.5 41.1 reduce-scatter.32
  2409.2 41.2 reduce-scatter.30
  2454.4 45.0 reduce-scatter.40
  2503.8 44.8 reduce-scatter.36
  2552.7 44.8 reduce-scatter.38
  2604.6 117.5 all-reduce.38
  2726.4 42.0 reduce-scatter.34
  (1 shorter events, 22.0 us)
where the time goes:
time: 2800 us; the launch traced here: 2780 us
  waiting for transfers between devices  1170 us (42%)
  matrix products  772 us (28%)
  other arithmetic  361 us (13%)
  local copies, waits for them, and re-layouts  338 us (12%)
  blocking collectives  97.1 us (3%)
    dot_general x96, matrix products, advance(): jnp.einsum('shcd,shde->shce', w_part, state, precision=lax.Precision.HIGH...  169 us
    dot_general x96, matrix products, advance(): jnp.einsum('shcm,shme->shce', score_part, fresh, precision=lax.Precision....  149 us
    dot_general x96, matrix products, advance(): jnp.einsum('shcd,shde->shce', query_part, state, precision=lax.Precision....  146 us
    reduce_scatter x1, waiting for transfers between devices, per_device(): lax.psum_scatter(mixer_pieces, 'mp', scatter_dimension=1, tiled=True)  143 us
    reduce_scatter x1, waiting for transfers between devices, per_device(): lax.psum_scatter(backward_pieces, 'mp', scatter_dimension=1, tiled=True)  135 us
    another operation x4, other arithmetic, spanned_rule(): jax.scipy.linalg.solve_triangular(lower, rhs_side, lower=True, unit_diago...  134 us
    psum x1, waiting for transfers between devices, per_device(): lax.psum((d_mix_gain, d_ffn_gain, d_head_gain, conv_full, rate_full, bias...  125 us
    dot_general x96, matrix products, advance(): jnp.einsum('shcd,shce->shde', keyed_part, fresh, precision=lax.Precision....  118 us
  transfers between devices with their start and end apart: 28, of which 22 were waited for; matrix products, arithmetic and copies ran while one was open for 25% of the time, Pallas kernels for 0%

commit v1 on v0

v1 whole, which is shorter than its diff:
```python
from functools import partial

import jax
import jax.numpy as jnp
from jax import lax
from jax.experimental import pallas as pl
from jax.experimental.pallas import tpu as pltpu
from jax.sharding import PartitionSpec as P

DK = 128
DV = 256
HEADW = 2 * DK + DV
TAPS = 4
CHUNK = 128
HALO = 8
WIDE = 256
F32 = jnp.float32
BF16 = jnp.bfloat16


def mm(a, b, ca=1, cb=0):
    return lax.dot_general(
        a, b, (((ca,), (cb,)), ((), ())), precision=lax.Precision.HIGHEST, preferred_element_type=F32
    )


def conv_chunk(raw_ref, convw, base, rows):
    total = None
    for i in range(TAPS):
        part = raw_ref[0, pl.ds(HALO - TAPS + 1 + i + base, rows), 0:HEADW] * convw[i : i + 1]
        total = part if total is None else total + part
    return total


def decays(ab_ref, base, rows, upper):
    ab = ab_ref[0, :, pl.ds(base, rows)]
    cum = mm(ab, upper)
    row_id = lax.broadcasted_iota(jnp.int32, ab.shape, 0)
    both = jnp.where(row_id == 0, cum, ab)
    cols = both.T
    return both[0:1], cols[:, 0:1], cols[:, 1:2]


def masks(size):
    rows = lax.broadcasted_iota(jnp.int32, (size, size), 0)
    cols = lax.broadcasted_iota(jnp.int32, (size, size), 1)
    return rows, cols


def fades(gamma_row, gamma_col, rows, cols):
    spread = jnp.minimum(gamma_col - gamma_row, 0.0)
    inclusive = jnp.where(rows >= cols, jnp.exp(spread), 0.0)
    strict = jnp.where(rows > cols, inclusive, 0.0)
    return inclusive, strict


def invert_many(lowers, rows, cols):
    size = lowers[0].shape[0]
    eye = (rows == cols).astype(F32)
    pair = ((rows // 2) == (cols // 2)) & (rows > cols)
    inverses = [eye - jnp.where(pair, low, 0.0) for low in lowers]
    width = 2
    while width < size:
        within = (rows // (2 * width)) == (cols // (2 * width))
        cross = within & ((rows // width) != (cols // width)) & (rows > cols)
        inner = [mm(jnp.where(cross, low, 0.0), inv) for low, inv in zip(lowers, inverses)]
        inverses = [inv - mm(inv, part) for inv, part in zip(inverses, inner)]
        width *= 2
    return inverses


def unit_parts(conv):
    sig = jax.nn.sigmoid(conv)
    silu = conv * sig
    q_silu = silu[:, :DK]
    k_silu = silu[:, DK : 2 * DK]
    value = silu[:, 2 * DK :]
    q_scale = lax.rsqrt(jnp.sum(q_silu * q_silu, axis=-1, keepdims=True) + 1e-06)
    k_scale = lax.rsqrt(jnp.sum(k_silu * k_silu, axis=-1, keepdims=True) + 1e-06)
    return sig, q_silu, k_silu, value, q_scale, k_scale


def greet(z, parts, first):
    @pl.when(first)
    def _():
        barrier = pltpu.get_barrier_semaphore()
        for delta in (1, parts - 1):
            pl.semaphore_signal(
                barrier, inc=1, device_id={"mp": lax.rem(z + delta, parts)},
                device_id_type=pl.DeviceIdType.MESH,
            )
        pl.semaphore_wait(barrier, 2)


def forward_kernel(
    heads, parts,
    raw_ref, gate_ref, convw_ref, ab_ref, gain_ref,
    head_ref, o_ref, s_ref, t_ref, qe_ref, phi_ref, phil_ref,
    qe_s, o0_s, phi_s, b_s, phil_s, bl_s, send_s, recv_s, send_sem, recv_sem,
):
    step = pl.program_id(0)
    z = lax.axis_index("mp")
    lag = parts - 1
    slots = lag + 1
    length = gate_ref.shape[1] - HALO
    size = min(CHUNK, length)
    chunks = length // size

    greet(z, parts, step == 0)

    def hop(h):
        return pltpu.make_async_remote_copy(
            src_ref=send_s.at[h], dst_ref=recv_s.at[h], send_sem=send_sem.at[h],
            recv_sem=recv_sem.at[h], device_id={"mp": lax.rem(z + 1, parts)},
            device_id_type=pl.DeviceIdType.MESH,
        )

    @pl.when((step == 0) & (z == 0))
    def _():
        recv_s[...] = jnp.zeros_like(recv_s)

    @pl.when(step < heads)
    def _():
        slot = lax.rem(step, slots)
        rows, cols = masks(size)
        upper = (rows <= cols).astype(F32)
        convw = convw_ref[0]
        kept = []
        lowers = []
        for c in range(chunks):
            conv = conv_chunk(raw_ref, convw, c * size, size)
            _, q_silu, k_silu, value, q_scale, k_scale = unit_parts(conv)
            query = q_silu * (q_scale * DK ** (-0.5))
            keyed = k_silu * k_scale
            gamma_row, gamma_col, beta = decays(ab_ref, c * size, size, upper)
            inclusive, strict = fades(gamma_row, gamma_col, rows, cols)
            gram = mm(jnp.concatenate([keyed, query], axis=0), keyed, 1, 1)
            lowers.append(beta * gram[:size] * strict)
            scores = gram[size:] * inclusive
            growth = jnp.exp(gamma_col)
            last = gamma_row[:, size - 1 :]
            rhs = jnp.concatenate([(beta * growth) * keyed, beta * value], axis=1)
            kept.append((scores, rhs, query * growth, keyed * jnp.exp(last - gamma_col), last))
        inverses = invert_many(lowers, rows, cols)
        eye = (masks(DK)[0] == masks(DK)[1]).astype(F32)
        phi_all = None
        b_all = None
        for c in range(chunks):
            scores, rhs, query_g, keyed_g, last = kept[c]
            t_ref[0, c] = inverses[c]
            solved = mm(inverses[c], rhs)
            mixed = mm(scores, solved)
            moved = mm(keyed_g, solved, 0, 0)
            query_e = query_g - mixed[:, :DK]
            phi = jnp.exp(last) * eye - moved[:, :DK]
            inflow = moved[:, DK:]
            qe_ref[0, c * size : (c + 1) * size] = query_e
            qe_s[slot, c * size : (c + 1) * size] = query_e
            o0_s[slot, c * size : (c + 1) * size] = mixed[:, DK:]
            phi_ref[0, c] = phi.T
            phi_s[slot, c] = phi
            b_s[slot, c] = inflow
            if c == 0:
                phi_all, b_all = phi, inflow
            else:
                moved_all = mm(phi, jnp.concatenate([phi_all, b_all], axis=1))
                phi_all = moved_all[:, :DK]
                b_all = moved_all[:, DK:] + inflow
        phil_ref[0] = phi_all.T
        phil_s[slot] = phi_all
        bl_s[slot] = b_all

    relay = step - z

    @pl.when((relay >= 0) & (relay < heads))
    def _():
        slot = lax.rem(relay, slots)

        @pl.when(z > 0)
        def _():
            hop(relay).wait_recv()

        @pl.when(z < parts - 1)
        def _():
            send_s[relay] = mm(phil_s[slot], recv_s[relay]) + bl_s[slot]
            hop(relay).start()

    @pl.when(step >= lag)
    def _():
        head = step - lag
        slot = lax.rem(head, slots)
        state = recv_s[head]
        for c in range(chunks):
            at = slice(c * size, (c + 1) * size)
            s_ref[0, c] = state
            result = mm(qe_s[slot, at], state) + o0_s[slot, at]
            if c + 1 < chunks:
                state = mm(phi_s[slot, c], state) + b_s[slot, c]
            o_ref[0, at] = result
            scale = lax.rsqrt(jnp.mean(result * result, axis=-1, keepdims=True) + 1e-05)
            gate = gate_ref[0, HALO + c * size : HALO + (c + 1) * size]
            gated = result * scale * gain_ref[...] * (gate * jax.nn.sigmoid(gate))
            head_ref[0, at] = gated.astype(BF16)

    @pl.when((step == pl.num_programs(0) - 1) & (z < parts - 1))
    def _():
        @pl.loop(0, heads)
        def _(h):
            hop(h).wait_send()


def backward_kernel(
    heads, parts,
    dhead_ref, o_ref, gate_ref, qe_ref, phi_ref, phil_ref,
    raw_ref, convw_ref, ab_ref, gain_ref, s_ref, t_ref, phi_late_ref,
    dproj_ref, dab_ref, dconv_ref, dgain_ref,
    do_s, d_s, dgate_s, dl_s, phil_s, g_s, dext_s, send_s, recv_s, halo_send, halo_recv,
    send_sem, recv_sem, halo_send_sem, halo_recv_sem,
):
    step = pl.program_id(0)
    z = lax.axis_index("mp")
    back = parts - 1 - z
    lag = parts - 1
    slots = lag + 1
    length = o_ref.shape[1]
    size = min(CHUNK, length)
    chunks = length // size

    greet(z, parts, step == 0)

    def hop(h):
        return pltpu.make_async_remote_copy(
            src_ref=send_s.at[h], dst_ref=recv_s.at[h], send_sem=send_sem.at[h],
            recv_sem=recv_sem.at[h], device_id={"mp": lax.rem(z + parts - 1, parts)},
            device_id_type=pl.DeviceIdType.MESH,
        )

    def halo_hop(h):
        return pltpu.make_async_remote_copy(
            src_ref=halo_send.at[h], dst_ref=halo_recv.at[h], send_sem=halo_send_sem.at[h],
            recv_sem=halo_recv_sem.at[h], device_id={"mp": lax.rem(z + parts - 1, parts)},
            device_id_type=pl.DeviceIdType.MESH,
        )

    @pl.when(step == 0)
    def _():
        dgain_ref[...] = jnp.zeros_like(dgain_ref)
        g_s[...] = jnp.zeros_like(g_s)

    @pl.when((step == 0) & (back == 0))
    def _():
        recv_s[...] = jnp.zeros_like(recv_s)
        halo_recv[...] = jnp.zeros_like(halo_recv)

    @pl.when(step < heads)
    def _():
        slot = lax.rem(step, slots)
        gslot = lax.rem(step, slots + 1)
        gain = gain_ref[...]
        d_gain = jnp.zeros((1, DV), F32)
        for c in range(chunks):
            at = slice(c * size, (c + 1) * size)
            out = o_ref[0, at]
            d_head = dhead_ref[0, at]
            gate = gate_ref[0, HALO + c * size : HALO + (c + 1) * size]
            scale = lax.rsqrt(jnp.mean(out * out, axis=-1, keepdims=True) + 1e-05)
            unit = out * scale
            sig = jax.nn.sigmoid(gate)
            gated = gate * sig
            both = d_head * unit
            d_gain = d_gain + jnp.sum(both * gated, axis=0, keepdims=True)
            e = d_head * gated * gain
            d_out = scale * (e - unit * jnp.mean(e * unit, axis=-1, keepdims=True))
            dgate_s[gslot, at] = (both * gain * sig * (1.0 + gate * (1.0 - sig))).astype(BF16)
            do_s[slot, at] = d_out
            d_s[slot, c] = mm(qe_ref[0, at], d_out, 0, 0)
        dgain_ref[...] += d_gain
        total = d_s[slot, chunks - 1]
        for c in range(chunks - 2, -1, -1):
            total = mm(phi_ref[0, c], total) + d_s[slot, c]
        dl_s[slot] = total
        phil_s[slot] = phil_ref[0]

    relay = step - back

    @pl.when((relay >= 0) & (relay < heads))
    def _():
        slot = lax.rem(relay, slots)

        @pl.when(back > 0)
        def _():
            hop(relay).wait_recv()

        @pl.when(z > 0)
        def _():
            send_s[relay] = mm(phil_s[slot], recv_s[relay]) + dl_s[slot]
            hop(relay).start()

    @pl.when((step >= lag) & (step < lag + heads))
    def _():
        head = step - lag
        slot = lax.rem(head, slots)
        eslot = lax.rem(head, 2)
        rows, cols = masks(size)
        upper = (rows <= cols).astype(F32)
        convw = convw_ref[0]
        d_state = recv_s[head]
        d_conv_rows = [jnp.zeros((1, HEADW), F32) for _ in range(TAPS)]
        for c in range(chunks - 1, -1, -1):
            at = slice(c * size, (c + 1) * size)
            conv = conv_chunk(raw_ref, convw, c * size, size)
            sig, q_silu, k_silu, value, q_scale, k_scale = unit_parts(conv)
            query = q_silu * (q_scale * DK ** (-0.5))
            keyed = k_silu * k_scale
            gamma_row, gamma_col, beta = decays(ab_ref, c * size, size, upper)
            inclusive, strict = fades(gamma_row, gamma_col, rows, cols)
            gram = mm(jnp.concatenate([keyed, query], axis=0), keyed, 1, 1)
            gram_f = gram[:size] * strict
            lower = beta * gram_f
            scores = gram[size:] * inclusive
            growth = jnp.exp(gamma_col)
            last = gamma_row[:, size - 1 :]
            tail = jnp.exp(last - gamma_col)
            query_g = query * growth
            grown = keyed * growth
            keyed_b = beta * grown
            keyed_g = keyed * tail
            state = s_ref[0, c]
            inverse = t_ref[0, c]
            d_out = do_s[slot, at]
            fresh = mm(inverse, beta * value - mm(keyed_b, state))
            d_fresh = mm(scores, d_out, 0, 0) + mm(keyed_g, d_state)
            d_rhs = mm(inverse, d_fresh, 0, 0)
            stacked = jnp.concatenate([d_out, d_rhs], axis=0)
            by_fresh = mm(stacked, fresh, 1, 1)
            by_state = mm(stacked, state, 1, 1)
            d_scores = by_fresh[:size] * inclusive
            d_lower = -by_fresh[size:]
            d_query_g = by_state[:size]
            d_keyed_b = -by_state[size:]
            d_keyed_g = mm(fresh, d_state, 1, 1)
            d_gram = d_lower * (beta * strict)
            by_keyed = mm(jnp.concatenate([d_scores, d_gram], axis=0), keyed)
            d_query = by_keyed[:size] + growth * d_query_g
            d_keyed = (
                by_keyed[size:]
                + mm(jnp.concatenate([d_scores, d_gram], axis=0),
                     jnp.concatenate([query, keyed], axis=0), 0, 0)
                + (beta * growth) * d_keyed_b
                + tail * d_keyed_g
            )
            d_value = beta * d_rhs
            d_beta = (
                jnp.sum(d_rhs * value, axis=-1, keepdims=True)
                + jnp.sum(d_lower * gram_f, axis=-1, keepdims=True)
                + jnp.sum(d_keyed_b * grown, axis=-1, keepdims=True)
            )
            moved = by_fresh[:size] * scores + d_lower * lower
            tail_part = jnp.sum(d_keyed_g * keyed_g, axis=-1, keepdims=True)
            d_gamma = (
                jnp.sum(moved, axis=-1, keepdims=True)
                + jnp.sum(d_query_g * query_g, axis=-1, keepdims=True)
                + jnp.sum(d_keyed_b * keyed_b, axis=-1, keepdims=True)
                - tail_part
            )
            at_end = jnp.sum(tail_part, axis=0, keepdims=True) + jnp.exp(last) * jnp.sum(
                jnp.sum(state * d_state, axis=-1, keepdims=True), axis=0, keepdims=True
            )
            lanes = lax.broadcasted_iota(jnp.int32, (size, DK), 1)
            packed = jnp.where(lanes == 0, d_gamma, jnp.where(lanes == 1, d_beta, 0.0)).T[:8]
            row_id = lax.broadcasted_iota(jnp.int32, packed.shape, 0)
            packed = packed - jnp.where(row_id == 0, jnp.sum(moved, axis=0, keepdims=True), 0.0)
            summed = mm(packed, upper, 1, 1) + at_end
            dab_ref[0, :, at] = jnp.where(row_id == 0, summed, packed)
            if c > 0:
                d_state = mm(phi_late_ref[0, c], d_state) + d_s[slot, c]
            d_q_silu = (DK ** (-0.5) * q_scale) * (
                d_query
                - q_silu * (q_scale * q_scale) * jnp.sum(q_silu * d_query, axis=-1, keepdims=True)
            )
            d_k_silu = k_scale * (
                d_keyed
                - k_silu * (k_scale * k_scale) * jnp.sum(k_silu * d_keyed, axis=-1, keepdims=True)
            )
            d_silu = jnp.concatenate([d_q_silu, d_k_silu, d_value], axis=1)
            d_conv = d_silu * sig * (1.0 + conv * (1.0 - sig))
            g_s[HALO + c * size : HALO + (c + 1) * size] = d_conv
            for i in range(TAPS):
                shifted = raw_ref[0, pl.ds(HALO - TAPS + 1 + i + c * size, size), 0:HEADW]
                d_conv_rows[i] = d_conv_rows[i] + jnp.sum(shifted * d_conv, axis=0, keepdims=True)
        for i in range(TAPS):
            dconv_ref[0, i : i + 1] = d_conv_rows[i]
        for base, count in [(0, HALO)] + [(HALO + c * size, size) for c in range(chunks)]:
            d_raw = None
            for i in range(TAPS):
                part = g_s[pl.ds(base + TAPS - 1 - i, count)] * convw[i : i + 1]
                d_raw = part if d_raw is None else d_raw + part
            if base == 0:
                halo_send[head] = d_raw
            else:
                dext_s[eslot, base - HALO : base - HALO + count] = d_raw

        @pl.when(z > 0)
        def _():
            halo_hop(head).start()

    @pl.when(step > lag)
    def _():
        head = step - lag - 1
        eslot = lax.rem(head, 2)
        gslot = lax.rem(head, slots + 1)

        @pl.when(back > 0)
        def _():
            halo_hop(head).wait_recv()

        dext_s[eslot, length - HALO : length] += halo_recv[head]
        dproj_ref[0, :, 0:HEADW] = dext_s[eslot].astype(BF16)
        dproj_ref[0, :, HEADW:] = dgate_s[gslot]

    @pl.when((step == pl.num_programs(0) - 1) & (z > 0))
    def _():
        @pl.loop(0, heads)
        def _(h):
            hop(h).wait_send()
            halo_hop(h).wait_send()


def forward_core(raw, convw, ab, gain, heads, parts):
    length = raw.shape[1] - HALO
    size = min(CHUNK, length)
    chunks = length // size
    per = heads // raw.shape[0]
    lag = parts - 1
    slots = lag + 1
    now = lambda s: jnp.minimum(s, heads - 1)
    late = lambda s: jnp.maximum(s - lag, 0)
    return pl.pallas_call(
        partial(forward_kernel, heads, parts),
        grid=(heads + lag,),
        out_shape=(
            jax.ShapeDtypeStruct((raw.shape[0], length, per * DV), BF16),
            jax.ShapeDtypeStruct((heads, length, DV), F32),
            jax.ShapeDtypeStruct((heads, chunks, DK, DV), F32),
            jax.ShapeDtypeStruct((heads, chunks, size, size), F32),
            jax.ShapeDtypeStruct((heads, length, DK), F32),
            jax.ShapeDtypeStruct((heads, chunks, DK, DK), F32),
            jax.ShapeDtypeStruct((heads, DK, DK), F32),
        ),
        in_specs=[
            pl.BlockSpec((1, length + HALO, HEADW + DV), lambda s: (now(s) // per, 0, now(s) % per)),
            pl.BlockSpec((1, length + HALO, DV), lambda s: (late(s) // per, 0, (late(s) % per) * 3 + 2)),
            pl.BlockSpec((1, TAPS, HEADW), lambda s: (now(s), 0, 0)),
            pl.BlockSpec((1, 8, length), lambda s: (now(s), 0, 0)),
            pl.BlockSpec((1, DV), lambda s: (0, 0)),
        ],
        out_specs=(
            pl.BlockSpec((1, length, DV), lambda s: (late(s) // per, 0, late(s) % per)),
            pl.BlockSpec((1, length, DV), lambda s: (late(s), 0, 0)),
            pl.BlockSpec((1, chunks, DK, DV), lambda s: (late(s), 0, 0, 0)),
            pl.BlockSpec((1, chunks, size, size), lambda s: (now(s), 0, 0, 0)),
            pl.BlockSpec((1, length, DK), lambda s: (now(s), 0, 0)),
            pl.BlockSpec((1, chunks, DK, DK), lambda s: (now(s), 0, 0, 0)),
            pl.BlockSpec((1, DK, DK), lambda s: (now(s), 0, 0)),
        ),
        scratch_shapes=[
            pltpu.VMEM((slots, length, DK), F32),
            pltpu.VMEM((slots, length, DV), F32),
            pltpu.VMEM((slots, chunks, DK, DK), F32),
            pltpu.VMEM((slots, chunks, DK, DV), F32),
            pltpu.VMEM((slots, DK, DK), F32),
            pltpu.VMEM((slots, DK, DV), F32),
            pltpu.VMEM((heads, DK, DV), F32),
            pltpu.VMEM((heads, DK, DV), F32),
            pltpu.SemaphoreType.DMA((heads,)),
            pltpu.SemaphoreType.DMA((heads,)),
        ],
        compiler_params=pltpu.CompilerParams(
            collective_id=0, has_side_effects=True, vmem_limit_bytes=56 * 2**20
        ),
        cost_estimate=pl.CostEstimate(flops=20 * 10**9, bytes_accessed=40 * 2**20, transcendentals=0),
        name="delta_forward",
    )(raw, raw, convw, ab, gain)


def backward_core(d_head, out, raw, query_e, phi, phi_all, convw, ab, gain, states, inverses, heads, parts):
    length = raw.shape[1] - HALO
    size = min(CHUNK, length)
    chunks = length // size
    per = heads // raw.shape[0]
    lag = parts - 1
    slots = lag + 1
    now = lambda s: jnp.minimum(s, heads - 1)
    late = lambda s: jnp.clip(s - lag, 0, heads - 1)
    later = lambda s: jnp.maximum(s - lag - 1, 0)
    return pl.pallas_call(
        partial(backward_kernel, heads, parts),
        grid=(heads + lag + 1,),
        out_shape=(
            jax.ShapeDtypeStruct((raw.shape[0], length, per * (HEADW + DV)), BF16),
            jax.ShapeDtypeStruct((heads, 8, length), F32),
            jax.ShapeDtypeStruct((heads, TAPS, HEADW), F32),
            jax.ShapeDtypeStruct((1, DV), F32),
        ),
        in_specs=[
            pl.BlockSpec((1, length, DV), lambda s: (now(s) // per, 0, now(s) % per)),
            pl.BlockSpec((1, length, DV), lambda s: (now(s), 0, 0)),
            pl.BlockSpec((1, length + HALO, DV), lambda s: (now(s) // per, 0, (now(s) % per) * 3 + 2)),
            pl.BlockSpec((1, length, DK), lambda s: (now(s), 0, 0)),
            pl.BlockSpec((1, chunks, DK, DK), lambda s: (now(s), 0, 0, 0)),
            pl.BlockSpec((1, DK, DK), lambda s: (now(s), 0, 0)),
            pl.BlockSpec((1, length + HALO, HEADW + DV), lambda s: (late(s) // per, 0, late(s) % per)),
            pl.BlockSpec((1, TAPS, HEADW), lambda s: (late(s), 0, 0)),
            pl.BlockSpec((1, 8, length), lambda s: (late(s), 0, 0)),
            pl.BlockSpec((1, DV), lambda s: (0, 0)),
            pl.BlockSpec((1, chunks, DK, DV), lambda s: (late(s), 0, 0, 0)),
            pl.BlockSpec((1, chunks, size, size), lambda s: (late(s), 0, 0, 0)),
            pl.BlockSpec((1, chunks, DK, DK), lambda s: (late(s), 0, 0, 0)),
        ],
        out_specs=(
            pl.BlockSpec((1, length, HEADW + DV), lambda s: (later(s) // per, 0, later(s) % per)),
            pl.BlockSpec((1, 8, length), lambda s: (late(s), 0, 0)),
            pl.BlockSpec((1, TAPS, HEADW), lambda s: (late(s), 0, 0)),
            pl.BlockSpec((1, DV), lambda s: (0, 0)),
        ),
        scratch_shapes=[
            pltpu.VMEM((slots, length, DV), F32),
            pltpu.VMEM((slots, chunks, DK, DV), F32),
            pltpu.VMEM((slots + 1, length, DV), BF16),
            pltpu.VMEM((slots, DK, DV), F32),
            pltpu.VMEM((slots, DK, DK), F32),
            pltpu.VMEM((length + 2 * HALO, HEADW), F32),
            pltpu.VMEM((2, length, HEADW), F32),
            pltpu.VMEM((heads, DK, DV), F32),
            pltpu.VMEM((heads, DK, DV), F32),
            pltpu.VMEM((heads, HALO, HEADW), F32),
            pltpu.VMEM((heads, HALO, HEADW), F32),
            pltpu.SemaphoreType.DMA((heads,)),
            pltpu.SemaphoreType.DMA((heads,)),
            pltpu.SemaphoreType.DMA((heads,)),
            pltpu.SemaphoreType.DMA((heads,)),
        ],
        compiler_params=pltpu.CompilerParams(
            collective_id=1, has_side_effects=True, vmem_limit_bytes=56 * 2**20
        ),
        cost_estimate=pl.CostEstimate(flops=40 * 10**9, bytes_accessed=60 * 2**20, transcendentals=0),
        name="delta_backward",
    )(d_head, out, raw, query_e, phi, phi_all, raw, convw, ab, gain, states, inverses, phi)


def scatter_kernel(bits, parts, plan, rows, length, lhs_ref, *refs):
    count = len(plan)
    sources = len({seg for seg, _, _ in plan})
    rhs_refs = refs[:sources]
    out_ref = refs[sources]
    rhs_s, grad_s, r1, *rest = refs[sources + 1 :]
    planes = bits - 1
    ra = rest[:planes]
    rb = rest[planes : 2 * planes]
    r4, load_sem, send1, recv1, send_a, recv_a, send_b, recv_b, send4, recv4 = rest[2 * planes :]
    d = lax.axis_index("dp")
    z = lax.axis_index("mp")
    half = 2 ** (bits - 1)
    mesh_id = pl.DeviceIdType.MESH

    def bit(b):
        return lax.rem(lax.div(d, 2**b), 2)

    def partner(b):
        return d + (1 - 2 * bit(b)) * 2**b

    barrier = pltpu.get_barrier_semaphore()
    for b in range(bits):
        pl.semaphore_signal(barrier, inc=1, device_id={"dp": partner(b)}, device_id_type=mesh_id)
    for delta in range(1, parts):
        pl.semaphore_signal(
            barrier, inc=1, device_id={"mp": lax.rem(z + delta, parts)}, device_id_type=mesh_id
        )
    pl.semaphore_wait(barrier, bits + parts - 1)

    def by_segment(t, act):
        for seg in range(sources):
            at = [k for k, item in enumerate(plan) if item[0] == seg]

            @pl.when((t >= at[0]) & (t <= at[-1]))
            def _():
                act(seg, plan[at[0]][1], t - at[0])

    def load(t):
        def act(seg, lhs_index, piece):
            pltpu.make_async_copy(
                rhs_refs[seg].at[:, :, pl.ds(pl.multiple_of(piece * WIDE, WIDE), WIDE)],
                rhs_s.at[lax.rem(t, 2)],
                load_sem.at[lax.rem(t, 2)],
            ).start()

        by_segment(t, act)

    def load_wait(t):
        slot = lax.rem(t, 2)
        pltpu.make_async_copy(
            rhs_refs[0].at[:, :, pl.ds(0, WIDE)], rhs_s.at[slot], load_sem.at[slot]
        ).wait()

    def first_hop(t):
        slot = lax.rem(t, 2)
        return pltpu.make_async_remote_copy(
            src_ref=grad_s.at[slot, :, :, 1 - bit(0)], dst_ref=r1.at[t], send_sem=send1.at[t],
            recv_sem=recv1.at[t], device_id={"dp": partner(0)}, device_id_type=mesh_id,
        )

    def a_hop(k, t):
        b = bits - 1 - k
        keep = half >> (k + 1)
        away = pl.ds((1 - bit(b)) * keep, keep)
        if k == 0:
            src = r1.at[t, :, away, :, 0 : WIDE // 2]
        else:
            src = ra[k - 1].at[t, :, away]
        return pltpu.make_async_remote_copy(
            src_ref=src, dst_ref=ra[k].at[t], send_sem=send_a.at[k, t], recv_sem=recv_a.at[k, t],
            device_id={"dp": partner(b)}, device_id_type=mesh_id,
        )

    def b_hops(k, t):
        b = 1 + k
        keep = half >> (k + 1)
        copies = []
        for hi in range(keep):
            away = 2 * hi + 1 - bit(b)
            if k == 0:
                src = r1.at[t, :, away, :, WIDE // 2 :]
            else:
                src = rb[k - 1].at[t, :, away]
            copies.append(
                pltpu.make_async_remote_copy(
                    src_ref=src, dst_ref=rb[k].at[t, :, hi], send_sem=send_b.at[k, t],
                    recv_sem=recv_b.at[k, t], device_id={"dp": partner(b)}, device_id_type=mesh_id,
                )
            )
        return copies

    def b_whole(k, t):
        return pltpu.make_async_remote_copy(
            src_ref=rb[k].at[t], dst_ref=rb[k].at[t], send_sem=send_b.at[k, t],
            recv_sem=recv_b.at[k, t], device_id={"dp": partner(1 + k)}, device_id_type=mesh_id,
        )

    def z_hops(t):
        copies = []
        for delta in range(1, parts):
            to = lax.rem(z + delta, parts)
            for side, buf in enumerate((ra[planes - 1], rb[planes - 1])):
                copies.append(
                    pltpu.make_async_remote_copy(
                        src_ref=buf.at[t, to, 0],
                        dst_ref=r4.at[t, parts - 1 - delta, :, side * (WIDE // 2) : (side + 1) * (WIDE // 2)],
                        send_sem=send4.at[t], recv_sem=recv4.at[t], device_id={"mp": to},
                        device_id_type=mesh_id,
                    )
                )
        return copies

    def z_whole(t):
        return pltpu.make_async_remote_copy(
            src_ref=r4.at[t], dst_ref=r4.at[t], send_sem=send4.at[t], recv_sem=recv4.at[t],
            device_id={"mp": lax.rem(z + 1, parts)}, device_id_type=mesh_id,
        )

    load(0)

    @pl.loop(0, count + planes + 2)
    def _(tick):
        t = tick - planes - 2

        @pl.when(t >= 0)
        def _():
            z_whole(t).wait_recv()
            side = WIDE // 2
            left = ra[planes - 1][t, z, 0].astype(F32)
            right = rb[planes - 1][t, z, 0].astype(F32)
            for s in range(parts - 1):
                left = left + r4[t, s, :, 0:side].astype(F32)
                right = right + r4[t, s, :, side:].astype(F32)
            out_ref[t, :, 0:side] = left
            out_ref[t, :, side:] = right

        for k in range(planes - 1, -1, -1):
            t_k = tick - k - 2

            @pl.when((t_k >= 0) & (t_k < count))
            def _():
                a_hop(k, t_k).wait_recv()
                b_whole(k, t_k).wait_recv()
                keep = half >> (k + 1)
                bit_a, bit_b = bit(bits - 1 - k), bit(1 + k)
                for m in range(keep):
                    own_a, own_b = bit_a * keep + m, 2 * m + bit_b
                    for j in range(parts):
                        if k == 0:
                            mine_a = r1[t_k, j, own_a, :, 0 : WIDE // 2]
                            mine_b = r1[t_k, j, own_b, :, WIDE // 2 :]
                        else:
                            mine_a = ra[k - 1][t_k, j, own_a]
                            mine_b = rb[k - 1][t_k, j, own_b]
                        ra[k][t_k, j, m] = (ra[k][t_k, j, m].astype(F32) + mine_a.astype(F32)).astype(BF16)
                        rb[k][t_k, j, m] = (rb[k][t_k, j, m].astype(F32) + mine_b.astype(F32)).astype(BF16)
                if k + 1 < planes:
                    a_hop(k + 1, t_k).start()
                    for copy in b_hops(k + 1, t_k):
                        copy.start()
                else:
                    for copy in z_hops(t_k):
                        copy.start()

        t_1 = tick - 1

        @pl.when((t_1 >= 0) & (t_1 < count))
        def _():
            first_hop(t_1).wait_recv()
            slot = lax.rem(t_1, 2)
            color = bit(0)

            @pl.loop(0, parts)
            def _(j):
                for m in range(half):
                    r1[t_1, j, m] = (
                        r1[t_1, j, m].astype(F32) + grad_s[slot, j, m, color].astype(F32)
                    ).astype(BF16)

            a_hop(0, t_1).start()
            for copy in b_hops(0, t_1):
                copy.start()

        @pl.when(tick < count)
        def _():
            slot = lax.rem(tick, 2)

            @pl.when(tick + 1 < count)
            def _():
                load(tick + 1)

            load_wait(tick)

            @pl.when(tick >= 2)
            def _():
                first_hop(tick - 2).wait_send()

            lhs_index = 0
            for k, item in enumerate(plan):
                lhs_index = jnp.where(tick == k, item[1], lhs_index)

            @pl.loop(0, parts)
            def _(j):
                full = jnp.dot(lhs_ref[lhs_index], rhs_s[slot, j], preferred_element_type=F32)
                grad_s[slot, j] = full.astype(BF16).reshape(half, 2, rows, WIDE)

            first_hop(tick).start()

    for t in range(max(count - 2, 0), count):
        first_hop(t).wait_send()

    @pl.loop(0, count)
    def _(t):
        for k in range(planes):
            a_hop(k, t).wait_send()
            b_whole(k, t).wait_send()
        z_whole(t).wait_send()


def scatter_sum(lefts, pairs, groups, parts, collective):
    kinds, width, length = lefts.shape
    bits = groups.bit_length() - 1
    rows = width // groups
    planes = bits - 1
    half = groups // 2
    plan = []
    for seg, (kind, right) in enumerate(pairs):
        plan += [(seg, kind, p) for p in range(right.shape[2] // WIDE)]
    count = len(plan)
    vmem = lambda *shape: pltpu.VMEM(shape, BF16)
    dma = lambda *shape: pltpu.SemaphoreType.DMA(shape)
    return pl.pallas_call(
        partial(scatter_kernel, bits, parts, plan, rows, length),
        out_shape=jax.ShapeDtypeStruct((count, rows, WIDE), F32),
        in_specs=[pl.BlockSpec(memory_space=pltpu.VMEM)] + [pl.BlockSpec(memory_space=pl.ANY)] * len(pairs),
        out_specs=pl.BlockSpec(memory_space=pltpu.VMEM),
        scratch_shapes=[
            vmem(2, parts, length, WIDE),
            vmem(2, parts, half, 2, rows, WIDE),
            vmem(count, parts, half, rows, WIDE),
            *[vmem(count, parts, half >> (k + 1), rows, WIDE // 2) for k in range(planes)],
            *[vmem(count, parts, half >> (k + 1), rows, WIDE // 2) for k in range(planes)],
            vmem(count, parts - 1, rows, WIDE),
            dma(2),
            dma(count), dma(count),
            dma(planes, count), dma(planes, count),
            dma(planes, count), dma(planes, count),
            dma(count), dma(count),
        ],
        compiler_params=pltpu.CompilerParams(
            collective_id=collective, has_side_effects=True, vmem_limit_bytes=60 * 2**20
        ),
        cost_estimate=pl.CostEstimate(
            flops=2 * count * WIDE * parts * length * width, bytes_accessed=count * parts * length * WIDE * 2,
            transcendentals=0,
        ),
        name="scatter_sum",
    )(lefts, *[right for _, right in pairs])


def dot(spec, a, b):
    return jnp.einsum(spec, a, b, preferred_element_type=F32)


def unit_rms(v):
    return lax.rsqrt(jnp.mean(v * v, axis=-1, keepdims=True) + 1e-05)


def per_device(
    tokens, out_grad, seq_lengths, mix_gain, w_query, w_key, w_value, w_outgate, w_decay, w_beta,
    conv_weight, rate_log, step_bias, head_gain, w_out, ffn_gain, w_ffn_gate, w_ffn_up, w_ffn_down,
):
    groups = lax.axis_size("dp")
    parts = lax.axis_size("mp")
    group = lax.axis_index("dp")
    share = lax.axis_index("mp")
    heads = rate_log.shape[0]
    per = heads // parts
    width = tokens.shape[2]
    local_rows = w_query.shape[0]

    x_bf = lax.all_to_all(tokens, "dp", split_axis=0, concat_axis=1, tiled=True)[0]
    dy_bf = lax.all_to_all(out_grad, "dp", split_axis=0, concat_axis=1, tiled=True)[0]
    length = x_bf.shape[0]
    before = lax.ppermute(x_bf[length - HALO :], "mp", [(i, i + 1) for i in range(parts - 1)])

    def by_head(w, size):
        return w.reshape(local_rows, per, size)

    joined = jnp.concatenate(
        [by_head(w_query, DK), by_head(w_key, DK), by_head(w_value, DV), by_head(w_outgate, DV)], axis=2
    ).reshape(local_rows, per * (HEADW + DV))
    main_cols = joined.shape[1]

    def gathered(w):
        whole = lax.all_gather(w, ("mp", "dp"), axis=0, tiled=True)
        return whole.reshape(parts, groups * local_rows, w.shape[1])

    g_proj = gathered(joined)
    g_small = gathered(jnp.concatenate([w_decay, w_beta], axis=1))
    g_out = gathered(w_out)
    g_gate = gathered(w_ffn_gate)
    g_up = gathered(w_ffn_up)
    g_down = gathered(w_ffn_down)

    my_length = lax.dynamic_slice_in_dim(seq_lengths, group, 1)
    positions = share * length + jnp.arange(length, dtype=jnp.int32)
    live = (positions < my_length).astype(F32)[:, None]

    x = x_bf.astype(F32)
    dy = live * dy_bf.astype(F32)
    d_ffo = dy.astype(BF16)
    ext = jnp.concatenate([before, x_bf], axis=0).astype(F32)
    h1_ext = (ext * unit_rms(ext) * mix_gain).astype(BF16)
    raw = dot("td,gdc->gtc", h1_ext, g_proj)
    h1 = h1_ext[HALO:]
    small = dot("td,gdc->gct", h1, g_small)
    decay_raw = small[:, :per].reshape(heads, length)
    beta_raw = small[:, per:].reshape(heads, length)
    rate = -jnp.exp(rate_log)[:, None]
    shifted = decay_raw + step_bias[:, None]
    decay = rate * jax.nn.softplus(shifted)
    beta = jax.nn.sigmoid(beta_raw)
    ab = jnp.concatenate(
        [decay[:, None], beta[:, None], jnp.zeros((heads, 6, length), F32)], axis=1
    )
    taps = conv_weight.shape[0]
    key_cols = heads * DK
    convw = jnp.concatenate(
        [
            conv_weight[:, :key_cols].reshape(taps, heads, DK),
            conv_weight[:, key_cols : 2 * key_cols].reshape(taps, heads, DK),
            conv_weight[:, 2 * key_cols :].reshape(taps, heads, DV),
        ],
        axis=2,
    ).transpose(1, 0, 2)
    gain_row = head_gain[None]
    head_out, mixed, states, inverses, query_e, phi, phi_all = forward_core(
        raw, convw, ab, gain_row, heads, parts
    )

    x1 = x + dot("gtc,gmc->tm", head_out, g_out)
    scale2 = unit_rms(x1)
    n2 = x1 * scale2
    h2 = (n2 * ffn_gain).astype(BF16)
    gate = dot("td,gdf->gtf", h2, g_gate)
    up = dot("td,gdf->gtf", h2, g_up)
    sig = jax.nn.sigmoid(gate)
    act = (gate * sig * up).astype(BF16)
    block_out = (live * (x1 + dot("gtf,gdf->td", act, g_down))).astype(BF16)
    d_act = dot("td,gdf->gtf", d_ffo, g_down)
    d_gate = (d_act * up * sig * (1.0 + gate * (1.0 - sig))).astype(BF16)
    d_up = (d_act * gate * sig).astype(BF16)
    d_h2 = dot("gtf,gdf->td", d_gate, g_gate) + dot("gtf,gdf->td", d_up, g_up)
    e2 = d_h2 * ffn_gain
    d_x1 = dy + scale2 * (e2 - n2 * jnp.mean(e2 * n2, axis=-1, keepdims=True))
    ffn_gain_grad = jnp.sum(d_h2 * n2, axis=0)
    d_mix = d_x1.astype(BF16)
    d_head = dot("tm,gmc->gtc", d_mix, g_out)

    d_proj, d_ab, d_convw, d_head_gain = backward_core(
        d_head, mixed, raw, query_e, phi, phi_all, convw, ab, gain_row, states, inverses, heads, parts
    )
    d_decay = d_ab[:, 0]
    d_beta_raw = d_ab[:, 1] * beta * (1.0 - beta)
    d_decay_raw = d_decay * rate * jax.nn.sigmoid(shifted)
    rate_grad = jnp.sum(d_decay * decay, axis=1)
    bias_grad = jnp.sum(d_decay_raw, axis=1)
    d_small = jnp.concatenate(
        [d_decay_raw.reshape(parts, per, length), d_beta_raw.reshape(parts, per, length)], axis=1
    ).astype(BF16)
    hidden = act.shape[2]
    wide = -(-hidden // WIDE) * WIDE
    padded = lambda v: jnp.pad(v, ((0, 0), (0, 0), (0, wide - hidden)))
    lefts = jnp.stack([h1.T, d_mix.T, h2.T, d_ffo.T])
    sums_w = scatter_sum(
        lefts,
        [(3, padded(act)), (2, padded(d_gate)), (2, padded(d_up)), (1, head_out), (0, d_proj)],
        groups, parts, 2,
    )

    def columns(start, size):
        pieces = -(-size // WIDE)
        return sums_w[start : start + pieces].transpose(1, 0, 2).reshape(local_rows, -1)[:, :size]

    step = wide // WIDE
    s_down = columns(0, hidden)
    s_gate = columns(step, hidden)
    s_up = columns(2 * step, hidden)
    s_out = columns(3 * step, per * DV)
    s_proj = columns(3 * step + per * DV // WIDE, main_cols)
    small_grad = dot("gct,td->gcd", d_small, h1)
    d_h1 = dot("gtc,gdc->td", d_proj, g_proj) + dot("gct,gdc->td", d_small, g_small)
    scale1 = unit_rms(x)
    n1 = x * scale1
    e1 = d_h1 * mix_gain
    d_x = d_x1 + scale1 * (e1 - n1 * jnp.mean(e1 * n1, axis=-1, keepdims=True))
    mix_gain_grad = jnp.sum(d_h1 * n1, axis=0)
    per_head = d_convw.transpose(1, 0, 2)
    d_conv = jnp.concatenate(
        [
            per_head[:, :, :DK].reshape(taps, key_cols),
            per_head[:, :, DK : 2 * DK].reshape(taps, key_cols),
            per_head[:, :, 2 * DK :].reshape(taps, heads * DV),
        ],
        axis=1,
    )
    sums = lax.psum(
        jnp.concatenate(
            [mix_gain_grad, ffn_gain_grad, d_head_gain[0], d_conv.reshape(-1), rate_grad, bias_grad,
             small_grad.reshape(-1)]
        ),
        ("dp", "mp"),
    )
    pieces = []
    start = 0
    for count in (width, width, DV, taps * conv_weight.shape[1], heads, heads):
        pieces.append(sums[start : start + count])
        start += count
    small_sum = sums[start:].reshape(parts, 2 * per, width)
    mine = lax.dynamic_slice(small_sum, (share, 0, group * local_rows), (1, 2 * per, local_rows))[0].T

    by = s_proj.reshape(local_rows, per, HEADW + DV)
    flat = lambda v: v.reshape(local_rows, -1)
    final_out = lax.all_to_all(block_out[None], "dp", split_axis=1, concat_axis=0, tiled=True)
    final_grad = lax.all_to_all(d_x.astype(BF16)[None], "dp", split_axis=1, concat_axis=0, tiled=True)
    return (
        final_out,
        final_grad,
        pieces[0],
        flat(by[:, :, :DK]),
        flat(by[:, :, DK : 2 * DK]),
        flat(by[:, :, 2 * DK : HEADW]),
        flat(by[:, :, HEADW:]),
        mine[:, :per],
        mine[:, per:],
        pieces[3].reshape(conv_weight.shape),
        pieces[4],
        pieces[5],
        pieces[2],
        s_out,
        pieces[1],
        s_gate,
        s_up,
        s_down,
    )


def solution(mesh):
    seq = P(None, ("mp", "dp"), None)
    shard = P("dp", "mp")
    rep = P()
    return jax.shard_map(
        per_device,
        mesh=mesh,
        in_specs=(
            seq, seq, rep, rep, shard, shard, shard, shard, shard, shard,
            rep, rep, rep, rep, shard, rep, shard, shard, shard,
        ),
        out_specs=(
            seq, seq, rep, shard, shard, shard, shard, shard, shard,
            rep, rep, rep, rep, shard, rep, shard, shard, shard,
        ),
        check_vma=False,
    )
```

time: 2800 us -> 964 us (0.34)
  waiting for transfers between devices: 1170 us -> 257 us
  matrix products: 772 us -> 86.8 us
  Pallas kernels: 0 us -> 396 us
  other arithmetic: 361 us -> 32.1 us
  local copies, waits for them, and re-layouts: 338 us -> 78.2 us
    dot_general x406 -> x13, matrix products: 755 us -> 86.8 us  [dot(): return jnp.einsum(spec, a, b, preferred_element_type=F32)]
    reduce_scatter x12 -> x0, waiting for transfers between devices: 658 us -> none  [the longest x1 143 us: per_device(): lax.psum_scatter(mixer_pieces, 'mp', scatter_dimension=1, tiled=True)]
    pallas_call x0 -> x3, Pallas kernels: none -> 396 us  [the longest x1 180 us: scatter_sum(): pl.pallas_call(partial(scatter_kernel, bits, parts, plan, rows, length),...]
    all_gather x10 -> x5, waiting for transfers between devices: 319 us -> 186 us  [gathered(): whole = lax.all_gather(w, ('mp', 'dp'), axis=0, tiled=True)]
    another operation x7 -> x4, other arithmetic: 135 us -> 5.43 us  [the longest x3 4.54 us: per_device(): lefts = jnp.stack([h1.T, d_mix.T, h2.T, d_ffo.T])]
    reduce_sum x51 -> x3, other arithmetic: 84.4 us -> 1.75 us  [the longest x2 1 us: unit_rms(): return lax.rsqrt(jnp.mean(v * v, axis=-1, keepdims=True) + 1e-05)]
    reshape x17 -> x10, local copies, waits for them, and re-layouts: 74.6 us -> 5.63 us  [the longest x4 3.68 us: by_head(): return w.reshape(local_rows, per, size)]
    dynamic_slice x98 -> x1, local copies, waits for them, and re-layouts: 64.9 us -> 0.58 us  [per_device(): my_length = lax.dynamic_slice_in_dim(seq_lengths, group, 1)]
  transfers between devices with their start and end apart: 28 -> 10, of which waited for: 22 -> 6; matrix products, arithmetic and copies ran while one was open for 25% -> 12% of each run, Pallas kernels for 0% -> 9%
where the time goes in v1:
time: 964 us; the launch traced here: 954 us
  Pallas kernels  396 us (41%)
  waiting for transfers between devices  257 us (27%)
  matrix products  86.8 us (9%)
  local copies, waits for them, and re-layouts  78.2 us (8%)
  blocking collectives  75.4 us (8%)
  other arithmetic  32.1 us (3%)
  between operations  15 us (2%)
  starting transfers between devices  13.1 us (1%)
    all_gather x5, waiting for transfers between devices, gathered(): whole = lax.all_gather(w, ('mp', 'dp'), axis=0, tiled=True)  186 us
    pallas_call x1, Pallas kernels, scatter_sum(): pl.pallas_call(partial(scatter_kernel, bits, parts, plan, rows, length),...  180 us
    pallas_call x1, Pallas kernels, backward_core(): pl.pallas_call(partial(backward_kernel, heads, parts), grid=(heads + lag...  132 us
    dot_general x13, matrix products, dot(): return jnp.einsum(spec, a, b, preferred_element_type=F32)  86.8 us
    pallas_call x1, Pallas kernels, forward_core(): pl.pallas_call(partial(forward_kernel, heads, parts), grid=(heads + lag,)...  84.6 us
    psum x1, waiting for transfers between devices, per_device(): lax.psum(jnp.concatenate([mix_gain_grad, ffn_gain_grad, d_head_gain[0], d...  61 us
    all_gather x1, blocking collectives, gathered(): whole = lax.all_gather(w, ('mp', 'dp'), axis=0, tiled=True)  52.2 us
    unnamed x95, local copies, waits for them, and re-layouts  25 us
  transfers between devices with their start and end apart: 10, of which 6 were waited for; matrix products, arithmetic and copies ran while one was open for 12% of the time, Pallas kernels for 9%

profile of v1, /device:TPU:0, one launch (start us, length us, event | category | flops | bytes accessed | tf_op | source)
XLA Modules:
  0.0 953.7 jit_solution(906224522977915874)
XLA Ops:
  14.9 23.1 %all_to_all.42 = bf16[8,64,1024]{2,1,0:T(8,128)(2,1)S(1)} all-to-all(bf16[8,64,1024]{2,1,0:T(8,128)(2,1)S(1)} %copy-done.13), channel_id=1, replica_groups=mesh['dp'=8,'mp'=4] {'dp'}, dimensions={0} | all-to-all | bytes 2097152 | tf_op jit(solution)/shard_map/all_to_all | solution.py:833
  43.7 52.2 %all_gather.19 = bf16[4096,4]{0,1:T(4,128)(2,1)S(1)} all-gather(bf16[128,4]{0,1:T(4,128)(2,1)S(1)} %pad_maximum_fusion.6), channel_id=1, replica_groups=mesh['dp'=8,'mp'=4] {'mp','dp'}, dimensions={0}, use_global_device_ids=true | all-gather | bytes 33792 | tf_op jit(solution)/shard_map/all_gather | solution.py:847
  104.5 7.9 collective-permute-done
  117.8 5.1 all-gather.6.cloned.1.call-done
  122.9 12.6 %convolution_bitcast_fusion.raw_ref.gate_ref = f32[4,520,1536]{2,1,0:T(8,128)} fusion(bf16[4,1024,1536]{2,1,0:T(8,128)(2,1)} %bitcast.240, bf16[520,1024]{0,1:T(8,128)(2,1)S(1)} %fusion.33), kind=kOutput, calls=%fused_computation | convolution fusion | flops 6543114240 | bytes 26427392 | tf_op jit(solution)/shard_map/td,gdc->gtc/dot_general | solution.py:813
  135.5 84.6 %delta_forward.1 = (bf16[4,512,512]{2,1,0:T(8,128)(2,1)}, f32[8,512,256]{2,1,0:T(8,128)}, f32[8,4,128,256]{3,2,1,0:T(8,128)}, f32[8,4,128,128]{3,2,1,0:T(8,128)}...) custom-call(f32[4,520,1536]{2,1,0:T(8,128)} %convolution_bitcast_fusion.raw_ref.gate_ref, ...), custom_call_target="tpu_custom_call" | custom-call | flops 20000000000 | bytes 41943040 | tf_op jit(solution)/shard_map/delta_forward/pallas_call | solution.py:438
  220.2 5.2 multiply_reduce_fusion.3
  226.9 44.4 %all-gather.10.cloned.1.call-done = bf16[4096,704]{0,1:T(8,128)(2,1)} async-done(((bf16[128,704]{0,1:T(8,128)(2,1)}), bf16[4096,704]{0,1:T(8,128)(2,1)}) %all-gather.10.cloned.1.call-update) | async-done | bytes 5767184 | tf_op jit(solution)/shard_map/all_gather | solution.py:847
  271.3 8.7 fusion.20
  280.0 68.0 %all-gather.12.cloned.1.call-done = bf16[4096,704]{0,1:T(8,128)(2,1)} async-done(((bf16[128,704]{0,1:T(8,128)(2,1)}), bf16[4096,704]{0,1:T(8,128)(2,1)}) %all-gather.12.cloned.1.call-update) | async-done | bytes 5767184 | tf_op jit(solution)/shard_map/all_gather | solution.py:847
  348.0 8.6 fusion.16
  356.6 68.1 %all-gather.14.cloned.1.call-done = bf16[4096,704]{0,1:T(8,128)(2,1)} async-done(((bf16[128,704]{0,1:T(8,128)(2,1)}), bf16[4096,704]{0,1:T(8,128)(2,1)}) %all-gather.14.cloned.1.call-update) | async-done | bytes 5767184 | tf_op jit(solution)/shard_map/all_gather | solution.py:847
  424.7 10.1 %fusion.2 = (bf16[4,512,704]{2,1,0:T(8,128)(2,1)S(1)}, bf16[4,512,704]{2,1,0:T(8,128)(2,1)S(1)}, bf16[4,512,704]{2,1,0:T(8,128)(2,1)S(1)}) fusion(f32[512,4,704]{2,0,1:T(8,128)} %fusion.16, f32[512,4,704]{2,0,1:T(8,128)} %fusion.20, bf16[512,1024,1]{1,0,2:T(8,128)(2,1)} %bitcast.225, bf16[88,4,8,1024]{3,2,1,0:T(8,128)(2,1)} %bitcast.242), kind=kOutput, calls=%fused_computation.5 | convolution fusion | flops 2975858688 | bytes 27000832 | tf_op jit(solution)/shard_map/td,gdf->gtf/dot_general | solution.py:813
  434.8 4.9 fusion.14
  444.0 6.9 multiply_reduce_fusion
  462.9 131.8 %delta_backward.1 = (bf16[4,512,1536]{2,1,0:T(8,128)(2,1)}, f32[8,8,512]{2,1,0:T(8,128)}, f32[8,4,512]{2,1,0:T(4,128)}, f32[1,256]{1,0:T(1,128)}) custom-call(f32[4,512,512]{2,1,0:T(8,128)} %convolution_bitcast_fusion.1.dhead_ref, f32[8,512,256]{2,1,0:T(8,128)} %get-tuple-element.30.o_ref, f32[4,520,1536]{2,1,0:T(8,128)} %convolution_bitcast_fusion.raw_ref.gate_ref, ...), custom_call_target="tpu_custom_call" | custom-call | flops 40000000000 | bytes 62914560 | tf_op jit(solution)/shard_map/delta_backward/pallas_call | solution.py:496
  594.7 179.7 %scatter_sum.1 = f32[17,128,256]{2,1,0:T(8,128)} custom-call(bf16[4,1024,512]{2,1,0:T(8,128)(2,1)} %pad_maximum_fusion.lhs_ref, bf16[4,512,768]{2,1,0:T(8,128)(2,1)} %pad.10.refs_0_, bf16[4,512,768]{2,1,0:T(8,128)(2,1)} %pad.11.refs_1_, bf16[4,512,768]{2,1,0:T(8,128)(2,1)} %pad.12.refs_2_, bf16[4,512,512]{2,1,0:T(8,128)(2,1)} %get-tuple-element.29.refs_3_, ...), custom_call_target="tpu_custom_call" | custom-call | flops 18253611008 | bytes 17825792 | tf_op jit(solution)/shard_map/scatter_sum/pallas_call | solution.py:783
  781.6 12.5 %fusion.82 = f32[512,1024,1]{0,1,2:T(8,128)} fusion(bf16[4,512,1536]{2,1,0:T(8,128)(2,1)} %get-tuple-element.36.refs_4_, bf16[4,1024,1536]{2,1,0:T(8,128)(2,1)} %bitcast.241), kind=kOutput, calls=%fused_computation.136 | convolution fusion | flops 6442450944 | bytes 20971520 | tf_op jit(solution)/shard_map/gtc,gdc->td/dot_general | solution.py:813
  814.5 4.7 copy.131
  819.7 7.8 reduce.6
  834.1 8.1 fusion.46
  852.1 4.7 copy.118
  856.8 7.8 reduce.5
  871.4 61.0 %all-reduce.5.cloned.1.call-done = f32[35088]{0:T(1024)} async-done(((f32[35088]{0:T(1024)}), f32[35088]{0:T(1024)}) %all-reduce.5.cloned.1.call-update) | async-done | bytes 140368 | tf_op jit(solution)/shard_map/psum | solution.py:959
  (194 shorter events, 110.2 us)
Async XLA Ops:
  7.2 115.7 %all-gather.6.cloned.1.call-start = ((), (), s32[]{:S(2)}) async-start(), calls=%async_computation.4 | async-start | bytes 12976128 | tf_op jit(solution)/shard_map/all_gather | solution.py:847
  12.1 208.0 %all-gather.8.cloned.1.call-start = ((), (), s32[]{:S(2)}) async-start(), calls=%async_computation.5 | async-start | bytes 4325376 | tf_op jit(solution)/shard_map/all_gather | solution.py:847
  12.9 258.4 %all-gather.10.cloned.1.call-start = ((), (), s32[]{:S(2)}) async-start(), calls=%async_computation.6 | async-start | bytes 5947392 | tf_op jit(solution)/shard_map/all_gather | solution.py:847
  13.6 334.4 %all-gather.12.cloned.1.call-start = ((), (), s32[]{:S(2)}) async-start(), calls=%async_computation.7 | async-start | bytes 5947392 | tf_op jit(solution)/shard_map/all_gather | solution.py:847
  14.2 27.4 %copy-start.37 = (f32[8]{0:T(128)S(1)}, f32[8]{0:T(128)}, u32[]{:S(2)}) copy-start(f32[8]{0:T(128)} %param.30) | copy-start | bytes 100
  14.2 28.1 %copy-start.29 = (f32[8]{0:T(128)S(1)}, f32[8]{0:T(128)}, u32[]{:S(2)}) copy-start(f32[8]{0:T(128)} %param.31) | copy-start | bytes 100
  14.2 28.9 %copy-start.38 = (s32[8]{0:T(128)S(1)}, s32[8]{0:T(128)}, u32[]{:S(2)}) copy-start(s32[8]{0:T(128)} %param.21) | copy-start | bytes 100
  14.2 29.5 %copy-start.33 = (bf16[128,2]{0,1:T(2,128)(2,1)S(1)}, bf16[128,2]{0,1:T(2,128)(2,1)}, u32[]{:S(2)}) copy-start(bf16[128,2]{0,1:T(2,128)(2,1)} %param.28) | copy-start | bytes 1540
  14.2 29.4 %copy-start.34 = (bf16[128,2]{0,1:T(2,128)(2,1)S(1)}, bf16[128,2]{0,1:T(2,128)(2,1)}, u32[]{:S(2)}) copy-start(bf16[128,2]{0,1:T(2,128)(2,1)} %param.27) | copy-start | bytes 1540
  14.2 83.0 %copy-start.19 = (f32[4,4096]{1,0:T(4,128)S(1)}, f32[4,4096]{1,0:T(4,128)}, u32[]{:S(2)}) copy-start(f32[4,4096]{1,0:T(4,128)} %param.29) | copy-start | bytes 196612
  14.3 410.4 %all-gather.14.cloned.1.call-start = ((), (), s32[]{:S(2)}) async-start(), calls=%async_computation.8 | async-start | bytes 5947392 | tf_op jit(solution)/shard_map/all_gather | solution.py:847
  14.9 82.4 %slice-start = ((f32[4,4096]{1,0:T(4,128)}), f32[4,2048]{1,0:T(4,128)S(1)}, s32[]{:S(2)}) async-start(f32[4,4096]{1,0:T(4,128)} %param.29), calls=%async_computation.10 | async-start | bytes 65536 | tf_op jit(solution)/shard_map/slice | solution.py:884
  38.0 62.9 %all-to-all-start.2 = ((bf16[8,64,1024]{2,1,0:T(8,128)(2,1)}), bf16[8,64,1024]{2,1,0:T(8,128)(2,1)S(1)}, u32[]{:S(2)}, u32[]{:S(2)}) async-start(bf16[8,64,1024]{2,1,0:T(8,128)(2,1)} %param.20), calls=%async_computation.2 | async-start | bytes 2097152 | tf_op jit(solution)/shard_map/all_to_all | solution.py:834
  41.6 890.9 %all-reduce.5.cloned.1.call-start = ((), (), s32[]{:S(2)}) async-start(), calls=%async_computation.9 | async-start | bytes 286720 | tf_op jit(solution)/shard_map/psum | solution.py:959
  41.7 73.8 %copy-start.31 = (f32[8]{0:T(128)}, f32[8]{0:T(128)S(1)}, u32[]{:S(2)}) copy-start(f32[8]{0:T(128)S(1)} %exponential_negate_fusion) | copy-start | bytes 100
  96.6 354.2 %copy-start.27 = (f32[512]{0:T(512)}, f32[512]{0:T(512)S(1)}, u32[]{:S(2)}) copy-start(f32[512]{0:T(512)S(1)} %fusion.72) | copy-start | bytes 6148
  99.3 13.1 %collective-permute-start = (bf16[8,1024]{0,1:T(8,128)(2,1)}, bf16[8,1024]{0,1:T(8,128)(2,1)S(1)}, u32[]{:S(2)}, u32[]{:S(2)}) collective-permute-start(bf16[8,1024]{0,1:T(8,128)(2,1)} %slice.132), channel_id=1, source_target_pairs={{0,1},{1,2},{2,3},{4,5},{5,6},{6,7},{8,9},{9,10},{10,11},{12,13},{... | collective-permute-start | bytes 49160 | tf_op jit(solution)/shard_map/ppermute | solution.py:836
  114.2 21.3 %copy-start = (bf16[520,1024]{0,1:T(8,128)(2,1)}, bf16[520,1024]{0,1:T(8,128)(2,1)S(1)}, u32[]{:S(2)}) copy-start(bf16[520,1024]{0,1:T(8,128)(2,1)S(1)} %fusion.33) | copy-start | bytes 3194884
  114.7 20.8 %copy-start.16 = (f32[4,4,512]{2,1,0:T(4,128)}, f32[4,4,512]{2,1,0:T(4,128)S(1)}, u32[]{:S(2)}) copy-start(f32[4,4,512]{2,1,0:T(4,128)S(1)} %fusion.56) | copy-start | bytes 98308
  114.8 20.7 %copy-start.17 = (f32[4,2,512]{2,1,0:T(2,128)}, f32[4,2,512]{2,1,0:T(2,128)S(1)}, u32[]{:S(2)}) copy-start(f32[4,2,512]{2,1,0:T(2,128)S(1)} %get-tuple-element.127) | copy-start | bytes 49156
  225.4 225.5 %copy-start.2 = (f32[512,1024]{0,1:T(8,128)}, f32[512,1024]{0,1:T(8,128)S(1)}, u32[]{:S(2)}) copy-start(f32[512,1024]{0,1:T(8,128)S(1)} %get-tuple-element.131) | copy-start | bytes 6291460
  434.8 23.4 %copy-start.9 = (bf16[4,512,704]{2,1,0:T(8,128)(2,1)}, bf16[4,512,704]{2,1,0:T(8,128)(2,1)S(1)}, u32[]{:S(2)}) copy-start(bf16[4,512,704]{2,1,0:T(8,128)(2,1)S(1)} %get-tuple-element.105) | copy-start | bytes 8650756
  830.3 36.9 %all-to-all-start.3 = ((bf16[8,2,32768]{2,1,0:T(2,128)(2,1)}), bf16[8,2,32768]{2,1,0:T(2,128)(2,1)S(1)}, u32[]{:S(2)}, u32[]{:S(2)}) async-start(bf16[8,2,32768]{2,1,0:T(2,128)(2,1)} %reshape.367), calls=%async_computation.3 | async-start | bytes 2097152 | tf_op jit(solution)/shard_map/all_to_all | solution.py:977
  867.2 73.8 %all-to-all-start.1 = ((bf16[8,2,32768]{2,1,0:T(2,128)(2,1)}), bf16[8,2,32768]{2,1,0:T(2,128)(2,1)}, u32[]{:S(2)}, u32[]{:S(2)}) async-start(bf16[8,2,32768]{2,1,0:T(2,128)(2,1)} %reshape.365), calls=%async_computation.1 | async-start | bytes 2097152 | tf_op jit(solution)/shard_map/all_to_all | solution.py:976
  (27 other events, 169.8 us)
Sparse Core Ops, SparseCore 0:
  12.2 110.5 all-gather.5
  125.7 64.3 all-gather.7
  192.9 78.3 all-gather.9
  274.0 73.9 all-gather.11
  350.7 73.9 all-gather.13
  811.4 120.9 all-reduce.4

commit v2 on v1

v2 whole, which is shorter than its diff:
```python
from functools import partial

import jax
import jax.numpy as jnp
from jax import lax
from jax.experimental import pallas as pl
from jax.experimental.pallas import tpu as pltpu
from jax.sharding import PartitionSpec as P

DK = 128
DV = 256
HEADW = 2 * DK + DV
TAPS = 4
CHUNK = 128
HALO = 8
WIDE = 256
STRIDE = 2
F32 = jnp.float32
BF16 = jnp.bfloat16


def halves(a):
    high = a.astype(BF16)
    return high, (a - high.astype(F32)).astype(BF16)


def mm(a, b, ca=1, cb=0):
    dims = (((ca,), (cb,)), ((), ()))
    a_high, a_low = halves(a)
    b_high, b_low = halves(b)
    one = lambda p, q: lax.dot_general(p, q, dims, preferred_element_type=F32)
    return one(a_high, b_high) + (one(a_high, b_low) + one(a_low, b_high))


def windows(raw_ref, ext_s, c, size):
    if c == 0:
        return [ext_s[pl.ds(HALO - TAPS + 1 + i, size)] for i in range(TAPS)]
    return [raw_ref[0, pl.ds(c * size - TAPS + 1 + i, size), 0:HEADW] for i in range(TAPS)]


def conv_of(shifted, convw):
    total = None
    for i in range(TAPS):
        part = shifted[i] * convw[i : i + 1]
        total = part if total is None else total + part
    return total


def decays(ab_ref, base, rows, upper):
    ab = ab_ref[0, :, pl.ds(base, rows)]
    cum = mm(ab, upper)
    row_id = lax.broadcasted_iota(jnp.int32, ab.shape, 0)
    both = jnp.where(row_id == 0, cum, ab)
    cols = both.T
    return both[0:1], cols[:, 0:1], cols[:, 1:2]


def masks(size):
    rows = lax.broadcasted_iota(jnp.int32, (size, size), 0)
    cols = lax.broadcasted_iota(jnp.int32, (size, size), 1)
    return rows, cols


def fades(gamma_row, gamma_col, rows, cols):
    spread = jnp.minimum(gamma_col - gamma_row, 0.0)
    inclusive = jnp.where(rows >= cols, jnp.exp(spread), 0.0)
    strict = jnp.where(rows > cols, inclusive, 0.0)
    return inclusive, strict


def invert_many(lowers, rows, cols):
    size = lowers[0].shape[0]
    eye = (rows == cols).astype(F32)
    pair = ((rows // 2) == (cols // 2)) & (rows > cols)
    inverses = [eye - jnp.where(pair, low, 0.0) for low in lowers]
    width = 2
    while width < size:
        within = (rows // (2 * width)) == (cols // (2 * width))
        cross = within & ((rows // width) != (cols // width)) & (rows > cols)
        inner = [mm(jnp.where(cross, low, 0.0), inv) for low, inv in zip(lowers, inverses)]
        inverses = [inv - mm(inv, part) for inv, part in zip(inverses, inner)]
        width *= 2
    return inverses


def unit_parts(conv):
    sig = jax.nn.sigmoid(conv)
    silu = conv * sig
    q_silu = silu[:, :DK]
    k_silu = silu[:, DK : 2 * DK]
    value = silu[:, 2 * DK :]
    q_scale = lax.rsqrt(jnp.sum(q_silu * q_silu, axis=-1, keepdims=True) + 1e-06)
    k_scale = lax.rsqrt(jnp.sum(k_silu * k_silu, axis=-1, keepdims=True) + 1e-06)
    return sig, q_silu, k_silu, value, q_scale, k_scale


class Gather:
    def __init__(self, bits, parts, sources, targets, pieces, sems):
        self.bits, self.parts, self.pieces = bits, parts, pieces
        self.sources, self.targets = sources, targets
        (self.own, self.z_send, self.z_recv, self.p_send, self.p_recv, self.s_send, self.s_recv) = sems
        self.d, self.z = lax.axis_index("dp"), lax.axis_index("mp")
        self.orders = (list(range(1, bits)), list(range(bits - 1, 0, -1)))
        self.ticks = bits + 1

    @staticmethod
    def scratch(bits, count):
        dma = lambda *shape: pltpu.SemaphoreType.DMA(shape)
        return [
            dma(count), dma(count), dma(count), dma(count, bits - 1, 2), dma(count, bits - 1, 2),
            dma(count), dma(count),
        ]

    def flip(self, index, b):
        return index + (1 - 2 * lax.rem(lax.div(self.d, 2**b), 2)) * 2**b

    def copy(self, src, dst, send, recv, to):
        return pltpu.make_async_remote_copy(
            src_ref=src, dst_ref=dst, send_sem=send, recv_sem=recv, device_id=to,
            device_id_type=pl.DeviceIdType.MESH,
        )

    def sides(self, p):
        _, start, mid, stop = self.pieces[p]
        return [(0, start, mid)] + ([(1, mid, stop)] if mid < stop else [])

    def held(self, side, k):
        out = [self.d]
        for b in self.orders[side][:k]:
            out = out + [self.flip(i, b) for i in out]
        return out

    def arrived(self, side, k):
        return [self.flip(i, self.orders[side][k]) for i in self.held(side, k)]

    def to_sibling(self, p, indices, start, stop):
        target = self.targets[self.pieces[p][0]]
        for i in indices:
            block = target.at[:, i, :, start:stop]
            self.copy(
                block, block, self.s_send.at[p], self.s_recv.at[p], {"dp": self.flip(self.d, 0)}
            ).start()

    def along(self, p, k, act):
        target = self.targets[self.pieces[p][0]]
        for side, start, stop in self.sides(p):
            b = self.orders[side][k]
            for i in self.held(side, k):
                block = target.at[:, i, :, start:stop]
                act(
                    self.copy(
                        block, block, self.p_send.at[p, k, side], self.p_recv.at[p, k, side],
                        {"dp": self.flip(self.d, b)},
                    )
                )

    def along_whole(self, p, k):
        target = self.targets[self.pieces[p][0]]
        out = []
        for side, start, stop in self.sides(p):
            block = target.at[:, pl.ds(0, 2**k), :, start:stop]
            out.append(
                self.copy(
                    block, block, self.p_send.at[p, k, side], self.p_recv.at[p, k, side],
                    {"dp": self.flip(self.d, self.orders[side][k])},
                )
            )
        return out

    def tick(self, p, stage):
        which, start, _, stop = self.pieces[p]
        source, target = self.sources[which], self.targets[which]
        if stage == 0:
            pltpu.make_async_copy(
                source.at[:, start:stop], target.at[self.z, self.d, :, start:stop], self.own.at[p]
            ).start()
            for delta in range(1, self.parts):
                self.copy(
                    source.at[:, start:stop], target.at[self.z, self.d, :, start:stop], self.z_send.at[p],
                    self.z_recv.at[p], {"mp": lax.rem(self.z + delta, self.parts)},
                ).start()
        elif stage == 1:
            pltpu.make_async_copy(
                source.at[:, start:stop], target.at[self.z, self.d, :, start:stop], self.own.at[p]
            ).wait()
            self.z_whole(p).wait_recv()
            self.along(p, 0, lambda copy: copy.start())
            self.to_sibling(p, [self.d], start, stop)
        elif stage <= self.bits:
            k = stage - 2
            for copy in self.along_whole(p, k):
                copy.wait_recv()
            if k + 1 < self.bits - 1:
                self.along(p, k + 1, lambda copy: copy.start())
            for side, low, high in self.sides(p):
                self.to_sibling(p, self.arrived(side, k), low, high)

    def moves(self):
        return len(self.pieces) + STRIDE * (self.ticks - 1)

    def move(self, now):
        for p in range(len(self.pieces)):
            if now >= p and (now - p) % STRIDE == 0 and (now - p) // STRIDE < self.ticks:
                self.tick(p, (now - p) // STRIDE)

    def z_whole(self, p):
        which, start, _, stop = self.pieces[p]
        block = self.targets[which].at[pl.ds(0, self.parts - 1), self.d, :, start:stop]
        return self.copy(
            block, block, self.z_send.at[p], self.z_recv.at[p],
            {"mp": lax.rem(self.z + 1, self.parts)},
        )

    def s_whole(self, p):
        which, start, _, stop = self.pieces[p]
        block = self.targets[which].at[:, pl.ds(0, 2 ** (self.bits - 1)), :, start:stop]
        return self.copy(
            block, block, self.s_send.at[p], self.s_recv.at[p], {"dp": self.flip(self.d, 0)}
        )

    def finish(self):
        for p in range(len(self.pieces)):
            self.s_whole(p).wait_recv()
            self.z_whole(p).wait_send()
            for k in range(self.bits - 1):
                for copy in self.along_whole(p, k):
                    copy.wait_send()
            self.s_whole(p).wait_send()


def greet_all(bits, parts, every):
    d, z = lax.axis_index("dp"), lax.axis_index("mp")
    barrier = pltpu.get_barrier_semaphore()
    if every:
        peers = [lax.rem(d + delta, 2**bits) for delta in range(1, 2**bits)]
    else:
        peers = [d + (1 - 2 * lax.rem(lax.div(d, 2**b), 2)) * 2**b for b in range(bits)]
    for peer in peers:
        pl.semaphore_signal(
            barrier, inc=1, device_id={"dp": peer}, device_id_type=pl.DeviceIdType.MESH
        )
    for delta in range(1, parts):
        pl.semaphore_signal(
            barrier, inc=1, device_id={"mp": lax.rem(z + delta, parts)},
            device_id_type=pl.DeviceIdType.MESH,
        )
    pl.semaphore_wait(barrier, len(peers) + parts - 1)


class Swap:
    def __init__(self, groups, source, target, own, send, recv):
        self.groups, self.source, self.target = groups, source, target
        self.own, self.send, self.recv = own, send, recv
        self.d = lax.axis_index("dp")

    def copy(self, src, dst, to):
        return pltpu.make_async_remote_copy(
            src_ref=src, dst_ref=dst, send_sem=self.send, recv_sem=self.recv, device_id={"dp": to},
            device_id_type=pl.DeviceIdType.MESH,
        )

    def local(self):
        return pltpu.make_async_copy(self.source.at[self.d], self.target.at[self.d], self.own)

    def start(self):
        self.local().start()
        for delta in range(1, self.groups):
            to = lax.rem(self.d + delta, self.groups)
            self.copy(self.source.at[to], self.target.at[self.d], to).start()

    def finish(self):
        self.local().wait()
        block = self.target.at[pl.ds(0, self.groups - 1)]
        whole = self.copy(block, block, lax.rem(self.d + 1, self.groups))
        whole.wait_recv()
        whole.wait_send()


def prologue_kernel(bits, parts, pieces, *refs):
    tokens, grads, joined, small, tokens_out, grads_out, joined_out, small_out = refs[:8]
    sems = refs[8:]
    gather = Gather(bits, parts, (joined, small), (joined_out, small_out), pieces, sems[:7])
    swaps = [
        Swap(2**bits, tokens, tokens_out, *[s.at[0] for s in sems[7:10]]),
        Swap(2**bits, grads, grads_out, *[s.at[1] for s in sems[7:10]]),
    ]
    greet_all(bits, parts, True)
    swaps[0].start()
    count = len(pieces)
    for now in range(gather.moves()):
        gather.move(now)
        if now == count - 1:
            swaps[1].start()
    gather.finish()
    for swap in swaps:
        swap.finish()


def prologue(tokens, grads, joined, small, groups, parts):
    bits = groups.bit_length() - 1
    rows, wide = joined.shape
    third = wide // 4
    pieces = [(1, 0, small.shape[1], small.shape[1])]
    pieces += [(0, 0, third, 2 * third), (0, 2 * third, 3 * third, wide)]
    swapped = jax.ShapeDtypeStruct(tokens.shape, BF16)
    any_spec = pl.BlockSpec(memory_space=pl.ANY)
    return pl.pallas_call(
        partial(prologue_kernel, bits, parts, pieces),
        out_shape=(
            swapped,
            swapped,
            jax.ShapeDtypeStruct((parts, groups, rows, wide), BF16),
            jax.ShapeDtypeStruct((parts, groups, rows, small.shape[1]), BF16),
        ),
        in_specs=[any_spec] * 4,
        out_specs=(any_spec,) * 4,
        scratch_shapes=Gather.scratch(bits, len(pieces)) + [pltpu.SemaphoreType.DMA((2,))] * 3,
        compiler_params=pltpu.CompilerParams(collective_id=3, has_side_effects=True),
        cost_estimate=pl.CostEstimate(flops=0, bytes_accessed=40 * 2**20, transcendentals=0),
        name="prologue",
    )(tokens, grads, joined, small)


def forward_kernel(
    heads, parts, bits, pieces,
    raw_ref, gate_ref, raw_any, convw_ref, ab_ref, gain_ref, *refs,
):
    weights = len({item[0] for item in pieces})
    sources, refs = refs[:weights], refs[weights:]
    head_ref, o_ref, s_ref, t_ref, qe_ref, phi_ref, phil_ref, halo_ref = refs[:8]
    targets, refs = refs[8 : 8 + weights], refs[8 + weights :]
    (qe_s, o0_s, phi_s, b_s, phil_s, bl_s, send_s, recv_s, halo_s, ext_s,
     send_sem, recv_sem, halo_send_sem, halo_recv_sem) = refs[:14]
    gather = Gather(bits, parts, sources, targets, pieces, refs[14:])
    step = pl.program_id(0)
    early = pl.program_id(1) == 0
    z = lax.axis_index("mp")
    lag = parts - 1
    slots = lag + 1
    length = gate_ref.shape[1]
    size = min(CHUNK, length)
    chunks = length // size
    per = heads // parts

    @pl.when((step == 0) & early)
    def _():
        greet_all(bits, parts, False)

    last = 2 * (heads + lag) - 1
    for now in range(min(gather.moves(), last)):
        @pl.when(step * 2 + pl.program_id(1) == now)
        def _():
            gather.move(now)

    @pl.when(step * 2 + pl.program_id(1) == last)
    def _():
        for now in range(last, gather.moves()):
            gather.move(now)

    def hop(h):
        return pltpu.make_async_remote_copy(
            src_ref=send_s.at[h], dst_ref=recv_s.at[h], send_sem=send_sem.at[h],
            recv_sem=recv_sem.at[h], device_id={"mp": lax.rem(z + 1, parts)},
            device_id_type=pl.DeviceIdType.MESH,
        )

    def halo_hop(g):
        return pltpu.make_async_remote_copy(
            src_ref=raw_any.at[g, length - HALO :], dst_ref=halo_s.at[g], send_sem=halo_send_sem.at[g],
            recv_sem=halo_recv_sem.at[g], device_id={"mp": lax.rem(z + 1, parts)},
            device_id_type=pl.DeviceIdType.MESH,
        )

    @pl.when((step == 0) & early & (z == 0))
    def _():
        recv_s[...] = jnp.zeros_like(recv_s)
        halo_s[...] = jnp.zeros_like(halo_s)

    @pl.when((step == 0) & early & (z < parts - 1))
    def _():
        for g in range(parts):
            halo_hop(g).start()

    @pl.when((step < heads) & early)
    def _():
        slot = lax.rem(step, slots)
        part, sub = lax.div(step, per), lax.rem(step, per)

        @pl.when((sub == 0) & (z > 0))
        def _():
            halo_hop(part).wait_recv()

        for k in range(per):
            @pl.when(sub == k)
            def _():
                ext_s[0:HALO] = halo_s[part, :, k * (HEADW + DV) : k * (HEADW + DV) + HEADW]

        ext_s[HALO:] = raw_ref[0, 0:size, 0:HEADW]
        rows, cols = masks(size)
        upper = (rows <= cols).astype(F32)
        convw = convw_ref[0]
        kept = []
        lowers = []
        for c in range(chunks):
            conv = conv_of(windows(raw_ref, ext_s, c, size), convw)
            _, q_silu, k_silu, value, q_scale, k_scale = unit_parts(conv)
            query = q_silu * (q_scale * DK ** (-0.5))
            keyed = k_silu * k_scale
            gamma_row, gamma_col, beta = decays(ab_ref, c * size, size, upper)
            inclusive, strict = fades(gamma_row, gamma_col, rows, cols)
            gram = mm(jnp.concatenate([keyed, query], axis=0), keyed, 1, 1)
            lowers.append(beta * gram[:size] * strict)
            scores = gram[size:] * inclusive
            growth = jnp.exp(gamma_col)
            last = gamma_row[:, size - 1 :]
            rhs = jnp.concatenate([(beta * growth) * keyed, beta * value], axis=1)
            kept.append((scores, rhs, query * growth, keyed * jnp.exp(last - gamma_col), last))
        inverses = invert_many(lowers, rows, cols)
        eye = (masks(DK)[0] == masks(DK)[1]).astype(F32)
        phi_all = None
        b_all = None
        for c in range(chunks):
            scores, rhs, query_g, keyed_g, last = kept[c]
            t_ref[0, c] = inverses[c]
            solved = mm(inverses[c], rhs)
            mixed = mm(scores, solved)
            moved = mm(keyed_g, solved, 0, 0)
            query_e = query_g - mixed[:, :DK]
            phi = jnp.exp(last) * eye - moved[:, :DK]
            inflow = moved[:, DK:]
            qe_ref[0, c * size : (c + 1) * size] = query_e
            qe_s[slot, c * size : (c + 1) * size] = query_e
            o0_s[slot, c * size : (c + 1) * size] = mixed[:, DK:]
            phi_ref[0, c] = phi.T
            phi_s[slot, c] = phi
            b_s[slot, c] = inflow
            if c == 0:
                phi_all, b_all = phi, inflow
            else:
                moved_all = mm(phi, jnp.concatenate([phi_all, b_all], axis=1))
                phi_all = moved_all[:, :DK]
                b_all = moved_all[:, DK:] + inflow
        phil_ref[0] = phi_all.T
        phil_s[slot] = phi_all
        bl_s[slot] = b_all

    relay = step - z

    @pl.when((relay >= 0) & (relay < heads) & ~early)
    def _():
        slot = lax.rem(relay, slots)

        @pl.when(z > 0)
        def _():
            hop(relay).wait_recv()

        @pl.when(z < parts - 1)
        def _():
            send_s[relay] = mm(phil_s[slot], recv_s[relay]) + bl_s[slot]
            hop(relay).start()

    @pl.when((step >= lag) & ~early)
    def _():
        head = step - lag
        slot = lax.rem(head, slots)
        state = recv_s[head]
        for c in range(chunks):
            at = slice(c * size, (c + 1) * size)
            s_ref[0, c] = state
            result = mm(qe_s[slot, at], state) + o0_s[slot, at]
            if c + 1 < chunks:
                state = mm(phi_s[slot, c], state) + b_s[slot, c]
            o_ref[0, at] = result
            scale = lax.rsqrt(jnp.mean(result * result, axis=-1, keepdims=True) + 1e-05)
            gate = gate_ref[0, c * size : (c + 1) * size]
            gated = result * scale * gain_ref[...] * (gate * jax.nn.sigmoid(gate))
            head_ref[0, at] = gated.astype(BF16)

    @pl.when((step == pl.num_programs(0) - 1) & ~early & (z < parts - 1))
    def _():
        @pl.loop(0, heads)
        def _(h):
            hop(h).wait_send()

        for g in range(parts):
            halo_hop(g).wait_send()

    @pl.when((step == pl.num_programs(0) - 1) & ~early)
    def _():
        halo_ref[...] = halo_s[...]
        gather.finish()


class Scatter:
    def __init__(self, bits, parts, plan, rows, lhs_ref, rhs_refs, out_ref, scratch):
        self.bits, self.parts, self.plan, self.rows = bits, parts, plan, rows
        self.lhs_ref, self.rhs_refs, self.out_ref = lhs_ref, rhs_refs, out_ref
        self.count = len(plan)
        self.planes = planes = bits - 1
        self.half = 2 ** (bits - 1)
        self.lhs_s, self.rhs_s, self.grad_s, self.r1, *rest = scratch
        self.ra, self.rb = rest[:planes], rest[planes : 2 * planes]
        (self.r4, self.load_sem, self.send1, self.recv1, self.send_a, self.recv_a, self.send_b,
         self.recv_b, self.send4, self.recv4) = rest[2 * planes :]
        self.d, self.z = lax.axis_index("dp"), lax.axis_index("mp")
        self.ticks = self.count + STRIDE * (planes + 2)

    @staticmethod
    def scratch(bits, parts, count, rows, length, width):
        planes, half = bits - 1, 2 ** (bits - 1)
        vmem = lambda *shape: pltpu.VMEM(shape, BF16)
        dma = lambda *shape: pltpu.SemaphoreType.DMA(shape)
        strips = [vmem(count, parts, half >> (k + 1), rows, WIDE // 2) for k in range(planes)]
        return [
            vmem(2, width, length),
            vmem(2, parts, length, WIDE),
            vmem(2, parts, half, 2, rows, WIDE),
            vmem(count, parts, half, rows, WIDE),
            *strips, *strips,
            vmem(count, parts - 1, rows, WIDE),
            dma(2, 2),
            dma(count), dma(count),
            dma(planes, count), dma(planes, count),
            dma(planes, count), dma(planes, count),
            dma(count), dma(count),
        ]

    def bit(self, b):
        return lax.rem(lax.div(self.d, 2**b), 2)

    def partner(self, b):
        return self.d + (1 - 2 * self.bit(b)) * 2**b

    def remote(self, src, dst, send, recv, to):
        return pltpu.make_async_remote_copy(
            src_ref=src, dst_ref=dst, send_sem=send, recv_sem=recv, device_id=to,
            device_id_type=pl.DeviceIdType.MESH,
        )

    def load(self, t):
        slot = lax.rem(t, 2)
        for seg in range(len(self.rhs_refs)):
            at = [k for k, item in enumerate(self.plan) if item[0] == seg]

            @pl.when((t >= at[0]) & (t <= at[-1]))
            def _():
                start = pl.multiple_of((t - at[0]) * WIDE, WIDE)
                pltpu.make_async_copy(
                    self.rhs_refs[seg].at[:, :, pl.ds(start, WIDE)], self.rhs_s.at[slot],
                    self.load_sem.at[0, slot],
                ).start()
                pltpu.make_async_copy(
                    self.lhs_ref.at[self.plan[at[0]][1]], self.lhs_s.at[slot], self.load_sem.at[1, slot]
                ).start()

    def load_wait(self, t):
        slot = lax.rem(t, 2)
        pltpu.make_async_copy(
            self.rhs_refs[0].at[:, :, pl.ds(0, WIDE)], self.rhs_s.at[slot], self.load_sem.at[0, slot]
        ).wait()
        pltpu.make_async_copy(
            self.lhs_ref.at[0], self.lhs_s.at[slot], self.load_sem.at[1, slot]
        ).wait()

    def first_hop(self, t):
        return self.remote(
            self.grad_s.at[lax.rem(t, 2), :, :, 1 - self.bit(0)], self.r1.at[t], self.send1.at[t],
            self.recv1.at[t], {"dp": self.partner(0)},
        )

    def a_hop(self, k, t):
        b = self.bits - 1 - k
        keep = self.half >> (k + 1)
        away = pl.ds((1 - self.bit(b)) * keep, keep)
        src = self.r1.at[t, :, away, :, 0 : WIDE // 2] if k == 0 else self.ra[k - 1].at[t, :, away]
        return self.remote(
            src, self.ra[k].at[t], self.send_a.at[k, t], self.recv_a.at[k, t], {"dp": self.partner(b)}
        )

    def b_hops(self, k, t):
        b = 1 + k
        copies = []
        for hi in range(self.half >> (k + 1)):
            away = 2 * hi + 1 - self.bit(b)
            src = self.r1.at[t, :, away, :, WIDE // 2 :] if k == 0 else self.rb[k - 1].at[t, :, away]
            copies.append(
                self.remote(
                    src, self.rb[k].at[t, :, hi], self.send_b.at[k, t], self.recv_b.at[k, t],
                    {"dp": self.partner(b)},
                )
            )
        return copies

    def b_whole(self, k, t):
        return self.remote(
            self.rb[k].at[t], self.rb[k].at[t], self.send_b.at[k, t], self.recv_b.at[k, t],
            {"dp": self.partner(1 + k)},
        )

    def z_hops(self, t):
        copies = []
        side = WIDE // 2
        for delta in range(1, self.parts):
            to = lax.rem(self.z + delta, self.parts)
            for i, buf in enumerate((self.ra[self.planes - 1], self.rb[self.planes - 1])):
                copies.append(
                    self.remote(
                        buf.at[t, to, 0],
                        self.r4.at[t, self.parts - 1 - delta, :, i * side : (i + 1) * side],
                        self.send4.at[t], self.recv4.at[t], {"mp": to},
                    )
                )
        return copies

    def z_whole(self, t):
        return self.remote(
            self.r4.at[t], self.r4.at[t], self.send4.at[t], self.recv4.at[t],
            {"mp": lax.rem(self.z + 1, self.parts)},
        )

    def tick(self, tick):
        count, planes, half, parts = self.count, self.planes, self.half, self.parts
        side = WIDE // 2

        @pl.when(tick == 0)
        def _():
            self.load(tick)

        t = tick - STRIDE * (planes + 2)

        @pl.when((t >= 0) & (t < count))
        def _():
            self.z_whole(t).wait_recv()
            left = self.ra[planes - 1][t, self.z, 0].astype(F32)
            right = self.rb[planes - 1][t, self.z, 0].astype(F32)
            for s in range(parts - 1):
                left = left + self.r4[t, s, :, 0:side].astype(F32)
                right = right + self.r4[t, s, :, side:].astype(F32)
            self.out_ref[t, :, 0:side] = left
            self.out_ref[t, :, side:] = right

        for k in range(planes - 1, -1, -1):
            t_k = tick - STRIDE * (k + 2)

            @pl.when((t_k >= 0) & (t_k < count))
            def _():
                self.a_hop(k, t_k).wait_recv()
                self.b_whole(k, t_k).wait_recv()
                keep = half >> (k + 1)
                bit_a, bit_b = self.bit(self.bits - 1 - k), self.bit(1 + k)
                for m in range(keep):
                    own_a, own_b = bit_a * keep + m, 2 * m + bit_b
                    for j in range(parts):
                        if k == 0:
                            mine_a = self.r1[t_k, j, own_a, :, 0:side]
                            mine_b = self.r1[t_k, j, own_b, :, side:]
                        else:
                            mine_a = self.ra[k - 1][t_k, j, own_a]
                            mine_b = self.rb[k - 1][t_k, j, own_b]
                        for buf, mine in ((self.ra[k], mine_a), (self.rb[k], mine_b)):
                            buf[t_k, j, m] = (buf[t_k, j, m].astype(F32) + mine.astype(F32)).astype(BF16)
                if k + 1 < planes:
                    self.a_hop(k + 1, t_k).start()
                    for copy in self.b_hops(k + 1, t_k):
                        copy.start()
                else:
                    for copy in self.z_hops(t_k):
                        copy.start()

        t_1 = tick - STRIDE

        @pl.when((t_1 >= 0) & (t_1 < count))
        def _():
            self.first_hop(t_1).wait_recv()
            slot = lax.rem(t_1, 2)
            color = self.bit(0)

            @pl.loop(0, parts)
            def _(j):
                for m in range(half):
                    self.r1[t_1, j, m] = (
                        self.r1[t_1, j, m].astype(F32) + self.grad_s[slot, j, m, color].astype(F32)
                    ).astype(BF16)

            self.a_hop(0, t_1).start()
            for copy in self.b_hops(0, t_1):
                copy.start()

        @pl.when(tick < count)
        def _():
            slot = lax.rem(tick, 2)

            @pl.when(tick + 1 < count)
            def _():
                self.load(tick + 1)

            self.load_wait(tick)

            @pl.when(tick >= 2)
            def _():
                self.first_hop(tick - 2).wait_send()

            @pl.loop(0, parts)
            def _(j):
                full = jnp.dot(self.lhs_s[slot], self.rhs_s[slot, j], preferred_element_type=F32)
                self.grad_s[slot, j] = full.astype(BF16).reshape(half, 2, self.rows, WIDE)

            self.first_hop(tick).start()

    def finish(self):
        for t in range(max(self.count - 2, 0), self.count):
            self.first_hop(t).wait_send()

        @pl.loop(0, self.count)
        def _(t):
            for k in range(self.planes):
                self.a_hop(k, t).wait_send()
                self.b_whole(k, t).wait_send()
            self.z_whole(t).wait_send()


def plan_of(pairs):
    plan = []
    for seg, (kind, right) in enumerate(pairs):
        plan += [(seg, kind)] * (right.shape[2] // WIDE)
    return plan


def scatter_kernel(bits, parts, plan, rows, lhs_ref, *refs):
    sources = len({item[0] for item in plan})
    rhs_refs, refs = refs[:sources], refs[sources:]
    vec_ref, y_ref, g_ref, out_ref, vec_out, y_out, g_out = refs[:7]
    v_acc, v_in, v_z, v_send, v_recv, v_z_send, v_z_recv = refs[7:14]
    swap_own, swap_send, swap_recv = refs[14:17]
    scatter = Scatter(bits, parts, plan, rows, lhs_ref, rhs_refs, out_ref, refs[17:])
    z = lax.axis_index("mp")
    mesh_id = pl.DeviceIdType.MESH
    greet_all(bits, parts, True)
    swaps = [
        Swap(2**bits, src, dst, swap_own.at[i], swap_send.at[i], swap_recv.at[i])
        for i, (src, dst) in enumerate(((y_ref, y_out), (g_ref, g_out)))
    ]

    def v_hop(b):
        return pltpu.make_async_remote_copy(
            src_ref=vec_ref if b == 0 else v_acc.at[b - 1], dst_ref=v_in.at[b], send_sem=v_send.at[b],
            recv_sem=v_recv.at[b], device_id={"dp": scatter.partner(b)}, device_id_type=mesh_id,
        )

    def v_z_hop(src, dst, delta):
        return pltpu.make_async_remote_copy(
            src_ref=src, dst_ref=dst, send_sem=v_z_send.at[0], recv_sem=v_z_recv.at[0],
            device_id={"mp": lax.rem(z + delta, parts)}, device_id_type=mesh_id,
        )

    def small_sum(stage):
        if stage == 0:
            v_hop(0).start()
        elif stage <= bits:
            b = stage - 1
            v_hop(b).wait_recv()
            total = (vec_ref[...] if b == 0 else v_acc[b - 1]) + v_in[b]
            if stage < bits:
                v_acc[b] = total
                v_hop(stage).start()
            else:
                v_z[z] = total
                for delta in range(1, parts):
                    v_z_hop(v_z.at[z], v_z.at[z], delta).start()
        else:
            whole = v_z.at[pl.ds(0, parts - 1)]
            v_z_hop(whole, whole, 1).wait_recv()
            total = v_z[0]
            for s in range(1, parts):
                total = total + v_z[s]
            vec_out[...] = total
            for b in range(bits):
                v_hop(b).wait_send()
            v_z_hop(whole, whole, 1).wait_send()
    for swap in swaps:
        swap.start()

    @pl.loop(0, scatter.ticks)
    def _(tick):
        for stage in range(bits + 2):
            @pl.when(tick == stage)
            def _():
                small_sum(stage)

        scatter.tick(tick)

    for swap in swaps:
        swap.finish()
    scatter.finish()


def scatter_sum(lefts, pairs, vector, block_out, d_x, groups, parts, collective):
    kinds, width, length = lefts.shape
    bits = groups.bit_length() - 1
    rows = width // groups
    plan = plan_of(pairs)
    count = len(plan)
    vmem_spec = pl.BlockSpec(memory_space=pltpu.VMEM)
    any_spec = pl.BlockSpec(memory_space=pl.ANY)
    dma = lambda *shape: pltpu.SemaphoreType.DMA(shape)
    return pl.pallas_call(
        partial(scatter_kernel, bits, parts, plan, rows),
        out_shape=(
            jax.ShapeDtypeStruct((count, rows, WIDE), F32),
            jax.ShapeDtypeStruct(vector.shape, F32),
            jax.ShapeDtypeStruct(block_out.shape, BF16),
            jax.ShapeDtypeStruct(d_x.shape, BF16),
        ),
        in_specs=[any_spec] * (1 + len(pairs)) + [vmem_spec, any_spec, any_spec],
        out_specs=(vmem_spec, vmem_spec, any_spec, any_spec),
        scratch_shapes=[
            pltpu.VMEM((bits - 1,) + vector.shape, F32),
            pltpu.VMEM((bits,) + vector.shape, F32),
            pltpu.VMEM((parts,) + vector.shape, F32),
            dma(bits), dma(bits), dma(1), dma(1),
            dma(2), dma(2), dma(2),
            *Scatter.scratch(bits, parts, count, rows, length, width),
        ],
        compiler_params=pltpu.CompilerParams(
            collective_id=collective, has_side_effects=True, vmem_limit_bytes=60 * 2**20
        ),
        cost_estimate=pl.CostEstimate(
            flops=2 * count * WIDE * parts * length * width, bytes_accessed=count * parts * length * WIDE * 2,
            transcendentals=0,
        ),
        name="scatter_sum",
    )(lefts, *[right for _, right in pairs], vector, block_out, d_x)


def backward_kernel(
    heads, parts, bits, plan, rows_held,
    dhead_ref, o_ref, gate_ref, qe_ref, phi_ref, phil_ref,
    raw_ref, halo_ref, convw_ref, ab_ref, gain_ref, s_ref, t_ref, phi_late_ref, lhs_ref, *refs,
):
    sources = len({item[0] for item in plan})
    rhs_refs, refs = refs[:sources], refs[sources:]
    dproj_ref, dab_ref, dconv_ref, dgain_ref, sums_ref = refs[:5]
    (do_s, d_s, dgate_s, dl_s, phil_s, g_s, dext_s, ext_s, send_s, recv_s, halo_send, halo_recv,
     send_sem, recv_sem, halo_send_sem, halo_recv_sem) = refs[5:21]
    scatter = Scatter(bits, parts, plan, rows_held, lhs_ref, rhs_refs, sums_ref, refs[21:])
    step = pl.program_id(0)
    early = pl.program_id(1) == 0
    z = lax.axis_index("mp")
    back = parts - 1 - z
    lag = parts - 1
    slots = lag + 1
    length = o_ref.shape[1]
    size = min(CHUNK, length)
    chunks = length // size

    @pl.when((step == 0) & early)
    def _():
        greet_all(bits, parts, False)

    now = step * 2 + pl.program_id(1)
    last = 2 * (heads + lag + 1) - 1
    stop = jnp.where(now == last, max(scatter.ticks, last + 1), now + 1)

    @pl.loop(now, stop)
    def _(tick):
        scatter.tick(tick)


    def hop(h):
        return pltpu.make_async_remote_copy(
            src_ref=send_s.at[h], dst_ref=recv_s.at[h], send_sem=send_sem.at[h],
            recv_sem=recv_sem.at[h], device_id={"mp": lax.rem(z + parts - 1, parts)},
            device_id_type=pl.DeviceIdType.MESH,
        )

    def halo_hop(h):
        return pltpu.make_async_remote_copy(
            src_ref=halo_send.at[h], dst_ref=halo_recv.at[h], send_sem=halo_send_sem.at[h],
            recv_sem=halo_recv_sem.at[h], device_id={"mp": lax.rem(z + parts - 1, parts)},
            device_id_type=pl.DeviceIdType.MESH,
        )

    @pl.when((step == 0) & early)
    def _():
        dgain_ref[...] = jnp.zeros_like(dgain_ref)
        g_s[...] = jnp.zeros_like(g_s)

    @pl.when((step == 0) & early & (back == 0))
    def _():
        recv_s[...] = jnp.zeros_like(recv_s)
        halo_recv[...] = jnp.zeros_like(halo_recv)

    @pl.when((step < heads) & early)
    def _():
        slot = lax.rem(step, slots)
        gslot = lax.rem(step, slots + 1)
        gain = gain_ref[...]
        d_gain = jnp.zeros((1, DV), F32)
        for c in range(chunks):
            at = slice(c * size, (c + 1) * size)
            out = o_ref[0, at]
            d_head = dhead_ref[0, at]
            gate = gate_ref[0, c * size : (c + 1) * size]
            scale = lax.rsqrt(jnp.mean(out * out, axis=-1, keepdims=True) + 1e-05)
            unit = out * scale
            sig = jax.nn.sigmoid(gate)
            gated = gate * sig
            both = d_head * unit
            d_gain = d_gain + jnp.sum(both * gated, axis=0, keepdims=True)
            e = d_head * gated * gain
            d_out = scale * (e - unit * jnp.mean(e * unit, axis=-1, keepdims=True))
            dgate_s[gslot, at] = (both * gain * sig * (1.0 + gate * (1.0 - sig))).astype(BF16)
            do_s[slot, at] = d_out
            d_s[slot, c] = mm(qe_ref[0, at], d_out, 0, 0)
        dgain_ref[...] += d_gain
        total = d_s[slot, chunks - 1]
        for c in range(chunks - 2, -1, -1):
            total = mm(phi_ref[0, c], total) + d_s[slot, c]
        dl_s[slot] = total
        phil_s[slot] = phil_ref[0]

    relay = step - back

    @pl.when((relay >= 0) & (relay < heads) & early)
    def _():
        slot = lax.rem(relay, slots)

        @pl.when(back > 0)
        def _():
            hop(relay).wait_recv()

        @pl.when(z > 0)
        def _():
            send_s[relay] = mm(phil_s[slot], recv_s[relay]) + dl_s[slot]
            hop(relay).start()

    @pl.when((step >= lag) & (step < lag + heads) & ~early)
    def _():
        head = step - lag
        slot = lax.rem(head, slots)
        eslot = lax.rem(head, 2)
        rows, cols = masks(size)
        upper = (rows <= cols).astype(F32)
        convw = convw_ref[0]
        d_state = recv_s[head]
        ext_s[0:HALO] = halo_ref[0, :, 0:HEADW]
        ext_s[HALO:] = raw_ref[0, 0:size, 0:HEADW]
        d_conv_rows = [jnp.zeros((1, HEADW), F32) for _ in range(TAPS)]
        for c in range(chunks - 1, -1, -1):
            at = slice(c * size, (c + 1) * size)
            shifted = windows(raw_ref, ext_s, c, size)
            conv = conv_of(shifted, convw)
            sig, q_silu, k_silu, value, q_scale, k_scale = unit_parts(conv)
            query = q_silu * (q_scale * DK ** (-0.5))
            keyed = k_silu * k_scale
            gamma_row, gamma_col, beta = decays(ab_ref, c * size, size, upper)
            inclusive, strict = fades(gamma_row, gamma_col, rows, cols)
            gram = mm(jnp.concatenate([keyed, query], axis=0), keyed, 1, 1)
            gram_f = gram[:size] * strict
            lower = beta * gram_f
            scores = gram[size:] * inclusive
            growth = jnp.exp(gamma_col)
            last = gamma_row[:, size - 1 :]
            tail = jnp.exp(last - gamma_col)
            query_g = query * growth
            grown = keyed * growth
            keyed_b = beta * grown
            keyed_g = keyed * tail
            state = s_ref[0, c]
            inverse = t_ref[0, c]
            d_out = do_s[slot, at]
            fresh = mm(inverse, beta * value - mm(keyed_b, state))
            d_fresh = mm(scores, d_out, 0, 0) + mm(keyed_g, d_state)
            d_rhs = mm(inverse, d_fresh, 0, 0)
            stacked = jnp.concatenate([d_out, d_rhs], axis=0)
            by_fresh = mm(stacked, fresh, 1, 1)
            by_state = mm(stacked, state, 1, 1)
            d_scores = by_fresh[:size] * inclusive
            d_lower = -by_fresh[size:]
            d_query_g = by_state[:size]
            d_keyed_b = -by_state[size:]
            d_keyed_g = mm(fresh, d_state, 1, 1)
            d_gram = d_lower * (beta * strict)
            by_keyed = mm(jnp.concatenate([d_scores, d_gram], axis=0), keyed)
            d_query = by_keyed[:size] + growth * d_query_g
            d_keyed = (
                by_keyed[size:]
                + mm(jnp.concatenate([d_scores, d_gram], axis=0),
                     jnp.concatenate([query, keyed], axis=0), 0, 0)
                + (beta * growth) * d_keyed_b
                + tail * d_keyed_g
            )
            d_value = beta * d_rhs
            d_beta = (
                jnp.sum(d_rhs * value, axis=-1, keepdims=True)
                + jnp.sum(d_lower * gram_f, axis=-1, keepdims=True)
                + jnp.sum(d_keyed_b * grown, axis=-1, keepdims=True)
            )
            moved = by_fresh[:size] * scores + d_lower * lower
            tail_part = jnp.sum(d_keyed_g * keyed_g, axis=-1, keepdims=True)
            d_gamma = (
                jnp.sum(moved, axis=-1, keepdims=True)
                + jnp.sum(d_query_g * query_g, axis=-1, keepdims=True)
                + jnp.sum(d_keyed_b * keyed_b, axis=-1, keepdims=True)
                - tail_part
            )
            at_end = jnp.sum(tail_part, axis=0, keepdims=True) + jnp.exp(last) * jnp.sum(
                jnp.sum(state * d_state, axis=-1, keepdims=True), axis=0, keepdims=True
            )
            lanes = lax.broadcasted_iota(jnp.int32, (size, DK), 1)
            packed = jnp.where(lanes == 0, d_gamma, jnp.where(lanes == 1, d_beta, 0.0)).T[:8]
            row_id = lax.broadcasted_iota(jnp.int32, packed.shape, 0)
            packed = packed - jnp.where(row_id == 0, jnp.sum(moved, axis=0, keepdims=True), 0.0)
            summed = mm(packed, upper, 1, 1) + at_end
            dab_ref[0, :, at] = jnp.where(row_id == 0, summed, packed)
            if c > 0:
                d_state = mm(phi_late_ref[0, c], d_state) + d_s[slot, c]
            d_q_silu = (DK ** (-0.5) * q_scale) * (
                d_query
                - q_silu * (q_scale * q_scale) * jnp.sum(q_silu * d_query, axis=-1, keepdims=True)
            )
            d_k_silu = k_scale * (
                d_keyed
                - k_silu * (k_scale * k_scale) * jnp.sum(k_silu * d_keyed, axis=-1, keepdims=True)
            )
            d_silu = jnp.concatenate([d_q_silu, d_k_silu, d_value], axis=1)
            d_conv = d_silu * sig * (1.0 + conv * (1.0 - sig))
            g_s[HALO + c * size : HALO + (c + 1) * size] = d_conv
            for i in range(TAPS):
                d_conv_rows[i] = d_conv_rows[i] + jnp.sum(shifted[i] * d_conv, axis=0, keepdims=True)
        for i in range(TAPS):
            dconv_ref[0, i : i + 1] = d_conv_rows[i]
        for base, count in [(0, HALO)] + [(HALO + c * size, size) for c in range(chunks)]:
            d_raw = None
            for i in range(TAPS):
                part = g_s[pl.ds(base + TAPS - 1 - i, count)] * convw[i : i + 1]
                d_raw = part if d_raw is None else d_raw + part
            if base == 0:
                halo_send[head] = d_raw
            else:
                dext_s[eslot, base - HALO : base - HALO + count] = d_raw

        @pl.when(z > 0)
        def _():
            halo_hop(head).start()

    @pl.when((step > lag) & ~early)
    def _():
        head = step - lag - 1
        eslot = lax.rem(head, 2)
        gslot = lax.rem(head, slots + 1)

        @pl.when(back > 0)
        def _():
            halo_hop(head).wait_recv()

        dext_s[eslot, length - HALO : length] += halo_recv[head]
        dproj_ref[0, :, 0:HEADW] = dext_s[eslot].astype(BF16)
        dproj_ref[0, :, HEADW:] = dgate_s[gslot]

    @pl.when((step == pl.num_programs(0) - 1) & ~early)
    def _():
        scatter.finish()

    @pl.when((step == pl.num_programs(0) - 1) & ~early & (z > 0))
    def _():
        @pl.loop(0, heads)
        def _(h):
            hop(h).wait_send()
            halo_hop(h).wait_send()


def forward_core(raw, convw, ab, gain, weights, heads, parts, groups):
    bits = groups.bit_length() - 1
    pieces = []
    for w, weight in enumerate(weights):
        wide = weight.shape[1]
        pieces += [(w, at, at + WIDE // 2, at + WIDE) for at in range(0, wide, WIDE)]
    rows = weights[0].shape[0]
    any_spec = pl.BlockSpec(memory_space=pl.ANY)
    length = raw.shape[1]
    size = min(CHUNK, length)
    chunks = length // size
    per = heads // raw.shape[0]
    lag = parts - 1
    slots = lag + 1
    now = lambda s: jnp.minimum(s, heads - 1)
    late = lambda s: jnp.maximum(s - lag, 0)
    return pl.pallas_call(
        partial(forward_kernel, heads, parts, bits, pieces),
        grid=(heads + lag, 2),
        out_shape=(
            jax.ShapeDtypeStruct((raw.shape[0], length, per * DV), BF16),
            jax.ShapeDtypeStruct((heads, length, DV), F32),
            jax.ShapeDtypeStruct((heads, chunks, DK, DV), F32),
            jax.ShapeDtypeStruct((heads, chunks, size, size), F32),
            jax.ShapeDtypeStruct((heads, length, DK), F32),
            jax.ShapeDtypeStruct((heads, chunks, DK, DK), F32),
            jax.ShapeDtypeStruct((heads, DK, DK), F32),
            jax.ShapeDtypeStruct((parts, HALO, per * (HEADW + DV)), F32),
            *[jax.ShapeDtypeStruct((parts, groups) + w.shape, BF16) for w in weights],
        ),
        in_specs=[
            pl.BlockSpec((1, length, HEADW + DV), lambda s, _: (now(s) // per, 0, now(s) % per)),
            pl.BlockSpec((1, length, DV), lambda s, _: (late(s) // per, 0, (late(s) % per) * 3 + 2)),
            any_spec,
            pl.BlockSpec((1, TAPS, HEADW), lambda s, _: (now(s), 0, 0)),
            pl.BlockSpec((1, 8, length), lambda s, _: (now(s), 0, 0)),
            pl.BlockSpec((1, DV), lambda s, _: (0, 0)),
            *[any_spec] * len(weights),
        ],
        out_specs=(
            pl.BlockSpec((1, length, DV), lambda s, _: (late(s) // per, 0, late(s) % per)),
            pl.BlockSpec((1, length, DV), lambda s, _: (late(s), 0, 0)),
            pl.BlockSpec((1, chunks, DK, DV), lambda s, _: (late(s), 0, 0, 0)),
            pl.BlockSpec((1, chunks, size, size), lambda s, _: (now(s), 0, 0, 0)),
            pl.BlockSpec((1, length, DK), lambda s, _: (now(s), 0, 0)),
            pl.BlockSpec((1, chunks, DK, DK), lambda s, _: (now(s), 0, 0, 0)),
            pl.BlockSpec((1, DK, DK), lambda s, _: (now(s), 0, 0)),
            pl.BlockSpec((parts, HALO, per * (HEADW + DV)), lambda s, _: (0, 0, 0)),
            *[any_spec] * len(weights),
        ),
        scratch_shapes=[
            pltpu.VMEM((slots, length, DK), F32),
            pltpu.VMEM((slots, length, DV), F32),
            pltpu.VMEM((slots, chunks, DK, DK), F32),
            pltpu.VMEM((slots, chunks, DK, DV), F32),
            pltpu.VMEM((slots, DK, DK), F32),
            pltpu.VMEM((slots, DK, DV), F32),
            pltpu.VMEM((heads, DK, DV), F32),
            pltpu.VMEM((heads, DK, DV), F32),
            pltpu.VMEM((parts, HALO, per * (HEADW + DV)), F32),
            pltpu.VMEM((HALO + size, HEADW), F32),
            pltpu.SemaphoreType.DMA((heads,)),
            pltpu.SemaphoreType.DMA((heads,)),
            pltpu.SemaphoreType.DMA((parts,)),
            pltpu.SemaphoreType.DMA((parts,)),
            *Gather.scratch(bits, len(pieces)),
        ],
        compiler_params=pltpu.CompilerParams(
            collective_id=0, has_side_effects=True, vmem_limit_bytes=56 * 2**20
        ),
        cost_estimate=pl.CostEstimate(flops=20 * 10**9, bytes_accessed=40 * 2**20, transcendentals=0),
        name="delta_forward",
    )(raw, raw, raw, convw, ab, gain, *weights)


def backward_core(d_head, out, raw, halo, query_e, phi, phi_all, convw, ab, gain, states, inverses, lefts, pairs,
                  heads, parts, groups):
    length = raw.shape[1]
    size = min(CHUNK, length)
    chunks = length // size
    per = heads // raw.shape[0]
    lag = parts - 1
    slots = lag + 1
    bits = groups.bit_length() - 1
    plan = plan_of(pairs)
    rows = lefts.shape[1] // groups
    any_spec = pl.BlockSpec(memory_space=pl.ANY)
    now = lambda s: jnp.minimum(s, heads - 1)
    late = lambda s: jnp.clip(s - lag, 0, heads - 1)
    later = lambda s: jnp.maximum(s - lag - 1, 0)
    return pl.pallas_call(
        partial(backward_kernel, heads, parts, bits, plan, rows),
        grid=(heads + lag + 1, 2),
        out_shape=(
            jax.ShapeDtypeStruct((raw.shape[0], length, per * (HEADW + DV)), BF16),
            jax.ShapeDtypeStruct((heads, 8, length), F32),
            jax.ShapeDtypeStruct((heads, TAPS, HEADW), F32),
            jax.ShapeDtypeStruct((1, DV), F32),
            jax.ShapeDtypeStruct((len(plan), rows, WIDE), F32),
        ),
        in_specs=[
            pl.BlockSpec((1, length, DV), lambda s, _: (now(s) // per, 0, now(s) % per)),
            pl.BlockSpec((1, length, DV), lambda s, _: (now(s), 0, 0)),
            pl.BlockSpec((1, length, DV), lambda s, _: (now(s) // per, 0, (now(s) % per) * 3 + 2)),
            pl.BlockSpec((1, length, DK), lambda s, _: (now(s), 0, 0)),
            pl.BlockSpec((1, chunks, DK, DK), lambda s, _: (now(s), 0, 0, 0)),
            pl.BlockSpec((1, DK, DK), lambda s, _: (now(s), 0, 0)),
            pl.BlockSpec((1, length, HEADW + DV), lambda s, _: (late(s) // per, 0, late(s) % per)),
            pl.BlockSpec((1, HALO, HEADW + DV), lambda s, _: (late(s) // per, 0, late(s) % per)),
            pl.BlockSpec((1, TAPS, HEADW), lambda s, _: (late(s), 0, 0)),
            pl.BlockSpec((1, 8, length), lambda s, _: (late(s), 0, 0)),
            pl.BlockSpec((1, DV), lambda s, _: (0, 0)),
            pl.BlockSpec((1, chunks, DK, DV), lambda s, _: (late(s), 0, 0, 0)),
            pl.BlockSpec((1, chunks, size, size), lambda s, _: (late(s), 0, 0, 0)),
            pl.BlockSpec((1, chunks, DK, DK), lambda s, _: (late(s), 0, 0, 0)),
            *[any_spec] * (1 + len(pairs)),
        ],
        out_specs=(
            pl.BlockSpec((1, length, HEADW + DV), lambda s, _: (later(s) // per, 0, later(s) % per)),
            pl.BlockSpec((1, 8, length), lambda s, _: (late(s), 0, 0)),
            pl.BlockSpec((1, TAPS, HEADW), lambda s, _: (late(s), 0, 0)),
            pl.BlockSpec((1, DV), lambda s, _: (0, 0)),
            pl.BlockSpec((len(plan), rows, WIDE), lambda s, _: (0, 0, 0)),
        ),
        scratch_shapes=[
            pltpu.VMEM((slots, length, DV), F32),
            pltpu.VMEM((slots, chunks, DK, DV), F32),
            pltpu.VMEM((slots + 1, length, DV), BF16),
            pltpu.VMEM((slots, DK, DV), F32),
            pltpu.VMEM((slots, DK, DK), F32),
            pltpu.VMEM((length + 2 * HALO, HEADW), F32),
            pltpu.VMEM((2, length, HEADW), F32),
            pltpu.VMEM((HALO + size, HEADW), F32),
            pltpu.VMEM((heads, DK, DV), F32),
            pltpu.VMEM((heads, DK, DV), F32),
            pltpu.VMEM((heads, HALO, HEADW), F32),
            pltpu.VMEM((heads, HALO, HEADW), F32),
            pltpu.SemaphoreType.DMA((heads,)),
            pltpu.SemaphoreType.DMA((heads,)),
            pltpu.SemaphoreType.DMA((heads,)),
            pltpu.SemaphoreType.DMA((heads,)),
            *Scatter.scratch(bits, parts, len(plan), rows, length, lefts.shape[1]),
        ],
        compiler_params=pltpu.CompilerParams(
            collective_id=1, has_side_effects=True, vmem_limit_bytes=62 * 2**20
        ),
        cost_estimate=pl.CostEstimate(flops=40 * 10**9, bytes_accessed=60 * 2**20, transcendentals=0),
        name="delta_backward",
    )(d_head, out, raw, query_e, phi, phi_all, raw, halo, convw, ab, gain, states, inverses, phi,
      lefts, *[right for _, right in pairs])


def dot(spec, a, b):
    return jnp.einsum(spec, a, b, preferred_element_type=F32)


def unit_rms(v):
    return lax.rsqrt(jnp.mean(v * v, axis=-1, keepdims=True) + 1e-05)


def per_device(
    tokens, out_grad, seq_lengths, mix_gain, w_query, w_key, w_value, w_outgate, w_decay, w_beta,
    conv_weight, rate_log, step_bias, head_gain, w_out, ffn_gain, w_ffn_gate, w_ffn_up, w_ffn_down,
):
    groups = lax.axis_size("dp")
    parts = lax.axis_size("mp")
    group = lax.axis_index("dp")
    share = lax.axis_index("mp")
    heads = rate_log.shape[0]
    per = heads // parts
    width = tokens.shape[2]
    local_rows = w_query.shape[0]

    def by_head(w, size):
        return w.reshape(local_rows, per, size)

    joined = jnp.concatenate(
        [by_head(w_query, DK), by_head(w_key, DK), by_head(w_value, DV), by_head(w_outgate, DV)], axis=2
    ).reshape(local_rows, per * (HEADW + DV))
    main_cols = joined.shape[1]

    hidden = w_ffn_gate.shape[1]
    wide = -(-hidden // WIDE) * WIDE
    small_w = jnp.concatenate([w_decay, w_beta], axis=1)
    lanes = -(-small_w.shape[1] // 128) * 128
    widen = lambda w, size: jnp.pad(w, ((0, 0), (0, size - w.shape[1])))
    x_bf, dy_bf, g_proj, g_small = prologue(
        tokens, out_grad, joined, widen(small_w, lanes), groups, parts
    )
    whole = lambda g: g.reshape(parts, width, g.shape[3])
    g_proj = whole(g_proj)
    g_small = whole(g_small)
    x_bf = x_bf.reshape(-1, width)
    dy_bf = dy_bf.reshape(-1, width)
    length = x_bf.shape[0]

    my_length = lax.dynamic_slice_in_dim(seq_lengths, group, 1)
    positions = share * length + jnp.arange(length, dtype=jnp.int32)
    live = (positions < my_length).astype(F32)[:, None]

    x = x_bf.astype(F32)
    dy = live * dy_bf.astype(F32)
    d_ffo = dy.astype(BF16)
    scale1 = unit_rms(x)
    n1 = x * scale1
    h1 = (n1 * mix_gain).astype(BF16)
    raw = dot("td,gdc->gtc", h1, g_proj)
    small = dot("td,gdc->gct", h1, g_small)[:, : 2 * per]
    decay_raw = small[:, :per].reshape(heads, length)
    beta_raw = small[:, per:].reshape(heads, length)
    rate = -jnp.exp(rate_log)[:, None]
    shifted = decay_raw + step_bias[:, None]
    decay = rate * jax.nn.softplus(shifted)
    beta = jax.nn.sigmoid(beta_raw)
    ab = jnp.concatenate(
        [decay[:, None], beta[:, None], jnp.zeros((heads, 6, length), F32)], axis=1
    )
    taps = conv_weight.shape[0]
    key_cols = heads * DK
    convw = jnp.concatenate(
        [
            conv_weight[:, :key_cols].reshape(taps, heads, DK),
            conv_weight[:, key_cols : 2 * key_cols].reshape(taps, heads, DK),
            conv_weight[:, 2 * key_cols :].reshape(taps, heads, DV),
        ],
        axis=2,
    ).transpose(1, 0, 2)
    gain_row = head_gain[None]
    head_out, mixed, states, inverses, query_e, phi, phi_all, halo, *rest = forward_core(
        raw, convw, ab, gain_row,
        [w_out] + [widen(w, wide) for w in (w_ffn_gate, w_ffn_up, w_ffn_down)],
        heads, parts, groups,
    )
    g_out, g_gate, g_up, g_down = [whole(w) for w in rest]

    x1 = x + dot("gtc,gmc->tm", head_out, g_out)
    scale2 = unit_rms(x1)
    n2 = x1 * scale2
    h2 = (n2 * ffn_gain).astype(BF16)
    gate = dot("td,gdf->gtf", h2, g_gate)
    up = dot("td,gdf->gtf", h2, g_up)
    sig = jax.nn.sigmoid(gate)
    act = (gate * sig * up).astype(BF16)
    block_out = (live * (x1 + dot("gtf,gdf->td", act, g_down))).astype(BF16)
    d_act = dot("td,gdf->gtf", d_ffo, g_down)
    d_gate = (d_act * up * sig * (1.0 + gate * (1.0 - sig))).astype(BF16)
    d_up = (d_act * gate * sig).astype(BF16)
    d_h2 = dot("gtf,gdf->td", d_gate, g_gate) + dot("gtf,gdf->td", d_up, g_up)
    e2 = d_h2 * ffn_gain
    d_x1 = dy + scale2 * (e2 - n2 * jnp.mean(e2 * n2, axis=-1, keepdims=True))
    ffn_gain_grad = jnp.sum(d_h2 * n2, axis=0)
    d_mix = d_x1.astype(BF16)
    d_head = dot("tm,gmc->gtc", d_mix, g_out)

    d_proj, d_ab, d_convw, d_head_gain, sums_ffn = backward_core(
        d_head, mixed, raw, halo, query_e, phi, phi_all, convw, ab, gain_row, states, inverses,
        jnp.stack([d_mix.T, h2.T, d_ffo.T]), [(2, act), (1, d_gate), (1, d_up), (0, head_out)],
        heads, parts, groups,
    )
    d_decay = d_ab[:, 0]
    d_beta_raw = d_ab[:, 1] * beta * (1.0 - beta)
    d_decay_raw = d_decay * rate * jax.nn.sigmoid(shifted)
    rate_grad = jnp.sum(d_decay * decay, axis=1)
    bias_grad = jnp.sum(d_decay_raw, axis=1)
    d_small = jnp.concatenate(
        [d_decay_raw.reshape(parts, per, length), d_beta_raw.reshape(parts, per, length)], axis=1
    ).astype(BF16)
    small_grad = dot("gct,td->gcd", d_small, h1)
    d_h1 = dot("gtc,gdc->td", d_proj, g_proj) + dot("gct,gdc->td", d_small, g_small[:, :, : 2 * per])
    e1 = d_h1 * mix_gain
    d_x = d_x1 + scale1 * (e1 - n1 * jnp.mean(e1 * n1, axis=-1, keepdims=True))
    mix_gain_grad = jnp.sum(d_h1 * n1, axis=0)
    per_head = d_convw.transpose(1, 0, 2)
    d_conv = jnp.concatenate(
        [
            per_head[:, :, :DK].reshape(taps, key_cols),
            per_head[:, :, DK : 2 * DK].reshape(taps, key_cols),
            per_head[:, :, 2 * DK :].reshape(taps, heads * DV),
        ],
        axis=1,
    )
    vector = jnp.concatenate(
        [mix_gain_grad, ffn_gain_grad, d_head_gain[0], d_conv.reshape(-1), rate_grad, bias_grad,
         small_grad.reshape(-1)]
    )
    used = vector.shape[0]
    vector = jnp.pad(vector, (0, -used % 1024)).reshape(-1, 128)
    sums_proj, sums, final_out, final_grad = scatter_sum(
        h1.T[None], [(0, d_proj)],
        vector, block_out.reshape(tokens.shape), d_x.astype(BF16).reshape(tokens.shape),
        groups, parts, 2,
    )
    sums = sums.reshape(-1)

    sums_w = jnp.concatenate([sums_ffn, sums_proj], axis=0)

    def columns(start, size):
        pieces = -(-size // WIDE)
        return sums_w[start : start + pieces].transpose(1, 0, 2).reshape(local_rows, -1)[:, :size]

    step = wide // WIDE
    s_down = columns(0, hidden)
    s_gate = columns(step, hidden)
    s_up = columns(2 * step, hidden)
    s_out = columns(3 * step, per * DV)
    s_proj = columns(3 * step + per * DV // WIDE, main_cols)
    pieces = []
    start = 0
    for count in (width, width, DV, taps * conv_weight.shape[1], heads, heads):
        pieces.append(sums[start : start + count])
        start += count
    small_sum = sums[start:used].reshape(parts, 2 * per, width)
    mine = lax.dynamic_slice(small_sum, (share, 0, group * local_rows), (1, 2 * per, local_rows))[0].T

    by = s_proj.reshape(local_rows, per, HEADW + DV)
    flat = lambda v: v.reshape(local_rows, -1)
    return (
        final_out,
        final_grad,
        pieces[0],
        flat(by[:, :, :DK]),
        flat(by[:, :, DK : 2 * DK]),
        flat(by[:, :, 2 * DK : HEADW]),
        flat(by[:, :, HEADW:]),
        mine[:, :per],
        mine[:, per:],
        pieces[3].reshape(conv_weight.shape),
        pieces[4],
        pieces[5],
        pieces[2],
        s_out,
        pieces[1],
        s_gate,
        s_up,
        s_down,
    )


def solution(mesh):
    seq = P(None, ("mp", "dp"), None)
    shard = P("dp", "mp")
    rep = P()
    return jax.shard_map(
        per_device,
        mesh=mesh,
        in_specs=(
            seq, seq, rep, rep, shard, shard, shard, shard, shard, shard,
            rep, rep, rep, rep, shard, rep, shard, shard, shard,
        ),
        out_specs=(
            seq, seq, rep, shard, shard, shard, shard, shard, shard,
            rep, rep, rep, rep, shard, rep, shard, shard, shard,
        ),
        check_vma=False,
    )
```

time: 964 us -> 614 us (0.64)
  waiting for transfers between devices: 257 us -> 0 us
  Pallas kernels: 396 us -> 474 us
  blocking collectives: 75.4 us -> 0 us
  local copies, waits for them, and re-layouts: 78.2 us -> 36.2 us
  other arithmetic: 32.1 us -> 16.8 us
  between operations: 15 us -> 1.7 us
  starting transfers between devices: 13.1 us -> 0 us
    all_gather x5 -> x0, waiting for transfers between devices: 186 us -> none  [gathered(): whole = lax.all_gather(w, ('mp', 'dp'), axis=0, tiled=True)]
    pallas_call x3 -> x4, Pallas kernels: 396 us -> 474 us  [the longest x1 156 us: backward_core(): pl.pallas_call(partial(backward_kernel, heads, parts, bits, plan, rows),...]
    psum x1 -> x0, waiting for transfers between devices: 61 us -> none  [per_device(): lax.psum(jnp.concatenate([mix_gain_grad, ffn_gain_grad, d_head_gain[0], d...]
    all_gather x1 -> x0, blocking collectives: 52.2 us -> none  [gathered(): whole = lax.all_gather(w, ('mp', 'dp'), axis=0, tiled=True)]
    all_to_all x1 -> x0, blocking collectives: 23.1 us -> none  [per_device(): lax.all_to_all(tokens, 'dp', split_axis=0, concat_axis=1, tiled=True)[0]]
    unnamed x3 -> x4, other arithmetic: 16.3 us -> 0.02 us
    unnamed x95 -> x111, local copies, waits for them, and re-layouts: 25 us -> 11.7 us
    all_to_all x3 -> x0, starting transfers between devices: 11.6 us -> none  [the longest x1 4.24 us: per_device(): lax.all_to_all(block_out[None], 'dp', split_axis=1, concat_axis=0, tiled=...]
  transfers between devices with their start and end apart: 10 -> 0, of which waited for: 6 -> 0; matrix products, arithmetic and copies ran while one was open for 12% -> 0% of each run, Pallas kernels for 9% -> 0%
where the time goes in v2:
time: 614 us; the launch traced here: 610 us
  Pallas kernels  474 us (77%)
  matrix products  81.7 us (13%)
  local copies, waits for them, and re-layouts  36.2 us (6%)
  other arithmetic  16.8 us (3%)
    pallas_call x1, Pallas kernels, backward_core(): pl.pallas_call(partial(backward_kernel, heads, parts, bits, plan, rows),...  156 us
    pallas_call x1, Pallas kernels, forward_core(): pl.pallas_call(partial(forward_kernel, heads, parts, bits, pieces), grid=...  134 us
    pallas_call x1, Pallas kernels, scatter_sum(): pl.pallas_call(partial(scatter_kernel, bits, parts, plan, rows), out_shap...  93.9 us
    pallas_call x1, Pallas kernels, prologue(): pl.pallas_call(partial(prologue_kernel, bits, parts, pieces), out_shape=(...  89.7 us
    dot_general x13, matrix products, dot(): return jnp.einsum(spec, a, b, preferred_element_type=F32)  81.7 us

profile of v2, /device:TPU:0, one launch (start us, length us, event | category | flops | bytes accessed | tf_op | source)
XLA Modules:
  0.0 610.1 jit_solution(12235489414021841587)
XLA Ops:
  8.2 89.7 %prologue.1 = (bf16[8,64,1024]{2,1,0:T(8,128)(2,1)}, bf16[8,64,1024]{2,1,0:T(8,128)(2,1)}, bf16[4,8,128,1536]{3,2,1,0:T(8,128)(2,1)}, bf16[4,8,128,128]{3,2,1,0:T(8,128)(2,1)}) custom-call(bf16[8,64,1024]{2,1,0:T(8,128)(2,1)} %refs_0_.2, bf16[8,64,1024]{2,1,0:T(8,128)(2,1)} %refs_1_.1, bf16[128,1536]{1,0:T(8,128)(2,1)} %bitcast.194, ...), custom_call_target="tpu_custom_call" | custom-call | bytes 41943040 | tf_op jit(solution)/shard_map/prologue/pallas_call | solution.py:307
  97.9 1.5 multiply_reduce_fusion.5
  99.4 3.1 multiply_convert_fusion.1
  105.8 14.4 %convolution_bitcast_fusion.raw_ref.gate_ref.raw_any = f32[4,512,1536]{2,1,0:T(8,128)} fusion(bf16[512,1024,1]{1,0,2:T(8,128)(2,1)S(1)} %bitcast.201, bf16[4,1024,1536]{2,1,0:T(8,128)(2,1)} %bitcast.221), kind=kOutput, calls=%fused_computation | convolution fusion | flops 6442450944 | bytes 26214400 | tf_op jit(solution)/shard_map/td,gdc->gtc/dot_general | solution.py:1226
  123.4 133.9 %delta_forward.1 = (bf16[4,512,512]{2,1,0:T(8,128)(2,1)}, f32[8,512,256]{2,1,0:T(8,128)}, f32[8,4,128,256]{3,2,1,0:T(8,128)}, f32[8,4,128,128]{3,2,1,0:T(8,128)}...) custom-call(f32[4,512,1536]{2,1,0:T(8,128)} %convolution_bitcast_fus, ...), custom_call_target="tpu_custom_call" | custom-call | flops 20000000000 | bytes 41943040 | tf_op jit(solution)/shard_map/delta_forward/pallas_call | solution.py:1089
  258.3 6.0 multiply_reduce_fusion.4
  264.4 5.7 fusion.19
  270.1 5.5 fusion.45
  275.6 12.1 %fusion.9 = (bf16[4,512,768]{2,1,0:T(8,128)(2,1)}, bf16[4,512,768]{2,1,0:T(8,128)(2,1)}, bf16[4,512,768]{2,1,0:T(8,128)(2,1)}) fusion(f32[4,768,512]{1,2,0:T(8,128)} %fusion.19, f32[4,768,512]{1,2,0:T(8,128)} %fusion.45, bf16[4,1024,768]{2,1,0:T(8,128)(2,1)S(1)} %bitcast.232, f32[512,1024]{0,1:T(8,128)S(1)} %get-tuple-element.141, f32[1024]{0:T(1024)S(1)} %copy-done.29, ...), kind=kOutput, calls=%fused_computation.14 | convolution fusion | flops 3247964160 | bytes 30414848 | tf_op jit(solution)/shard_map/td,gdf->gtf/dot_general | solution.py:1226
  288.4 5.3 fusion.12
  293.7 1.3 copy.141
  297.2 5.9 fusion.43
  303.2 5.0 multiply_reduce_fusion.1
  308.2 1.7 copy.120
  309.9 2.9 convert_bitcast_fusion
  312.9 1.9 pad_maximum_fusion.lhs_ref
  315.5 1.4 copy-done.40
  317.0 4.9 convolution_bitcast_fusion.1.dhead_ref
  321.8 156.2 %delta_backward.1 = (bf16[4,512,1536]{2,1,0:T(8,128)(2,1)}, f32[8,8,512]{2,1,0:T(8,128)}, f32[8,4,512]{2,1,0:T(4,128)}, f32[1,256]{1,0:T(1,128)}, f32[11,128,256]{2,1,0:T(8,128)}) custom-call(f32[4,512,512]{2,1,0:T(8,128)} %convolution_bitcast_fusion.1.dhead_ref, f32[8,512,256]{2,1,0:T(8,128)} %get-tuple-element.52.o_ref, ...), custom_call_target="tpu_custom_call" | custom-call | flops 40000000000 | bytes 62914560 | tf_op jit(solution)/shard_map/delta_backward/pallas_call | solution.py:1163
  478.2 12.8 %fusion.44 = f32[512,1024,1]{0,1,2:T(8,128)} fusion(bf16[4,512,1536]{2,1,0:T(8,128)(2,1)} %get-tuple-element.59.refs_0_, bf16[4,1024,1536]{2,1,0:T(8,128)(2,1)} %bitcast.222), kind=kOutput, calls=%fused_computation.105 | convolution fusion | flops 6442450944 | bytes 20971520 | tf_op jit(solution)/shard_map/gtc,gdc->td/dot_general | solution.py:1226
  493.4 2.7 multiply_reduce_fusion
  496.1 1.6 add_convert_fusion
  500.7 93.9 %scatter_sum.1 = (f32[6,128,256]{2,1,0:T(8,128)}, f32[280,128]{1,0:T(8,128)}, bf16[8,64,1024]{2,1,0:T(8,128)(2,1)}, bf16[8,64,1024]{2,1,0:T(8,128)(2,1)}) custom-call(bf16[1,1024,512]{2,1,0:T(8,128)(2,1)} %get-tuple-element.118.lhs_ref, bf16[4,512,1536]{2,1,0:T(8,128)(2,1)} %get-tuple-element.59.refs_0_, f32[280,128]{1,0:T(8,128)} %pad_bitcast_fusion.refs_1_, ...), custom_call_target="tpu_custom_call" | custom-call | flops 6442450944 | bytes 6291456 | tf_op jit(solution)/shard_map/scatter_sum/pallas_call | solution.py:806
  594.6 1.4 copy.143
  (183 shorter events, 37.3 us)
Async XLA Ops:
  0.7 6.7 %copy-start.37 = (bf16[128,2]{0,1:T(2,128)(2,1)S(1)}, bf16[128,2]{0,1:T(2,128)(2,1)}, u32[]{:S(2)}) copy-start(bf16[128,2]{0,1:T(2,128)(2,1)} %param.27) | copy-start | bytes 1540
  0.7 6.7 %copy-start.36 = (bf16[128,2]{0,1:T(2,128)(2,1)S(1)}, bf16[128,2]{0,1:T(2,128)(2,1)}, u32[]{:S(2)}) copy-start(bf16[128,2]{0,1:T(2,128)(2,1)} %param.28) | copy-start | bytes 1540
  6.6 92.8 %copy-start.24 = (f32[1024]{0:T(1024)S(1)}, f32[1024]{0:T(1024)}, u32[]{:S(2)}) copy-start(f32[1024]{0:T(1024)} %param.22) | copy-start | bytes 12292
  105.7 14.5 %copy-start.23 = (f32[4,4096]{1,0:T(4,128)S(1)}, f32[4,4096]{1,0:T(4,128)}, u32[]{:S(2)}) copy-start(f32[4,4096]{1,0:T(4,128)} %param.29) | copy-start | bytes 196612
  105.7 14.5 %slice-start = ((f32[4,4096]{1,0:T(4,128)}), f32[4,2048]{1,0:T(4,128)S(1)}, s32[]{:S(2)}) async-start(f32[4,4096]{1,0:T(4,128)} %param.29), calls=%async_computation | async-start | bytes 65536 | tf_op jit(solution)/shard_map/slice | solution.py:1296
  105.7 15.1 %copy-start.15 = (bf16[128,704]{0,1:T(8,128)(2,1)S(1)}, bf16[128,704]{0,1:T(8,128)(2,1)}, u32[]{:S(2)}) copy-start(bf16[128,704]{0,1:T(8,128)(2,1)} %param.35) | copy-start | bytes 540676
  105.7 16.0 %copy-start.16 = (bf16[128,704]{0,1:T(8,128)(2,1)S(1)}, bf16[128,704]{0,1:T(8,128)(2,1)}, u32[]{:S(2)}) copy-start(bf16[128,704]{0,1:T(8,128)(2,1)} %param.36) | copy-start | bytes 540676
  105.7 16.8 %copy-start.17 = (bf16[128,704]{0,1:T(8,128)(2,1)S(1)}, bf16[128,704]{0,1:T(8,128)(2,1)}, u32[]{:S(2)}) copy-start(bf16[128,704]{0,1:T(8,128)(2,1)} %param.37) | copy-start | bytes 540676
  123.4 133.9 %copy-start.2 = (bf16[8,64,1024]{2,1,0:T(8,128)(2,1)S(1)}, bf16[8,64,1024]{2,1,0:T(8,128)(2,1)}, u32[]{:S(2)}) copy-start(bf16[8,64,1024]{2,1,0:T(8,128)(2,1)} %get-tuple-element.43) | copy-start | bytes 3145732
  258.3 6.0 copy-start
  258.3 6.0 copy-start.29
  258.3 6.0 copy-start.39
  258.3 11.8 %slice-start.5 = ((s8[6291456]{0:T(1024)(128)(4,1)}), s8[4194304]{0:T(1024)(128)(4,1)S(1)}, s32[]{:S(2)}) async-start(s8[6291456]{0:T(1024)(128)(4,1)} %bitcast.233), calls=%async_computation.5 | async-start | bytes 8388608
  264.3 24.1 %copy-start.5 = (f32[512,1024]{0,1:T(8,128)}, f32[512,1024]{0,1:T(8,128)S(1)}, u32[]{:S(2)}) copy-start(f32[512,1024]{0,1:T(8,128)S(1)} %get-tuple-element.141) | copy-start | bytes 6291460
  264.4 11.2 %slice-start.3 = ((s8[6291456]{0:T(1024)(128)(4,1)}), s8[2097152]{0:T(1024)(128)(4,1)S(1)}, s32[]{:S(2)}) async-start(s8[6291456]{0:T(1024)(128)(4,1)} %bitcast.230), calls=%async_computation.3 | async-start | bytes 4194304
  295.7 7.4 %slice-start.1 = ((s8[6291456]{0:T(1024)(128)(4,1)}), s8[4194304]{0:T(1024)(128)(4,1)S(1)}, s32[]{:S(2)}) async-start(s8[6291456]{0:T(1024)(128)(4,1)} %bitcast.226), calls=%async_computation.1 | async-start | bytes 8388608
  478.1 14.0 %copy-start.33 = (f32[8]{0:T(128)S(1)}, f32[8]{0:T(128)}, u32[]{:S(2)}) copy-start(f32[8]{0:T(128)} %copy-done.32) | copy-start | bytes 100
  478.1 14.1 %copy-start.31 = (f32[8]{0:T(128)S(1)}, f32[8]{0:T(128)}, u32[]{:S(2)}) copy-start(f32[8]{0:T(128)} %param.31) | copy-start | bytes 100
  478.1 15.1 %copy-start.21 = (f32[4,2,512]{2,1,0:T(2,128)S(1)}, f32[4,2,512]{2,1,0:T(2,128)}, u32[]{:S(2)}) copy-start(f32[4,2,512]{2,1,0:T(2,128)} %copy-done.20) | copy-start | bytes 49156
  478.1 15.2 %copy-start.28 = (f32[8,64]{1,0:T(8,128)S(1)}, f32[8,64]{1,0:T(8,128)}, u32[]{:S(2)}) copy-start(f32[8,64]{1,0:T(8,128)} %copy-done.27) | copy-start | bytes 6148
  478.1 15.2 %copy-start.1 = (f32[512,1024]{0,1:T(8,128)S(1)}, f32[512,1024]{0,1:T(8,128)}, u32[]{:S(2)}) copy-start(f32[512,1024]{0,1:T(8,128)} %copy-done) | copy-start | bytes 6291460
  478.1 15.2 %copy-start.14 = (bf16[4,8,128,128]{3,2,1,0:T(8,128)(2,1)S(1)}, bf16[4,8,128,128]{3,2,1,0:T(8,128)(2,1)}, u32[]{:S(2)}) copy-start(bf16[4,8,128,128]{3,2,1,0:T(8,128)(2,1)} %get-tuple-element.45) | copy-start | bytes 3145732
  478.1 15.2 %copy-start.25 = (f32[1024]{0:T(1024)S(1)}, f32[1024]{0:T(1024)}, u32[]{:S(2)}) copy-start(f32[1024]{0:T(1024)} %param.22) | copy-start | bytes 12292
  596.0 6.4 %copy-start.9 = (f32[11,128,256]{2,1,0:T(8,128)S(1)}, f32[11,128,256]{2,1,0:T(8,128)}, u32[]{:S(2)}) copy-start(f32[11,128,256]{2,1,0:T(8,128)} %get-tuple-element.67) | copy-start | bytes 4325380
  (26 other events, 82.7 us)

commit v3 on v2

--- a/solution.py
+++ b/solution.py
@@ -29,6 +29,10 @@
     a_high, a_low = halves(a)
     b_high, b_low = halves(b)
     one = lambda p, q: lax.dot_general(p, q, dims, preferred_element_type=F32)
+    if a.shape[ca] <= 128:
+        return one(
+            jnp.concatenate([a_high, a_low], axis=ca), jnp.concatenate([b_high, b_high], axis=cb)
+        ) + one(a_high, b_low)
     return one(a_high, b_high) + (one(a_high, b_low) + one(a_low, b_high))
 
 
@@ -218,9 +222,10 @@
             block, block, self.s_send.at[p], self.s_recv.at[p], {"dp": self.flip(self.d, 0)}
         )
 
-    def finish(self):
+    def finish(self, waited=()):
         for p in range(len(self.pieces)):
-            self.s_whole(p).wait_recv()
+            if p not in waited:
+                self.s_whole(p).wait_recv()
             self.z_whole(p).wait_send()
             for k in range(self.bits - 1):
                 for copy in self.along_whole(p, k):
@@ -277,48 +282,148 @@
 
 
 def prologue_kernel(bits, parts, pieces, *refs):
-    tokens, grads, joined, small, tokens_out, grads_out, joined_out, small_out = refs[:8]
-    sems = refs[8:]
+    tokens, small, gain, *refs = refs
+    members, narrow, refs = refs[:4], refs[4:7], refs[7:]
+    tokens_out, joined_out, small_out, raw_out, h1_out, h1t_out = refs[:6]
+    padded, refs = refs[6:9], refs[9:]
+    member_s, narrow_s, padded_s, refs = refs[:4], refs[4:7], refs[7:10], refs[10:]
+    in_sem, out_sem, joined, x_s, w_s, raw_s, x_sem, w_sem, raw_sem, *sems = refs
+    loads = [
+        pltpu.make_async_copy(src, dst, in_sem.at[i])
+        for i, (src, dst) in enumerate(zip((*members, *narrow), (*member_s, *narrow_s)))
+    ]
+    for load in loads:
+        load.start()
     gather = Gather(bits, parts, (joined, small), (joined_out, small_out), pieces, sems[:7])
-    swaps = [
-        Swap(2**bits, tokens, tokens_out, *[s.at[0] for s in sems[7:10]]),
-        Swap(2**bits, grads, grads_out, *[s.at[1] for s in sems[7:10]]),
-    ]
+    swap = Swap(2**bits, tokens, tokens_out, *[s.at[0] for s in sems[7:10]])
     greet_all(bits, parts, True)
-    swaps[0].start()
-    count = len(pieces)
-    for now in range(gather.moves()):
-        gather.move(now)
-        if now == count - 1:
-            swaps[1].start()
-    gather.finish()
-    for swap in swaps:
+    swap.start()
+    blocks, rows, width = x_s.shape
+    at = 0
+    for load in loads[:4]:
+        load.wait()
+    for h in range(joined.shape[1] // (HEADW + DV)):
+        for member, size in zip(member_s, (DK, DK, DV, DV)):
+            joined[:, at : at + size] = member[:, h * size : (h + 1) * size]
+            at += size
+
+    def put(i):
+        return pltpu.make_async_copy(padded_s[i], padded[i], out_sem.at[i])
+
+    def widen():
+        for i, (source, target) in enumerate(zip(narrow_s, padded_s)):
+            loads[4 + i].wait()
+            have, wide = source.shape[0], target.shape[1]
+            edge = have // 128 * 128
+            target[:, edge:] = jnp.zeros((target.shape[0], wide - edge), BF16)
+            target[:, 0:have] = source[...].T
+            put(i).start()
+
+    def normalize():
         swap.finish()
-
-
-def prologue(tokens, grads, joined, small, groups, parts):
+        copy = pltpu.make_async_copy(tokens_out, x_s, x_sem.at[0])
+        copy.start()
+        copy.wait()
+
+        @pl.loop(0, blocks)
+        def _(i):
+            x = x_s[i].astype(F32)
+            scale = lax.rsqrt(jnp.mean(x * x, axis=-1, keepdims=True) + 1e-05)
+            h1_out[i] = (x * scale * gain[...]).astype(BF16)
+
+        h1t_out[...] = h1_out[...].reshape(blocks * rows, width).T
+
+    def fetch(p):
+        _, start, _, stop = pieces[p]
+        return pltpu.make_async_copy(
+            joined_out.at[:, :, :, start:stop], w_s.at[p % 2], w_sem.at[p % 2]
+        )
+
+    def store(p):
+        _, start, _, stop = pieces[p]
+        return pltpu.make_async_copy(raw_s.at[p % 2], raw_out.at[:, :, start:stop], raw_sem.at[p % 2])
+
+    main = [p for p, item in enumerate(pieces) if item[0] == 0]
+
+    def project(p):
+        if p - 2 in main:
+            store(p - 2).wait()
+        fetch(p).wait()
+        h1 = h1_out[...].reshape(blocks * rows, width)
+
+        @pl.loop(0, parts)
+        def _(g):
+            raw_s[p % 2, g] = jnp.dot(
+                h1, w_s[p % 2, g].reshape(width, WIDE), preferred_element_type=F32
+            )
+
+        store(p).start()
+
+    ready = {p + STRIDE * gather.ticks: p for p in main}
+    for now in range(max(ready) + 2):
+        if now < gather.moves():
+            gather.move(now)
+        if now == 1:
+            widen()
+        if now == min(ready):
+            normalize()
+        if now - 1 in ready:
+            project(ready[now - 1])
+        if now in ready:
+            gather.s_whole(ready[now]).wait_recv()
+            fetch(ready[now]).start()
+    gather.finish(main)
+    for p in main[-2:]:
+        store(p).wait()
+    for i in range(3):
+        put(i).wait()
+
+
+def prologue(tokens, small, gain, members, narrow, groups, parts):
     bits = groups.bit_length() - 1
-    rows, wide = joined.shape
-    third = wide // 4
+    rows = members[0].shape[0]
+    wide = sum(w.shape[1] for w in members)
+    padded = -(-narrow[0].shape[0] // WIDE) * WIDE
+    blocks, token_rows, width = tokens.shape
     pieces = [(1, 0, small.shape[1], small.shape[1])]
-    pieces += [(0, 0, third, 2 * third), (0, 2 * third, 3 * third, wide)]
-    swapped = jax.ShapeDtypeStruct(tokens.shape, BF16)
+    pieces += [(0, at, at + WIDE // 2, at + WIDE) for at in range(0, wide, WIDE)]
+    length = blocks * token_rows
     any_spec = pl.BlockSpec(memory_space=pl.ANY)
+    vmem_spec = pl.BlockSpec(memory_space=pltpu.VMEM)
+    dma = lambda *shape: pltpu.SemaphoreType.DMA(shape)
     return pl.pallas_call(
         partial(prologue_kernel, bits, parts, pieces),
         out_shape=(
-            swapped,
-            swapped,
+            jax.ShapeDtypeStruct(tokens.shape, BF16),
             jax.ShapeDtypeStruct((parts, groups, rows, wide), BF16),
-            jax.ShapeDtypeStruct((parts, groups, rows, small.shape[1]), BF16),
+            jax.ShapeDtypeStruct((parts, groups) + small.shape, BF16),
+            jax.ShapeDtypeStruct((parts, length, wide), F32),
+            jax.ShapeDtypeStruct(tokens.shape, BF16),
+            jax.ShapeDtypeStruct((width, length), BF16),
+            *[jax.ShapeDtypeStruct((rows, padded), BF16)] * 3,
         ),
-        in_specs=[any_spec] * 4,
-        out_specs=(any_spec,) * 4,
-        scratch_shapes=Gather.scratch(bits, len(pieces)) + [pltpu.SemaphoreType.DMA((2,))] * 3,
-        compiler_params=pltpu.CompilerParams(collective_id=3, has_side_effects=True),
-        cost_estimate=pl.CostEstimate(flops=0, bytes_accessed=40 * 2**20, transcendentals=0),
+        in_specs=[any_spec] * 2 + [vmem_spec] + [any_spec] * 7,
+        out_specs=(any_spec,) * 4 + (vmem_spec,) * 2 + (any_spec,) * 3,
+        scratch_shapes=[
+            *[pltpu.VMEM(w.shape, BF16) for w in (*members, *narrow)],
+            *[pltpu.VMEM((rows, padded), BF16)] * 3,
+            dma(7), dma(3),
+            pltpu.VMEM((rows, wide), BF16),
+            pltpu.VMEM(tokens.shape, BF16),
+            pltpu.VMEM((2, parts, groups, rows, WIDE), BF16),
+            pltpu.VMEM((2, parts, length, WIDE), F32),
+            dma(1), dma(2), dma(2),
+            *Gather.scratch(bits, len(pieces)),
+            dma(1), dma(1), dma(1),
+        ],
+        compiler_params=pltpu.CompilerParams(
+            collective_id=3, has_side_effects=True, vmem_limit_bytes=62 * 2**20
+        ),
+        cost_estimate=pl.CostEstimate(
+            flops=2 * length * width * wide * parts, bytes_accessed=40 * 2**20, transcendentals=0
+        ),
         name="prologue",
-    )(tokens, grads, joined, small)
+    )(tokens, small, gain, *members, *narrow)
 
 
 def forward_kernel(
@@ -326,12 +431,13 @@
     raw_ref, gate_ref, raw_any, convw_ref, ab_ref, gain_ref, *refs,
 ):
     weights = len({item[0] for item in pieces})
-    sources, refs = refs[:weights], refs[weights:]
+    swap_in, sources, refs = refs[0], refs[1 : 1 + weights], refs[1 + weights :]
     head_ref, o_ref, s_ref, t_ref, qe_ref, phi_ref, phil_ref, halo_ref = refs[:8]
-    targets, refs = refs[8 : 8 + weights], refs[8 + weights :]
+    swap_out, targets, refs = refs[8], refs[9 : 9 + weights], refs[9 + weights :]
     (qe_s, o0_s, phi_s, b_s, phil_s, bl_s, send_s, recv_s, halo_s, ext_s,
      send_sem, recv_sem, halo_send_sem, halo_recv_sem) = refs[:14]
-    gather = Gather(bits, parts, sources, targets, pieces, refs[14:])
+    swap = Swap(2**bits, swap_in, swap_out, *[s.at[0] for s in refs[14:17]])
+    gather = Gather(bits, parts, sources, targets, pieces, refs[17:])
     step = pl.program_id(0)
     early = pl.program_id(1) == 0
     z = lax.axis_index("mp")
@@ -344,7 +450,8 @@
 
     @pl.when((step == 0) & early)
     def _():
-        greet_all(bits, parts, False)
+        greet_all(bits, parts, True)
+        swap.start()
 
     last = 2 * (heads + lag) - 1
     for now in range(min(gather.moves(), last)):
@@ -489,12 +596,14 @@
     def _():
         halo_ref[...] = halo_s[...]
         gather.finish()
+        swap.finish()
 
 
 class Scatter:
-    def __init__(self, bits, parts, plan, rows, lhs_ref, rhs_refs, out_ref, scratch):
+    def __init__(self, bits, parts, plan, rows, lhs_refs, rhs_refs, out_ref, scratch, stride):
+        self.stride = stride
         self.bits, self.parts, self.plan, self.rows = bits, parts, plan, rows
-        self.lhs_ref, self.rhs_refs, self.out_ref = lhs_ref, rhs_refs, out_ref
+        self.lhs_refs, self.rhs_refs, self.out_ref = lhs_refs, rhs_refs, out_ref
         self.count = len(plan)
         self.planes = planes = bits - 1
         self.half = 2 ** (bits - 1)
@@ -503,7 +612,7 @@
         (self.r4, self.load_sem, self.send1, self.recv1, self.send_a, self.recv_a, self.send_b,
          self.recv_b, self.send4, self.recv4) = rest[2 * planes :]
         self.d, self.z = lax.axis_index("dp"), lax.axis_index("mp")
-        self.ticks = self.count + STRIDE * (planes + 2)
+        self.ticks = self.count + 1 + self.stride * (planes + 1)
 
     @staticmethod
     def scratch(bits, parts, count, rows, length, width):
@@ -550,7 +659,7 @@
                     self.load_sem.at[0, slot],
                 ).start()
                 pltpu.make_async_copy(
-                    self.lhs_ref.at[self.plan[at[0]][1]], self.lhs_s.at[slot], self.load_sem.at[1, slot]
+                    self.lhs_refs[self.plan[at[0]][1]], self.lhs_s.at[slot], self.load_sem.at[1, slot]
                 ).start()
 
     def load_wait(self, t):
@@ -559,7 +668,7 @@
             self.rhs_refs[0].at[:, :, pl.ds(0, WIDE)], self.rhs_s.at[slot], self.load_sem.at[0, slot]
         ).wait()
         pltpu.make_async_copy(
-            self.lhs_ref.at[0], self.lhs_s.at[slot], self.load_sem.at[1, slot]
+            self.lhs_refs[0], self.lhs_s.at[slot], self.load_sem.at[1, slot]
         ).wait()
 
     def first_hop(self, t):
@@ -626,7 +735,7 @@
         def _():
             self.load(tick)
 
-        t = tick - STRIDE * (planes + 2)
+        t = tick - 1 - self.stride * (planes + 1)
 
         @pl.when((t >= 0) & (t < count))
         def _():
@@ -640,7 +749,7 @@
             self.out_ref[t, :, side:] = right
 
         for k in range(planes - 1, -1, -1):
-            t_k = tick - STRIDE * (k + 2)
+            t_k = tick - 1 - self.stride * (k + 1)
 
             @pl.when((t_k >= 0) & (t_k < count))
             def _():
@@ -667,7 +776,7 @@
                     for copy in self.z_hops(t_k):
                         copy.start()
 
-        t_1 = tick - STRIDE
+        t_1 = tick - 1
 
         @pl.when((t_1 >= 0) & (t_1 < count))
         def _():
@@ -726,24 +835,31 @@
     return plan
 
 
+def small_rows(heads, width, smalls):
+    starts = [0]
+    for count in (width // 128, width // 128, DV // 128, heads * TAPS * HEADW // 128, 1, smalls * width // 128):
+        starts.append(starts[-1] + count)
+    return starts, -(-starts[-1] // 8) * 8
+
+
 def scatter_kernel(bits, parts, plan, rows, lhs_ref, *refs):
     sources = len({item[0] for item in plan})
     rhs_refs, refs = refs[:sources], refs[sources:]
-    vec_ref, y_ref, g_ref, out_ref, vec_out, y_out, g_out = refs[:7]
-    v_acc, v_in, v_z, v_send, v_recv, v_z_send, v_z_recv = refs[7:14]
-    swap_own, swap_send, swap_recv = refs[14:17]
-    scatter = Scatter(bits, parts, plan, rows, lhs_ref, rhs_refs, out_ref, refs[17:])
+    (ffn_ref, hgain_ref, conv_ref, line_ref, w_ref, d_small, w_small, x_ref, dx1_ref, gain_ref, out_ref, vec_out,
+     g_out) = refs[:13]
+    refs = refs[3:]
+    v_own, v_acc, v_in, v_z, v_send, v_recv, v_z_send, v_z_recv = refs[10:18]
+    swap_own, swap_send, swap_recv = refs[18:21]
+    dp_s, w_s, acc_s, dx_s, in_sem = refs[21:26]
+    scatter = Scatter(bits, parts, plan, rows, [lhs_ref], rhs_refs, out_ref, refs[26:], STRIDE)
     z = lax.axis_index("mp")
     mesh_id = pl.DeviceIdType.MESH
     greet_all(bits, parts, True)
-    swaps = [
-        Swap(2**bits, src, dst, swap_own.at[i], swap_send.at[i], swap_recv.at[i])
-        for i, (src, dst) in enumerate(((y_ref, y_out), (g_ref, g_out)))
-    ]
+    swap = Swap(2**bits, dx_s, g_out, swap_own.at[0], swap_send.at[0], swap_recv.at[0])
 
     def v_hop(b):
         return pltpu.make_async_remote_copy(
-            src_ref=vec_ref if b == 0 else v_acc.at[b - 1], dst_ref=v_in.at[b], send_sem=v_send.at[b],
+            src_ref=v_own if b == 0 else v_acc.at[b - 1], dst_ref=v_in.at[b], send_sem=v_send.at[b],
             recv_sem=v_recv.at[b], device_id={"dp": scatter.partner(b)}, device_id_type=mesh_id,
         )
 
@@ -759,7 +875,7 @@
         elif stage <= bits:
             b = stage - 1
             v_hop(b).wait_recv()
-            total = (vec_ref[...] if b == 0 else v_acc[b - 1]) + v_in[b]
+            total = (v_own[...] if b == 0 else v_acc[b - 1]) + v_in[b]
             if stage < bits:
                 v_acc[b] = total
                 v_hop(stage).start()
@@ -777,25 +893,100 @@
             for b in range(bits):
                 v_hop(b).wait_send()
             v_z_hop(whole, whole, 1).wait_send()
-    for swap in swaps:
-        swap.start()
-
-    @pl.loop(0, scatter.ticks)
-    def _(tick):
+
+    def fetch(g, slot):
+        return (
+            pltpu.make_async_copy(rhs_refs[0].at[g], dp_s.at[slot], in_sem.at[0, slot]),
+            pltpu.make_async_copy(w_ref.at[g], w_s.at[slot], in_sem.at[1, slot]),
+        )
+
+    def input_grad():
+        acc_s[...] += lax.dot_general(
+            d_small[...], w_small[...], (((0,), (0,)), ((), ())), preferred_element_type=F32
+        )
+        blocks, token_rows, width = x_ref.shape
+
+        def body(i, gain_sum):
+            x = x_ref[i].astype(F32)
+            scale = lax.rsqrt(jnp.mean(x * x, axis=-1, keepdims=True) + 1e-05)
+            unit = x * scale
+            at = pl.ds(pl.multiple_of(i * token_rows, token_rows), token_rows)
+            d_h1 = acc_s[at]
+            e = d_h1 * gain_ref[...]
+            d_x = dx1_ref[at] + scale * (e - unit * jnp.mean(e * unit, axis=-1, keepdims=True))
+            dx_s[i] = d_x.astype(BF16)
+            return gain_sum + jnp.sum(d_h1 * unit, axis=0, keepdims=True)
+
+        gain_sum = lax.fori_loop(0, blocks, body, jnp.zeros((1, width), F32))
+        starts, _ = small_rows(conv_ref.shape[0], width, d_small.shape[0])
+
+        def put(start, row):
+            for i in range(row.shape[1] // 128):
+                v_own[start + i : start + i + 1] = row[:, i * 128 : (i + 1) * 128]
+
+        put(starts[0], gain_sum)
+        put(starts[1], ffn_ref[...])
+        put(starts[2], hgain_ref[...])
+        for h in range(conv_ref.shape[0]):
+            for tap in range(TAPS):
+                put(starts[3] + (h * TAPS + tap) * HEADW // 128, conv_ref[h, tap : tap + 1])
+        put(starts[4], line_ref[...])
+        small_grad = lax.dot_general(
+            d_small[...], scatter.lhs_s[0], (((1,), (1,)), ((), ())), preferred_element_type=F32
+        )
+        for i in range(d_small.shape[0]):
+            put(starts[5] + i * width // 128, small_grad[i : i + 1])
+        if starts[6] < v_own.shape[0]:
+            v_own[starts[6] :] = jnp.zeros((v_own.shape[0] - starts[6], 128), F32)
+
+    for copy in fetch(0, 0):
+        copy.start()
+
+    @pl.loop(0, max(scatter.ticks, 2 + parts + bits + 2))
+    def _(now):
+        scatter.tick(now)
+        tick = now - 2
+
+        @pl.when((tick >= 0) & (tick < parts))
+        def _():
+            slot = lax.rem(tick, 2)
+
+            @pl.when(tick + 1 < parts)
+            def _():
+                for copy in fetch(tick + 1, 1 - slot):
+                    copy.start()
+
+            for copy in fetch(tick, slot):
+                copy.wait()
+            part = lax.dot_general(
+                dp_s[slot], w_s[slot], (((1,), (1,)), ((), ())), preferred_element_type=F32
+            )
+
+            @pl.when(tick == 0)
+            def _():
+                acc_s[...] = part
+
+            @pl.when(tick > 0)
+            def _():
+                acc_s[...] += part
+
+        @pl.when(tick == parts)
+        def _():
+            input_grad()
+            swap.start()
+
         for stage in range(bits + 2):
-            @pl.when(tick == stage)
+            @pl.when(tick == parts + stage)
             def _():
                 small_sum(stage)
 
-        scatter.tick(tick)
-
-    for swap in swaps:
-        swap.finish()
+    swap.finish()
     scatter.finish()
 
 
-def scatter_sum(lefts, pairs, vector, block_out, d_x, groups, parts, collective):
-    kinds, width, length = lefts.shape
+def scatter_sum(left, pairs, smalls, weight, d_small, w_small, x, d_x1, gain, groups, parts, collective):
+    width, length = left.shape
+    vector = jax.ShapeDtypeStruct((small_rows(smalls[2].shape[0], width, d_small.shape[0])[1], 128), F32)
     bits = groups.bit_length() - 1
     rows = width // groups
     plan = plan_of(pairs)
@@ -808,41 +999,49 @@
         out_shape=(
             jax.ShapeDtypeStruct((count, rows, WIDE), F32),
             jax.ShapeDtypeStruct(vector.shape, F32),
-            jax.ShapeDtypeStruct(block_out.shape, BF16),
-            jax.ShapeDtypeStruct(d_x.shape, BF16),
+            jax.ShapeDtypeStruct(x.shape, BF16),
         ),
-        in_specs=[any_spec] * (1 + len(pairs)) + [vmem_spec, any_spec, any_spec],
-        out_specs=(vmem_spec, vmem_spec, any_spec, any_spec),
+        in_specs=[any_spec] * (1 + len(pairs)) + [vmem_spec] * 4 + [any_spec] + [vmem_spec] * 5,
+        out_specs=(vmem_spec, vmem_spec, any_spec),
         scratch_shapes=[
+            pltpu.VMEM(vector.shape, F32),
             pltpu.VMEM((bits - 1,) + vector.shape, F32),
             pltpu.VMEM((bits,) + vector.shape, F32),
             pltpu.VMEM((parts,) + vector.shape, F32),
             dma(bits), dma(bits), dma(1), dma(1),
-            dma(2), dma(2), dma(2),
+            dma(1), dma(1), dma(1),
+            pltpu.VMEM((2,) + pairs[0][1].shape[1:], BF16),
+            pltpu.VMEM((2,) + weight.shape[1:], BF16),
+            pltpu.VMEM((length, width), F32),
+            pltpu.VMEM(x.shape, BF16),
+            dma(2, 2),
             *Scatter.scratch(bits, parts, count, rows, length, width),
         ],
         compiler_params=pltpu.CompilerParams(
             collective_id=collective, has_side_effects=True, vmem_limit_bytes=60 * 2**20
         ),
         cost_estimate=pl.CostEstimate(
-            flops=2 * count * WIDE * parts * length * width, bytes_accessed=count * parts * length * WIDE * 2,
+            flops=4 * count * WIDE * parts * length * width, bytes_accessed=count * parts * length * WIDE * 4,
             transcendentals=0,
         ),
         name="scatter_sum",
-    )(lefts, *[right for _, right in pairs], vector, block_out, d_x)
+    )(left, *[right for _, right in pairs], *smalls, weight, d_small, w_small, x, d_x1, gain)
 
 
 def backward_kernel(
     heads, parts, bits, plan, rows_held,
     dhead_ref, o_ref, gate_ref, qe_ref, phi_ref, phil_ref,
-    raw_ref, halo_ref, convw_ref, ab_ref, gain_ref, s_ref, t_ref, phi_late_ref, lhs_ref, *refs,
+    raw_ref, halo_ref, convw_ref, ab_ref, gain_ref, s_ref, t_ref, phi_late_ref, *refs,
 ):
     sources = len({item[0] for item in plan})
-    rhs_refs, refs = refs[:sources], refs[sources:]
-    dproj_ref, dab_ref, dconv_ref, dgain_ref, sums_ref = refs[:5]
+    kinds = len({item[1] for item in plan})
+    lhs_refs, refs = refs[:kinds], refs[kinds:]
+    rhs_refs, swap_in, refs = refs[:sources], refs[sources], refs[sources + 1 :]
+    dproj_ref, dab_ref, dconv_ref, dgain_ref, sums_ref, swap_out = refs[:6]
     (do_s, d_s, dgate_s, dl_s, phil_s, g_s, dext_s, ext_s, send_s, recv_s, halo_send, halo_recv,
-     send_sem, recv_sem, halo_send_sem, halo_recv_sem) = refs[5:21]
-    scatter = Scatter(bits, parts, plan, rows_held, lhs_ref, rhs_refs, sums_ref, refs[21:])
+     send_sem, recv_sem, halo_send_sem, halo_recv_sem) = refs[6:22]
+    scatter = Scatter(bits, parts, plan, rows_held, lhs_refs, rhs_refs, sums_ref, refs[25:], 3)
+    swap = Swap(2**bits, swap_in, swap_out, *[s.at[0] for s in refs[22:25]])
     step = pl.program_id(0)
     early = pl.program_id(1) == 0
     z = lax.axis_index("mp")
@@ -855,11 +1054,14 @@
 
     @pl.when((step == 0) & early)
     def _():
-        greet_all(bits, parts, False)
-
-    now = step * 2 + pl.program_id(1)
-    last = 2 * (heads + lag + 1) - 1
+        greet_all(bits, parts, True)
+        swap.start()
+
+    sub = pl.program_id(1)
+    now = jnp.where(step < lag, step, lag + 2 * (step - lag) + sub)
+    last = lag + 2 * (heads + 1) - 1
     stop = jnp.where(now == last, max(scatter.ticks, last + 1), now + 1)
+    stop = jnp.where((step < lag) & early, now, stop)
 
     @pl.loop(now, stop)
     def _(tick):
@@ -1061,6 +1263,7 @@
     @pl.when((step == pl.num_programs(0) - 1) & ~early)
     def _():
         scatter.finish()
+        swap.finish()
 
     @pl.when((step == pl.num_programs(0) - 1) & ~early & (z > 0))
     def _():
@@ -1070,7 +1273,57 @@
             halo_hop(h).wait_send()
 
 
-def forward_core(raw, convw, ab, gain, weights, heads, parts, groups):
+def assemble_kernel(
+    per, base, ffn_ref, proj_ref, vec_ref, y_ref, g_ref,
+    query_ref, key_ref, value_ref, outgate_ref, out_ref, gate_ref, up_ref, down_ref, conv_ref, y_out, g_out,
+):
+    y_out[...] = y_ref[...]
+    g_out[...] = g_ref[...]
+    for h in range(per):
+        query_ref[:, h * DK : (h + 1) * DK] = proj_ref[3 * h, :, 0:DK]
+        key_ref[:, h * DK : (h + 1) * DK] = proj_ref[3 * h, :, DK:]
+        value_ref[:, h * DV : (h + 1) * DV] = proj_ref[3 * h + 1]
+        outgate_ref[:, h * DV : (h + 1) * DV] = proj_ref[3 * h + 2]
+    piece = 0
+    for target in (down_ref, gate_ref, up_ref):
+        total = target.shape[0]
+        for start in range(0, total, WIDE):
+            size = min(WIDE, total - start)
+            target[start : start + size] = ffn_ref[piece].T[0:size]
+            piece += 1
+    for start in range(0, out_ref.shape[1], WIDE):
+        out_ref[:, start : start + WIDE] = ffn_ref[piece]
+        piece += 1
+    width = conv_ref.shape[1]
+    heads = width // HEADW
+    for h in range(heads):
+        for tap in range(TAPS):
+            row = base + (h * TAPS + tap) * HEADW // 128
+            spots = [h * DK, (heads + h) * DK, 2 * heads * DK + h * DV, 2 * heads * DK + h * DV + 128]
+            for i, spot in enumerate(spots):
+                conv_ref[tap : tap + 1, spot : spot + 128] = vec_ref[row + i : row + i + 1]
+
+
+def assemble(ffn, proj, vec, y, g, per, hidden, base, conv_shape):
+    rows = ffn.shape[1]
+    f32 = lambda *shape: jax.ShapeDtypeStruct(shape, F32)
+    vmem_spec = pl.BlockSpec(memory_space=pltpu.VMEM)
+    return pl.pallas_call(
+        partial(assemble_kernel, per, base),
+        out_shape=(
+            f32(rows, per * DK), f32(rows, per * DK), f32(rows, per * DV), f32(rows, per * DV), f32(rows, per * DV),
+            f32(hidden, rows), f32(hidden, rows), f32(hidden, rows), f32(*conv_shape),
+            jax.ShapeDtypeStruct(y.shape, BF16), jax.ShapeDtypeStruct(g.shape, BF16),
+        ),
+        in_specs=[vmem_spec] * 5,
+        out_specs=(vmem_spec,) * 11,
+        compiler_params=pltpu.CompilerParams(vmem_limit_bytes=40 * 2**20),
+        cost_estimate=pl.CostEstimate(flops=0, bytes_accessed=10 * 2**20, transcendentals=0),
+        name="assemble",
+    )(ffn, proj, vec, y, g)
+
+
+def forward_core(raw, convw, ab, gain, swapped, weights, heads, parts, groups):
     bits = groups.bit_length() - 1
     pieces = []
     for w, weight in enumerate(weights):
@@ -1098,6 +1351,7 @@
             jax.ShapeDtypeStruct((heads, chunks, DK, DK), F32),
             jax.ShapeDtypeStruct((heads, DK, DK), F32),
             jax.ShapeDtypeStruct((parts, HALO, per * (HEADW + DV)), F32),
+            jax.ShapeDtypeStruct(swapped.shape, BF16),
             *[jax.ShapeDtypeStruct((parts, groups) + w.shape, BF16) for w in weights],
         ),
         in_specs=[
@@ -1107,7 +1361,7 @@
             pl.BlockSpec((1, TAPS, HEADW), lambda s, _: (now(s), 0, 0)),
             pl.BlockSpec((1, 8, length), lambda s, _: (now(s), 0, 0)),
             pl.BlockSpec((1, DV), lambda s, _: (0, 0)),
-            *[any_spec] * len(weights),
+            *[any_spec] * (1 + len(weights)),
         ],
         out_specs=(
             pl.BlockSpec((1, length, DV), lambda s, _: (late(s) // per, 0, late(s) % per)),
@@ -1118,7 +1372,7 @@
             pl.BlockSpec((1, chunks, DK, DK), lambda s, _: (now(s), 0, 0, 0)),
             pl.BlockSpec((1, DK, DK), lambda s, _: (now(s), 0, 0)),
             pl.BlockSpec((parts, HALO, per * (HEADW + DV)), lambda s, _: (0, 0, 0)),
-            *[any_spec] * len(weights),
+            *[any_spec] * (1 + len(weights)),
         ),
         scratch_shapes=[
             pltpu.VMEM((slots, length, DK), F32),
@@ -1135,6 +1389,7 @@
             pltpu.SemaphoreType.DMA((heads,)),
             pltpu.SemaphoreType.DMA((parts,)),
             pltpu.SemaphoreType.DMA((parts,)),
+            *[pltpu.SemaphoreType.DMA((1,))] * 3,
             *Gather.scratch(bits, len(pieces)),
         ],
         compiler_params=pltpu.CompilerParams(
@@ -1142,10 +1397,10 @@
         ),
         cost_estimate=pl.CostEstimate(flops=20 * 10**9, bytes_accessed=40 * 2**20, transcendentals=0),
         name="delta_forward",
-    )(raw, raw, raw, convw, ab, gain, *weights)
-
-
-def backward_core(d_head, out, raw, halo, query_e, phi, phi_all, convw, ab, gain, states, inverses, lefts, pairs,
+    )(raw, raw, raw, convw, ab, gain, swapped, *weights)
+
+
+def backward_core(d_head, out, raw, halo, query_e, phi, phi_all, convw, ab, gain, states, inverses, lefts, pairs, swapped,
                   heads, parts, groups):
     length = raw.shape[1]
     size = min(CHUNK, length)
@@ -1155,7 +1410,7 @@
     slots = lag + 1
     bits = groups.bit_length() - 1
     plan = plan_of(pairs)
-    rows = lefts.shape[1] // groups
+    rows = lefts[0].shape[0] // groups
     any_spec = pl.BlockSpec(memory_space=pl.ANY)
     now = lambda s: jnp.minimum(s, heads - 1)
     late = lambda s: jnp.clip(s - lag, 0, heads - 1)
@@ -1169,6 +1424,7 @@
             jax.ShapeDtypeStruct((heads, TAPS, HEADW), F32),
             jax.ShapeDtypeStruct((1, DV), F32),
             jax.ShapeDtypeStruct((len(plan), rows, WIDE), F32),
+            jax.ShapeDtypeStruct(swapped.shape, BF16),
         ),
         in_specs=[
             pl.BlockSpec((1, length, DV), lambda s, _: (now(s) // per, 0, now(s) % per)),
@@ -1185,7 +1441,7 @@
             pl.BlockSpec((1, chunks, DK, DV), lambda s, _: (late(s), 0, 0, 0)),
             pl.BlockSpec((1, chunks, size, size), lambda s, _: (late(s), 0, 0, 0)),
             pl.BlockSpec((1, chunks, DK, DK), lambda s, _: (late(s), 0, 0, 0)),
-            *[any_spec] * (1 + len(pairs)),
+            *[any_spec] * (1 + len(lefts) + len(pairs)),
         ],
         out_specs=(
             pl.BlockSpec((1, length, HEADW + DV), lambda s, _: (later(s) // per, 0, later(s) % per)),
@@ -1193,6 +1449,7 @@
             pl.BlockSpec((1, TAPS, HEADW), lambda s, _: (late(s), 0, 0)),
             pl.BlockSpec((1, DV), lambda s, _: (0, 0)),
             pl.BlockSpec((len(plan), rows, WIDE), lambda s, _: (0, 0, 0)),
+            any_spec,
         ),
         scratch_shapes=[
             pltpu.VMEM((slots, length, DV), F32),
@@ -1211,7 +1468,8 @@
             pltpu.SemaphoreType.DMA((heads,)),
             pltpu.SemaphoreType.DMA((heads,)),
             pltpu.SemaphoreType.DMA((heads,)),
-            *Scatter.scratch(bits, parts, len(plan), rows, length, lefts.shape[1]),
+            *[pltpu.SemaphoreType.DMA((1,))] * 3,
+            *Scatter.scratch(bits, parts, len(plan), rows, length, lefts[0].shape[0]),
         ],
         compiler_params=pltpu.CompilerParams(
             collective_id=1, has_side_effects=True, vmem_limit_bytes=62 * 2**20
@@ -1219,7 +1477,7 @@
         cost_estimate=pl.CostEstimate(flops=40 * 10**9, bytes_accessed=60 * 2**20, transcendentals=0),
         name="delta_backward",
     )(d_head, out, raw, query_e, phi, phi_all, raw, halo, convw, ab, gain, states, inverses, phi,
-      lefts, *[right for _, right in pairs])
+      *lefts, *[right for _, right in pairs], swapped)
 
 
 def dot(spec, a, b):
@@ -1243,27 +1501,20 @@
     width = tokens.shape[2]
     local_rows = w_query.shape[0]
 
-    def by_head(w, size):
-        return w.reshape(local_rows, per, size)
-
-    joined = jnp.concatenate(
-        [by_head(w_query, DK), by_head(w_key, DK), by_head(w_value, DV), by_head(w_outgate, DV)], axis=2
-    ).reshape(local_rows, per * (HEADW + DV))
-    main_cols = joined.shape[1]
-
     hidden = w_ffn_gate.shape[1]
     wide = -(-hidden // WIDE) * WIDE
-    small_w = jnp.concatenate([w_decay, w_beta], axis=1)
-    lanes = -(-small_w.shape[1] // 128) * 128
-    widen = lambda w, size: jnp.pad(w, ((0, 0), (0, size - w.shape[1])))
-    x_bf, dy_bf, g_proj, g_small = prologue(
-        tokens, out_grad, joined, widen(small_w, lanes), groups, parts
+    small_w = jnp.concatenate([w_decay, w_beta], axis=1).T
+    small_w = jnp.pad(small_w, ((0, -small_w.shape[0] % 16), (0, 0)))
+    x_bf, g_proj, g_small, raw, h1, h1_t, *padded = prologue(
+        tokens, small_w, mix_gain[None], (w_query, w_key, w_value, w_outgate),
+        (w_ffn_gate.T, w_ffn_up.T, w_ffn_down.T), groups, parts,
     )
+    h1 = h1.reshape(-1, width)
     whole = lambda g: g.reshape(parts, width, g.shape[3])
     g_proj = whole(g_proj)
-    g_small = whole(g_small)
+    g_small = g_small[:, :, : 2 * per].transpose(0, 2, 1, 3).reshape(parts, 2 * per, width)
+    x_swapped = x_bf
     x_bf = x_bf.reshape(-1, width)
-    dy_bf = dy_bf.reshape(-1, width)
     length = x_bf.shape[0]
 
     my_length = lax.dynamic_slice_in_dim(seq_lengths, group, 1)
@@ -1271,13 +1522,7 @@
     live = (positions < my_length).astype(F32)[:, None]
 
     x = x_bf.astype(F32)
-    dy = live * dy_bf.astype(F32)
-    d_ffo = dy.astype(BF16)
-    scale1 = unit_rms(x)
-    n1 = x * scale1
-    h1 = (n1 * mix_gain).astype(BF16)
-    raw = dot("td,gdc->gtc", h1, g_proj)
-    small = dot("td,gdc->gct", h1, g_small)[:, : 2 * per]
+    small = dot("td,gcd->gct", h1, g_small)
     decay_raw = small[:, :per].reshape(heads, length)
     beta_raw = small[:, per:].reshape(heads, length)
     rate = -jnp.exp(rate_log)[:, None]
@@ -1298,13 +1543,15 @@
         axis=2,
     ).transpose(1, 0, 2)
     gain_row = head_gain[None]
-    head_out, mixed, states, inverses, query_e, phi, phi_all, halo, *rest = forward_core(
-        raw, convw, ab, gain_row,
-        [w_out] + [widen(w, wide) for w in (w_ffn_gate, w_ffn_up, w_ffn_down)],
+    head_out, mixed, states, inverses, query_e, phi, phi_all, halo, dy_bf, *rest = forward_core(
+        raw, convw, ab, gain_row, out_grad,
+        [w_out] + padded,
         heads, parts, groups,
     )
     g_out, g_gate, g_up, g_down = [whole(w) for w in rest]
 
+    dy = live * dy_bf.reshape(-1, width).astype(F32)
+    d_ffo = dy.astype(BF16)
     x1 = x + dot("gtc,gmc->tm", head_out, g_out)
     scale2 = unit_rms(x1)
     n2 = x1 * scale2
@@ -1324,10 +1571,10 @@
     d_mix = d_x1.astype(BF16)
     d_head = dot("tm,gmc->gtc", d_mix, g_out)
 
-    d_proj, d_ab, d_convw, d_head_gain, sums_ffn = backward_core(
+    d_proj, d_ab, d_convw, d_head_gain, sums_ffn, final_out = backward_core(
         d_head, mixed, raw, halo, query_e, phi, phi_all, convw, ab, gain_row, states, inverses,
-        jnp.stack([d_mix.T, h2.T, d_ffo.T]), [(2, act), (1, d_gate), (1, d_up), (0, head_out)],
-        heads, parts, groups,
+        [d_mix.T, h2.T, d_ffo.T], [(2, act), (1, d_gate), (1, d_up), (0, head_out)],
+        block_out.reshape(tokens.shape), heads, parts, groups,
     )
     d_decay = d_ab[:, 0]
     d_beta_raw = d_ab[:, 1] * beta * (1.0 - beta)
@@ -1337,74 +1584,39 @@
     d_small = jnp.concatenate(
         [d_decay_raw.reshape(parts, per, length), d_beta_raw.reshape(parts, per, length)], axis=1
     ).astype(BF16)
-    small_grad = dot("gct,td->gcd", d_small, h1)
-    d_h1 = dot("gtc,gdc->td", d_proj, g_proj) + dot("gct,gdc->td", d_small, g_small[:, :, : 2 * per])
-    e1 = d_h1 * mix_gain
-    d_x = d_x1 + scale1 * (e1 - n1 * jnp.mean(e1 * n1, axis=-1, keepdims=True))
-    mix_gain_grad = jnp.sum(d_h1 * n1, axis=0)
-    per_head = d_convw.transpose(1, 0, 2)
-    d_conv = jnp.concatenate(
-        [
-            per_head[:, :, :DK].reshape(taps, key_cols),
-            per_head[:, :, DK : 2 * DK].reshape(taps, key_cols),
-            per_head[:, :, 2 * DK :].reshape(taps, heads * DV),
-        ],
-        axis=1,
+    line = jnp.pad(jnp.concatenate([rate_grad, bias_grad])[None], ((0, 0), (0, 128 - 2 * heads)))
+    sums_proj, sums, final_grad = scatter_sum(
+        h1_t, [(0, d_proj)],
+        (ffn_gain_grad[None], d_head_gain, d_convw, line), g_proj, d_small.reshape(-1, length),
+        g_small.reshape(-1, width), x_swapped, d_x1, mix_gain[None], groups, parts, 2,
     )
-    vector = jnp.concatenate(
-        [mix_gain_grad, ffn_gain_grad, d_head_gain[0], d_conv.reshape(-1), rate_grad, bias_grad,
-         small_grad.reshape(-1)]
+    starts, _ = small_rows(heads, width, 2 * heads)
+    part = lambda i: sums[starts[i] : starts[i + 1]].reshape(-1)
+    (s_query, s_key, s_value, s_outgate, s_out, s_gate, s_up, s_down, s_conv, final_out, final_grad) = assemble(
+        sums_ffn, sums_proj, sums, final_out, final_grad, per, hidden, starts[3], conv_weight.shape
     )
-    used = vector.shape[0]
-    vector = jnp.pad(vector, (0, -used % 1024)).reshape(-1, 128)
-    sums_proj, sums, final_out, final_grad = scatter_sum(
-        h1.T[None], [(0, d_proj)],
-        vector, block_out.reshape(tokens.shape), d_x.astype(BF16).reshape(tokens.shape),
-        groups, parts, 2,
-    )
-    sums = sums.reshape(-1)
-
-    sums_w = jnp.concatenate([sums_ffn, sums_proj], axis=0)
-
-    def columns(start, size):
-        pieces = -(-size // WIDE)
-        return sums_w[start : start + pieces].transpose(1, 0, 2).reshape(local_rows, -1)[:, :size]
-
-    step = wide // WIDE
-    s_down = columns(0, hidden)
-    s_gate = columns(step, hidden)
-    s_up = columns(2 * step, hidden)
-    s_out = columns(3 * step, per * DV)
-    s_proj = columns(3 * step + per * DV // WIDE, main_cols)
-    pieces = []
-    start = 0
-    for count in (width, width, DV, taps * conv_weight.shape[1], heads, heads):
-        pieces.append(sums[start : start + count])
-        start += count
-    small_sum = sums[start:used].reshape(parts, 2 * per, width)
+    small_sum = part(5).reshape(parts, 2 * per, width)
     mine = lax.dynamic_slice(small_sum, (share, 0, group * local_rows), (1, 2 * per, local_rows))[0].T
 
-    by = s_proj.reshape(local_rows, per, HEADW + DV)
-    flat = lambda v: v.reshape(local_rows, -1)
     return (
         final_out,
         final_grad,
-        pieces[0],
-        flat(by[:, :, :DK]),
-        flat(by[:, :, DK : 2 * DK]),
-        flat(by[:, :, 2 * DK : HEADW]),
-        flat(by[:, :, HEADW:]),
+        part(0),
+        s_query,
+        s_key,
+        s_value,
+        s_outgate,
         mine[:, :per],
         mine[:, per:],
-        pieces[3].reshape(conv_weight.shape),
-        pieces[4],
-        pieces[5],
-        pieces[2],
+        s_conv,
+        part(4)[:heads],
+        part(4)[heads : 2 * heads],
+        part(2),
         s_out,
-        pieces[1],
-        s_gate,
-        s_up,
-        s_down,
+        part(1),
+        s_gate.T,
+        s_up.T,
+        s_down.T,
     )
 
 

time: 614 us -> 550 us (0.90)
  matrix products: 81.7 us -> 60.8 us
  local copies, waits for them, and re-layouts: 36.2 us -> 17.9 us
  Pallas kernels: 474 us -> 457 us
  other arithmetic: 16.8 us -> 7.53 us
    dot_general x13 -> x9, matrix products: 81.7 us -> 60.8 us  [dot(): return jnp.einsum(spec, a, b, preferred_element_type=F32)]
    pallas_call x1, Pallas kernels: 156 us -> 140 us  [backward_core(): pl.pallas_call(partial(backward_kernel, heads, parts, bits, plan, rows),...]
    pallas_call x1, Pallas kernels: 134 us -> 124 us  [forward_core(): pl.pallas_call(partial(forward_kernel, heads, parts, bits, pieces), grid=...]
    pallas_call x1, Pallas kernels: 93.9 us -> 102 us  [scatter_sum(): pl.pallas_call(partial(scatter_kernel, bits, parts, plan, rows), out_shap...]
    another operation x5 -> x1, other arithmetic: 7.06 us -> 0.1 us  [the longest x3 6.1 us: per_device(): jnp.stack([d_mix.T, h2.T, d_ffo.T])]
    unnamed x111 -> x51, local copies, waits for them, and re-layouts: 11.7 us -> 4.84 us
where the time goes in v3:
time: 550 us; the launch traced here: 545 us
  Pallas kernels  457 us (83%)
  matrix products  60.8 us (11%)
  local copies, waits for them, and re-layouts  17.9 us (3%)
  other arithmetic  7.53 us (1%)
    pallas_call x1, Pallas kernels, backward_core(): pl.pallas_call(partial(backward_kernel, heads, parts, bits, plan, rows),...  140 us
    pallas_call x1, Pallas kernels, forward_core(): pl.pallas_call(partial(forward_kernel, heads, parts, bits, pieces), grid=...  124 us
    pallas_call x1, Pallas kernels, scatter_sum(): pl.pallas_call(partial(scatter_kernel, bits, parts, plan, rows), out_shap...  102 us
    pallas_call x1, Pallas kernels, prologue(): pl.pallas_call(partial(prologue_kernel, bits, parts, pieces), out_shape=(...  89.3 us
    dot_general x9, matrix products, dot(): return jnp.einsum(spec, a, b, preferred_element_type=F32)  60.8 us

profile of v3, /device:TPU:0, one launch (start us, length us, event | category | flops | bytes accessed | tf_op | source)
XLA Modules:
  0.0 544.7 jit_solution(3488461545179646845)
XLA Ops:
  1.9 89.3 %prologue.1 = (bf16[8,64,1024]{2,1,0:T(8,128)(2,1)}, bf16[4,8,128,1536]{3,2,1,0:T(8,128)(2,1)}, bf16[4,8,16,128]{3,2,1,0:T(8,128)(2,1)}, f32[4,512,1536]{2,1,0:T...) custom-call(bf16[8,64,1024]{2,1,0:T(8,128)(2,1)} %refs_0_.2, ...), custom_call_target="tpu_custom_call" | custom-call | flops 6442450944 | bytes 41943040 | tf_op jit(solution)/shard_map/prologue/pallas_call | solution.py:394
  91.3 1.7 fusion.20
  94.7 123.9 %delta_forward.1 = (bf16[4,512,512]{2,1,0:T(8,128)(2,1)}, f32[8,512,256]{2,1,0:T(8,128)}, f32[8,4,128,256]{3,2,1,0:T(8,128)}, f32[8,4,128,128]{3,2,1,0:T(8,128)}...) custom-call(f32[4,512,1536]{2,1,0:T(8,128)} %get-tuple-element.60.ra, ...), custom_call_target="tpu_custom_call" | custom-call | flops 20000000000 | bytes 41943040 | tf_op jit(solution)/shard_map/delta_forward/pallas_call | solution.py:1342
  219.9 1.6 multiply_convert_fusion.1
  221.6 8.2 %fusion.38 = f32[4,768,512]{1,2,0:T(8,128)} fusion(bf16[512,1024,1]{1,0,2:T(8,128)(2,1)S(1)} %bitcast.160, bf16[4,1024,768]{2,1,0:T(8,128)(2,1)} %bitcast.183), kind=kOutput, calls=%fused_computation.83 | convolution fusion | flops 3221225472 | bytes 13631488 | tf_op jit(solution)/shard_map/td,gdf->gtf/dot_general | solution.py:1484
  229.8 2.5 multiply_reduce_fusion.2
  232.3 5.6 %fusion.15 = f32[4,768,512]{1,2,0:T(8,128)} fusion(bf16[4,1024,768]{2,1,0:T(8,128)(2,1)S(1)} %bitcast.178, f32[512,1024]{1,0:T(8,128)S(1)} %get-tuple-element.126, f32[1024]{0:T(1024)S(1)} %copy-done.9, f32[512]{0:T(512)S(1)} %add_rsqrt_fusion), kind=kOutput, calls=%fused_computation.31 | convolution fusion | flops 3222798336 | bytes 14686208 | tf_op jit(solution)/shard_map/td,gdf->gtf/dot_general | solution.py:1484
  237.9 10.8 %fusion.9 = (bf16[4,512,768]{2,1,0:T(8,128)(2,1)S(1)}, bf16[4,512,768]{2,1,0:T(8,128)(2,1)}, bf16[4,512,768]{2,1,0:T(8,128)(2,1)}) fusion(f32[4,768,512]{1,2,0:T(8,128)} %fusion.15, f32[4,768,512]{1,2,0:T(8,128)} %fusion.38, bf16[4,1024,768]{2,1,0:T(8,128)(2,1)S(1)} %bitcast.182, f32[512,1024]{1,0:T(8,128)S(1)} %get-tuple-element.126, ...), kind=kOutput, calls=%fused_computation.13 | convolution fusion | flops 3247964160 | bytes 30414848 | tf_op jit(solution)/shard_map/td,gdf->gtf/dot_general | solution.py:1484
  249.4 4.5 fusion.12
  254.2 1.3 copy.58.refs_1_
  255.5 6.7 %fusion.37 = f32[512,1024,1]{1,0,2:T(8,128)S(1)} fusion(bf16[4,512,768]{2,1,0:T(8,128)(2,1)} %get-tuple-element.111.refs_4_, bf16[4,1024,768]{2,1,0:T(8,128)(2,1)} %bitcast.179), kind=kOutput, calls=%fused_computation.82 | convolution fusion | flops 3221225472 | bytes 11534336 | tf_op jit(solution)/shard_map/gtf,gdf->td/dot_general | solution.py:1484
  262.2 16.6 %multiply_reduce_fusion = (f32[1024]{0:T(1024)}, f32[512]{0:T(512)S(1)}, f32[512,1024]{1,0:T(8,128)S(1)}) fusion(f32[512,1024]{1,0:T(8,128)S(1)} %get-tuple-element.126, f32[512]{0:T(512)S(1)} %add_rsqrt_fusion, f32[1024]{0:T(1024)S(1)} %copy-done.9, bf16[4,512,768]{2,1,0:T(8,128)(2,1)S(1)} %copy-done.17, bf16[4,1024,768]{2,1,0:T(8,128)(2,1)} %bitcast.175, ...), kind=kOutput, calls=%fused_computation.23 | convolution fusion | flops 3224893952 | bytes 15740928 | tf_op jit(solution)/shard_map/gtf,gdf->td/dot_general | solution.py:1484
  278.8 1.7 convert_bitcast_fusion
  281.3 4.3 convolution_bitcast_fusion.dhead_ref
  285.6 1.3 copy.57.refs_0_
  287.0 1.3 copy.59.refs_2_
  288.3 140.1 %delta_backward.1 = (bf16[4,512,1536]{2,1,0:T(8,128)(2,1)}, f32[8,8,512]{2,1,0:T(8,128)}, f32[8,4,512]{2,1,0:T(4,128)}, f32[1,256]{1,0:T(1,128)}, f32[11,128,256]{2,1,0:T(8,128)}, /*index=5*/bf16[8,64,1024]{2,1,0:T(8,128)(2,1)}) custom-call(f32[4,512,512]{2,1,0:T(8,128)} %convolution_bitcast_fusion.dhead_ref, f32[8,512,256]{2,1,0:T(8,128)} %get-tuple-element.73.o_ref, ...), custom_call_target="tpu_custom_call" | custom-call | flops 40000000000 | bytes 62914560 | tf_op jit(solution)/shard_map/delta_backward/pallas_call | solution.py:1418
  432.7 101.6 %scatter_sum.1 = (f32[6,128,256]{2,1,0:T(8,128)}, f32[280,128]{1,0:T(8,128)}, bf16[8,64,1024]{2,1,0:T(8,128)(2,1)}) custom-call(bf16[1024,512]{1,0:T(8,128)(2,1)} %get-tuple-element.81.lhs_ref, bf16[4,512,1536]{2,1,0:T(8,128)(2,1)} %get-tuple-element.82.refs_0_, f32[1,1024]{1,0:T(1,128)} %bitcast.191, f32[1,256]{1,0:T(1,128)} %get-tuple-element.83.refs_2_, ...), custom_call_target="tpu_custom_call" | custom-call | flops 12884901888 | bytes 12582912 | tf_op jit(solution)/shard_map/scatter_sum/pallas_call | solution.py:997
  534.4 1.2 copy-done.2
  535.6 1.1 copy-done.3
  537.7 2.3 assemble.1
  540.6 1.3 slice_bitcast_fusion.3
  541.9 1.3 slice_bitcast_fusion.6
  543.2 1.2 slice_bitcast_fusion.5
  (90 shorter events, 12.0 us)
Async XLA Ops:
  1.9 91.1 %copy-start.11 = (f32[8]{0:T(128)S(1)}, f32[8]{0:T(128)}, u32[]{:S(2)}) copy-start(f32[8]{0:T(128)} %param.30) | copy-start | bytes 100
  1.9 91.1 %copy-start.10 = (f32[8]{0:T(128)S(1)}, f32[8]{0:T(128)}, u32[]{:S(2)}) copy-start(f32[8]{0:T(128)} %param.31) | copy-start | bytes 100
  1.9 92.1 %copy-start.8 = (f32[4,4096]{1,0:T(4,128)S(1)}, f32[4,4096]{1,0:T(4,128)}, u32[]{:S(2)}) copy-start(f32[4,4096]{1,0:T(4,128)} %param.29) | copy-start | bytes 196612
  1.9 92.1 %slice-start = ((f32[4,4096]{1,0:T(4,128)}), f32[4,2048]{1,0:T(4,128)S(1)}, s32[]{:S(2)}) async-start(f32[4,4096]{1,0:T(4,128)} %param.29), calls=%async_computation | async-start | bytes 65536 | tf_op jit(solution)/shard_map/slice | solution.py:1541
  94.7 123.9 %copy-start.12 = (s32[8]{0:T(128)S(1)}, s32[8]{0:T(128)}, u32[]{:S(2)}) copy-start(s32[8]{0:T(128)} %param.21) | copy-start | bytes 100
  219.9 12.4 %slice-start.1 = ((s8[6291456]{0:T(1024)(128)(4,1)}), s8[4194304]{0:T(1024)(128)(4,1)S(1)}, s32[]{:S(2)}) async-start(s8[6291456]{0:T(1024)(128)(4,1)} %bitcast.176), calls=%async_computation.1 | async-start | bytes 8388608
  221.5 8.3 %copy-start.13 = (bf16[4,8,128,512]{3,2,1,0:T(8,128)(2,1)S(1)}, bf16[4,8,128,512]{3,2,1,0:T(8,128)(2,1)}, u32[]{:S(2)}) copy-start(bf16[4,8,128,512]{3,2,1,0:T(8,128)(2,1)} %get-tuple-element.66) | copy-start | bytes 12582916
  221.5 8.3 %copy-start.15 = (bf16[8,64,1024]{2,1,0:T(8,128)(2,1)S(1)}, bf16[8,64,1024]{2,1,0:T(8,128)(2,1)}, u32[]{:S(2)}) copy-start(bf16[8,64,1024]{2,1,0:T(8,128)(2,1)} %get-tuple-element.68.refs_8_) | copy-start | bytes 3145732
  221.5 8.2 %copy-start.16 = (bf16[4,512,512]{2,1,0:T(8,128)(2,1)S(1)}, bf16[4,512,512]{2,1,0:T(8,128)(2,1)}, u32[]{:S(2)}) copy-start(bf16[4,512,512]{2,1,0:T(8,128)(2,1)} %get-tuple-element.69.refs_6_) | copy-start | bytes 6291460
  221.5 10.7 %slice-start.2 = ((s8[6291456]{0:T(1024)(128)(4,1)}), s8[2097152]{0:T(1024)(128)(4,1)S(1)}, s32[]{:S(2)}) async-start(s8[6291456]{0:T(1024)(128)(4,1)} %bitcast.176), calls=%async_computation.2 | async-start | bytes 4194304
  229.8 2.5 copy-start.9
  229.8 8.1 %slice-start.3 = ((s8[6291456]{0:T(1024)(128)(4,1)}), s8[4194304]{0:T(1024)(128)(4,1)S(1)}, s32[]{:S(2)}) async-start(s8[6291456]{0:T(1024)(128)(4,1)} %bitcast.180), calls=%async_computation.3 | async-start | bytes 8388608
  232.3 5.6 %slice-start.4 = ((s8[6291456]{0:T(1024)(128)(4,1)}), s8[2097152]{0:T(1024)(128)(4,1)S(1)}, s32[]{:S(2)}) async-start(s8[6291456]{0:T(1024)(128)(4,1)} %bitcast.180), calls=%async_computation.4 | async-start | bytes 4194304
  232.3 17.1 %slice-start.5 = ((s8[6291456]{0:T(1024)(128)(4,1)}), s8[4194304]{0:T(1024)(128)(4,1)S(1)}, s32[]{:S(2)}) async-start(s8[6291456]{0:T(1024)(128)(4,1)} %bitcast.184), calls=%async_computation.5 | async-start | bytes 8388608
  237.9 11.5 %slice-start.6 = ((s8[6291456]{0:T(1024)(128)(4,1)}), s8[2097152]{0:T(1024)(128)(4,1)S(1)}, s32[]{:S(2)}) async-start(s8[6291456]{0:T(1024)(128)(4,1)} %bitcast.184), calls=%async_computation.6 | async-start | bytes 4194304
  248.8 5.2 copy-start.18
  255.5 6.7 %copy-start.17 = (bf16[4,512,768]{2,1,0:T(8,128)(2,1)S(1)}, bf16[4,512,768]{2,1,0:T(8,128)(2,1)}, u32[]{:S(2)}) copy-start(bf16[4,512,768]{2,1,0:T(8,128)(2,1)} %get-tuple-element.112.refs_5_) | copy-start | bytes 9437188
  262.1 16.6 %copy-start.5 = (bf16[8,64,1024]{2,1,0:T(8,128)(2,1)S(1)}, bf16[8,64,1024]{2,1,0:T(8,128)(2,1)}, u32[]{:S(2)}) copy-start(bf16[8,64,1024]{2,1,0:T(8,128)(2,1)} %get-tuple-element.67) | copy-start | bytes 3145732
  278.8 2.6 copy-start.14
  280.5 5.2 copy-start.7
  281.3 4.3 copy-start.6
  432.7 101.6 %copy-start = (f32[11,128,256]{2,1,0:T(8,128)S(1)}, f32[11,128,256]{2,1,0:T(8,128)}, u32[]{:S(2)}) copy-start(f32[11,128,256]{2,1,0:T(8,128)} %get-tuple-element.80.ffn_ref) | copy-start | bytes 4325380
  432.7 101.6 %copy-start.1 = (bf16[8,64,1024]{2,1,0:T(8,128)(2,1)S(1)}, bf16[8,64,1024]{2,1,0:T(8,128)(2,1)}, u32[]{:S(2)}) copy-start(bf16[8,64,1024]{2,1,0:T(8,128)(2,1)} %get-tuple-element.89.y_ref) | copy-start | bytes 3145732
  534.4 1.2 copy-start.2
  (2 other events, 2.0 us)

commit v4 on v3

--- a/solution.py
+++ b/solution.py
@@ -85,6 +85,11 @@
         inverses = [inv - mm(inv, part) for inv, part in zip(inverses, inner)]
         width *= 2
     return inverses
+
+
+def in_step(works):
+    while works:
+        works = [work for work in works if next(work, True) is None]
 
 
 def unit_parts(conv):
@@ -506,47 +511,56 @@
         rows, cols = masks(size)
         upper = (rows <= cols).astype(F32)
         convw = convw_ref[0]
-        kept = []
-        lowers = []
-        for c in range(chunks):
+        kept = [None] * chunks
+        lowers = [None] * chunks
+
+        def open_chunk(c):
             conv = conv_of(windows(raw_ref, ext_s, c, size), convw)
             _, q_silu, k_silu, value, q_scale, k_scale = unit_parts(conv)
             query = q_silu * (q_scale * DK ** (-0.5))
             keyed = k_silu * k_scale
+            yield
             gamma_row, gamma_col, beta = decays(ab_ref, c * size, size, upper)
             inclusive, strict = fades(gamma_row, gamma_col, rows, cols)
             gram = mm(jnp.concatenate([keyed, query], axis=0), keyed, 1, 1)
-            lowers.append(beta * gram[:size] * strict)
+            yield
+            lowers[c] = beta * gram[:size] * strict
             scores = gram[size:] * inclusive
             growth = jnp.exp(gamma_col)
             last = gamma_row[:, size - 1 :]
             rhs = jnp.concatenate([(beta * growth) * keyed, beta * value], axis=1)
-            kept.append((scores, rhs, query * growth, keyed * jnp.exp(last - gamma_col), last))
+            kept[c] = (scores, rhs, query * growth, keyed * jnp.exp(last - gamma_col), last)
+
+        in_step([open_chunk(c) for c in range(chunks)])
         inverses = invert_many(lowers, rows, cols)
         eye = (masks(DK)[0] == masks(DK)[1]).astype(F32)
-        phi_all = None
-        b_all = None
-        for c in range(chunks):
+        flows = [None] * chunks
+
+        def close_chunk(c):
             scores, rhs, query_g, keyed_g, last = kept[c]
             t_ref[0, c] = inverses[c]
             solved = mm(inverses[c], rhs)
+            yield
             mixed = mm(scores, solved)
+            yield
             moved = mm(keyed_g, solved, 0, 0)
+            yield
             query_e = query_g - mixed[:, :DK]
             phi = jnp.exp(last) * eye - moved[:, :DK]
-            inflow = moved[:, DK:]
             qe_ref[0, c * size : (c + 1) * size] = query_e
             qe_s[slot, c * size : (c + 1) * size] = query_e
             o0_s[slot, c * size : (c + 1) * size] = mixed[:, DK:]
             phi_ref[0, c] = phi.T
             phi_s[slot, c] = phi
-            b_s[slot, c] = inflow
-            if c == 0:
-                phi_all, b_all = phi, inflow
-            else:
-                moved_all = mm(phi, jnp.concatenate([phi_all, b_all], axis=1))
-                phi_all = moved_all[:, :DK]
-                b_all = moved_all[:, DK:] + inflow
+            b_s[slot, c] = moved[:, DK:]
+            flows[c] = phi
+
+        in_step([close_chunk(c) for c in range(chunks)])
+        phi_all, b_all = flows[0], b_s[slot, 0]
+        for c in range(1, chunks):
+            moved_all = mm(flows[c], jnp.concatenate([phi_all, b_all], axis=1))
+            phi_all = moved_all[:, :DK]
+            b_all = moved_all[:, DK:] + b_s[slot, c]
         phil_ref[0] = phi_all.T
         phil_s[slot] = phi_all
         bl_s[slot] = b_all
@@ -1147,17 +1161,24 @@
         d_state = recv_s[head]
         ext_s[0:HALO] = halo_ref[0, :, 0:HEADW]
         ext_s[HALO:] = raw_ref[0, 0:size, 0:HEADW]
-        d_conv_rows = [jnp.zeros((1, HEADW), F32) for _ in range(TAPS)]
-        for c in range(chunks - 1, -1, -1):
+        d_states = [None] * chunks
+        d_states[chunks - 1] = d_state
+        for c in range(chunks - 1, 0, -1):
+            d_states[c - 1] = mm(phi_late_ref[0, c], d_states[c]) + d_s[slot, c]
+        taps_grad = [None] * chunks
+
+        def work(c):
             at = slice(c * size, (c + 1) * size)
             shifted = windows(raw_ref, ext_s, c, size)
             conv = conv_of(shifted, convw)
             sig, q_silu, k_silu, value, q_scale, k_scale = unit_parts(conv)
             query = q_silu * (q_scale * DK ** (-0.5))
             keyed = k_silu * k_scale
+            yield
             gamma_row, gamma_col, beta = decays(ab_ref, c * size, size, upper)
             inclusive, strict = fades(gamma_row, gamma_col, rows, cols)
             gram = mm(jnp.concatenate([keyed, query], axis=0), keyed, 1, 1)
+            yield
             gram_f = gram[:size] * strict
             lower = beta * gram_f
             scores = gram[size:] * inclusive
@@ -1169,21 +1190,31 @@
             keyed_b = beta * grown
             keyed_g = keyed * tail
             state = s_ref[0, c]
+            d_state = d_states[c]
             inverse = t_ref[0, c]
             d_out = do_s[slot, at]
-            fresh = mm(inverse, beta * value - mm(keyed_b, state))
+            held = mm(keyed_b, state)
+            yield
+            fresh = mm(inverse, beta * value - held)
+            yield
             d_fresh = mm(scores, d_out, 0, 0) + mm(keyed_g, d_state)
+            yield
             d_rhs = mm(inverse, d_fresh, 0, 0)
+            yield
             stacked = jnp.concatenate([d_out, d_rhs], axis=0)
             by_fresh = mm(stacked, fresh, 1, 1)
+            yield
             by_state = mm(stacked, state, 1, 1)
+            yield
             d_scores = by_fresh[:size] * inclusive
             d_lower = -by_fresh[size:]
             d_query_g = by_state[:size]
             d_keyed_b = -by_state[size:]
             d_keyed_g = mm(fresh, d_state, 1, 1)
+            yield
             d_gram = d_lower * (beta * strict)
             by_keyed = mm(jnp.concatenate([d_scores, d_gram], axis=0), keyed)
+            yield
             d_query = by_keyed[:size] + growth * d_query_g
             d_keyed = (
                 by_keyed[size:]
@@ -1192,6 +1223,7 @@
                 + (beta * growth) * d_keyed_b
                 + tail * d_keyed_g
             )
+            yield
             d_value = beta * d_rhs
             d_beta = (
                 jnp.sum(d_rhs * value, axis=-1, keepdims=True)
@@ -1213,10 +1245,9 @@
             packed = jnp.where(lanes == 0, d_gamma, jnp.where(lanes == 1, d_beta, 0.0)).T[:8]
             row_id = lax.broadcasted_iota(jnp.int32, packed.shape, 0)
             packed = packed - jnp.where(row_id == 0, jnp.sum(moved, axis=0, keepdims=True), 0.0)
+            yield
             summed = mm(packed, upper, 1, 1) + at_end
             dab_ref[0, :, at] = jnp.where(row_id == 0, summed, packed)
-            if c > 0:
-                d_state = mm(phi_late_ref[0, c], d_state) + d_s[slot, c]
             d_q_silu = (DK ** (-0.5) * q_scale) * (
                 d_query
                 - q_silu * (q_scale * q_scale) * jnp.sum(q_silu * d_query, axis=-1, keepdims=True)
@@ -1228,8 +1259,11 @@
             d_silu = jnp.concatenate([d_q_silu, d_k_silu, d_value], axis=1)
             d_conv = d_silu * sig * (1.0 + conv * (1.0 - sig))
             g_s[HALO + c * size : HALO + (c + 1) * size] = d_conv
-            for i in range(TAPS):
-                d_conv_rows[i] = d_conv_rows[i] + jnp.sum(shifted[i] * d_conv, axis=0, keepdims=True)
+            taps_grad[c] = [jnp.sum(shifted[i] * d_conv, axis=0, keepdims=True) for i in range(TAPS)]
+
+        for first in range(0, chunks, 2):
+            in_step([work(c) for c in range(first, min(first + 2, chunks))])
+        d_conv_rows = [sum(row[i] for row in taps_grad[1:]) + taps_grad[0][i] for i in range(TAPS)]
         for i in range(TAPS):
             dconv_ref[0, i : i + 1] = d_conv_rows[i]
         for base, count in [(0, HALO)] + [(HALO + c * size, size) for c in range(chunks)]:

time: 550 us -> 543 us (0.987)
  matrix products: 60.8 us -> 51.3 us
    dot_general x9, matrix products: 60.8 us -> 51.3 us  [dot(): return jnp.einsum(spec, a, b, preferred_element_type=F32)]
where the time goes in v4:
time: 543 us; the launch traced here: 533 us
  Pallas kernels  455 us (84%)
  matrix products  51.3 us (9%)
  local copies, waits for them, and re-layouts  17.9 us (3%)
  other arithmetic  7.53 us (1%)
    pallas_call x1, Pallas kernels, backward_core(): pl.pallas_call(partial(backward_kernel, heads, parts, bits, plan, rows),...  138 us
    pallas_call x1, Pallas kernels, forward_core(): pl.pallas_call(partial(forward_kernel, heads, parts, bits, pieces), grid=...  123 us
    pallas_call x1, Pallas kernels, scatter_sum(): pl.pallas_call(partial(scatter_kernel, bits, parts, plan, rows), out_shap...  102 us
    pallas_call x1, Pallas kernels, prologue(): pl.pallas_call(partial(prologue_kernel, bits, parts, pieces), out_shape=(...  89.3 us
    dot_general x9, matrix products, dot(): return jnp.einsum(spec, a, b, preferred_element_type=F32)  51.3 us

profile of v4, /device:TPU:0, one launch (start us, length us, event | category | flops | bytes accessed | tf_op | source)
XLA Modules:
  0.0 533.0 jit_solution(10715102185155735918)
XLA Ops:
  1.9 89.3 %prologue.1 = (bf16[8,64,1024]{2,1,0:T(8,128)(2,1)}, bf16[4,8,128,1536]{3,2,1,0:T(8,128)(2,1)}, bf16[4,8,16,128]{3,2,1,0:T(8,128)(2,1)}, f32[4,512,1536]{2,1,0:T...) custom-call(bf16[8,64,1024]{2,1,0:T(8,128)(2,1)} %refs_0_.2, ...), custom_call_target="tpu_custom_call" | custom-call | flops 6442450944 | bytes 41943040 | tf_op jit(solution)/shard_map/prologue/pallas_call | solution.py:399
  91.3 1.7 fusion.20
  94.7 123.1 %delta_forward.1 = (bf16[4,512,512]{2,1,0:T(8,128)(2,1)}, f32[8,512,256]{2,1,0:T(8,128)}, f32[8,4,128,256]{3,2,1,0:T(8,128)}, f32[8,4,128,128]{3,2,1,0:T(8,128)}...) custom-call(f32[4,512,1536]{2,1,0:T(8,128)} %get-tuple-element.60.ra, ...), custom_call_target="tpu_custom_call" | custom-call | flops 20000000000 | bytes 41943040 | tf_op jit(solution)/shard_map/delta_forward/pallas_call | solution.py:1376
  219.1 1.6 multiply_convert_fusion.1
  220.8 8.6 %fusion.38 = f32[4,768,512]{1,2,0:T(8,128)} fusion(bf16[512,1024,1]{1,0,2:T(8,128)(2,1)S(1)} %bitcast.160, bf16[4,1024,768]{2,1,0:T(8,128)(2,1)} %bitcast.183), kind=kOutput, calls=%fused_computation.83 | convolution fusion | flops 3221225472 | bytes 13631488 | tf_op jit(solution)/shard_map/td,gdf->gtf/dot_general | solution.py:1518
  229.4 2.5 multiply_reduce_fusion.2
  232.0 5.6 %fusion.15 = f32[4,768,512]{1,2,0:T(8,128)} fusion(bf16[4,1024,768]{2,1,0:T(8,128)(2,1)S(1)} %bitcast.178, f32[512,1024]{1,0:T(8,128)S(1)} %get-tuple-element.126, f32[1024]{0:T(1024)S(1)} %copy-done.9, f32[512]{0:T(512)S(1)} %add_rsqrt_fusion), kind=kOutput, calls=%fused_computation.31 | convolution fusion | flops 3222798336 | bytes 14686208 | tf_op jit(solution)/shard_map/td,gdf->gtf/dot_general | solution.py:1518
  237.6 10.8 %fusion.9 = (bf16[4,512,768]{2,1,0:T(8,128)(2,1)S(1)}, bf16[4,512,768]{2,1,0:T(8,128)(2,1)}, bf16[4,512,768]{2,1,0:T(8,128)(2,1)}) fusion(f32[4,768,512]{1,2,0:T(8,128)} %fusion.15, f32[4,768,512]{1,2,0:T(8,128)} %fusion.38, bf16[4,1024,768]{2,1,0:T(8,128)(2,1)S(1)} %bitcast.182, f32[512,1024]{1,0:T(8,128)S(1)} %get-tuple-element.126, ...), kind=kOutput, calls=%fused_computation.13 | convolution fusion | flops 3247964160 | bytes 30414848 | tf_op jit(solution)/shard_map/td,gdf->gtf/dot_general | solution.py:1518
  249.1 4.5 fusion.12
  253.8 1.3 copy.58.refs_1_
  255.1 6.7 %fusion.37 = f32[512,1024,1]{1,0,2:T(8,128)S(1)} fusion(bf16[4,512,768]{2,1,0:T(8,128)(2,1)} %get-tuple-element.111.refs_4_, bf16[4,1024,768]{2,1,0:T(8,128)(2,1)} %bitcast.179), kind=kOutput, calls=%fused_computation.82 | convolution fusion | flops 3221225472 | bytes 11534336 | tf_op jit(solution)/shard_map/gtf,gdf->td/dot_general | solution.py:1518
  261.8 6.8 %multiply_reduce_fusion = (f32[1024]{0:T(1024)}, f32[512]{0:T(512)S(1)}, f32[512,1024]{1,0:T(8,128)S(1)}) fusion(f32[512,1024]{1,0:T(8,128)S(1)} %get-tuple-element.126, f32[512]{0:T(512)S(1)} %add_rsqrt_fusion, f32[1024]{0:T(1024)S(1)} %copy-done.9, bf16[4,512,768]{2,1,0:T(8,128)(2,1)S(1)} %copy-done.17, bf16[4,1024,768]{2,1,0:T(8,128)(2,1)} %bitcast.175, ...), kind=kOutput, calls=%fused_computation.23 | convolution fusion | flops 3224893952 | bytes 15740928 | tf_op jit(solution)/shard_map/gtf,gdf->td/dot_general | solution.py:1518
  268.6 1.7 convert_bitcast_fusion
  271.2 4.3 convolution_bitcast_fusion.dhead_ref
  275.5 1.3 copy.57.refs_0_
  276.8 1.3 copy.59.refs_2_
  278.1 137.7 %delta_backward.1 = (bf16[4,512,1536]{2,1,0:T(8,128)(2,1)}, f32[8,8,512]{2,1,0:T(8,128)}, f32[8,4,512]{2,1,0:T(4,128)}, f32[1,256]{1,0:T(1,128)}, f32[11,128,256]{2,1,0:T(8,128)}, /*index=5*/bf16[8,64,1024]{2,1,0:T(8,128)(2,1)}) custom-call(f32[4,512,512]{2,1,0:T(8,128)} %convolution_bitcast_fusion.dhead_ref, f32[8,512,256]{2,1,0:T(8,128)} %get-tuple-element.73.o_ref, ...), custom_call_target="tpu_custom_call" | custom-call | flops 40000000000 | bytes 62914560 | tf_op jit(solution)/shard_map/delta_backward/pallas_call | solution.py:1452
  420.2 102.4 %scatter_sum.1 = (f32[6,128,256]{2,1,0:T(8,128)}, f32[280,128]{1,0:T(8,128)}, bf16[8,64,1024]{2,1,0:T(8,128)(2,1)}) custom-call(bf16[1024,512]{1,0:T(8,128)(2,1)} %get-tuple-element.81.lhs_ref, bf16[4,512,1536]{2,1,0:T(8,128)(2,1)} %get-tuple-element.82.refs_0_, f32[1,1024]{1,0:T(1,128)} %bitcast.191, f32[1,256]{1,0:T(1,128)} %get-tuple-element.83.refs_2_, ...), custom_call_target="tpu_custom_call" | custom-call | flops 12884901888 | bytes 12582912 | tf_op jit(solution)/shard_map/scatter_sum/pallas_call | solution.py:1011
  522.7 1.2 copy-done.2
  523.9 1.1 copy-done.3
  525.9 2.3 assemble.1
  528.9 1.3 slice_bitcast_fusion.3
  530.1 1.3 slice_bitcast_fusion.6
  531.5 1.2 slice_bitcast_fusion.5
  (90 shorter events, 12.0 us)
Async XLA Ops:
  1.9 91.1 %copy-start.11 = (f32[8]{0:T(128)S(1)}, f32[8]{0:T(128)}, u32[]{:S(2)}) copy-start(f32[8]{0:T(128)} %param.30) | copy-start | bytes 100
  1.9 91.1 %copy-start.10 = (f32[8]{0:T(128)S(1)}, f32[8]{0:T(128)}, u32[]{:S(2)}) copy-start(f32[8]{0:T(128)} %param.31) | copy-start | bytes 100
  1.9 92.1 %copy-start.8 = (f32[4,4096]{1,0:T(4,128)S(1)}, f32[4,4096]{1,0:T(4,128)}, u32[]{:S(2)}) copy-start(f32[4,4096]{1,0:T(4,128)} %param.29) | copy-start | bytes 196612
  1.9 92.1 %slice-start = ((f32[4,4096]{1,0:T(4,128)}), f32[4,2048]{1,0:T(4,128)S(1)}, s32[]{:S(2)}) async-start(f32[4,4096]{1,0:T(4,128)} %param.29), calls=%async_computation | async-start | bytes 65536 | tf_op jit(solution)/shard_map/slice | solution.py:1575
  94.7 123.2 %copy-start.12 = (s32[8]{0:T(128)S(1)}, s32[8]{0:T(128)}, u32[]{:S(2)}) copy-start(s32[8]{0:T(128)} %param.21) | copy-start | bytes 100
  219.1 12.8 %slice-start.1 = ((s8[6291456]{0:T(1024)(128)(4,1)}), s8[4194304]{0:T(1024)(128)(4,1)S(1)}, s32[]{:S(2)}) async-start(s8[6291456]{0:T(1024)(128)(4,1)} %bitcast.176), calls=%async_computation.1 | async-start | bytes 8388608
  220.8 8.7 %copy-start.13 = (bf16[4,8,128,512]{3,2,1,0:T(8,128)(2,1)S(1)}, bf16[4,8,128,512]{3,2,1,0:T(8,128)(2,1)}, u32[]{:S(2)}) copy-start(bf16[4,8,128,512]{3,2,1,0:T(8,128)(2,1)} %get-tuple-element.66) | copy-start | bytes 12582916
  220.8 8.6 %copy-start.15 = (bf16[8,64,1024]{2,1,0:T(8,128)(2,1)S(1)}, bf16[8,64,1024]{2,1,0:T(8,128)(2,1)}, u32[]{:S(2)}) copy-start(bf16[8,64,1024]{2,1,0:T(8,128)(2,1)} %get-tuple-element.68.refs_8_) | copy-start | bytes 3145732
  220.8 8.6 %copy-start.16 = (bf16[4,512,512]{2,1,0:T(8,128)(2,1)S(1)}, bf16[4,512,512]{2,1,0:T(8,128)(2,1)}, u32[]{:S(2)}) copy-start(bf16[4,512,512]{2,1,0:T(8,128)(2,1)} %get-tuple-element.69.refs_6_) | copy-start | bytes 6291460
  220.8 11.1 %slice-start.2 = ((s8[6291456]{0:T(1024)(128)(4,1)}), s8[2097152]{0:T(1024)(128)(4,1)S(1)}, s32[]{:S(2)}) async-start(s8[6291456]{0:T(1024)(128)(4,1)} %bitcast.176), calls=%async_computation.2 | async-start | bytes 4194304
  229.4 2.5 copy-start.9
  229.4 8.1 %slice-start.3 = ((s8[6291456]{0:T(1024)(128)(4,1)}), s8[4194304]{0:T(1024)(128)(4,1)S(1)}, s32[]{:S(2)}) async-start(s8[6291456]{0:T(1024)(128)(4,1)} %bitcast.180), calls=%async_computation.3 | async-start | bytes 8388608
  231.9 5.6 %slice-start.4 = ((s8[6291456]{0:T(1024)(128)(4,1)}), s8[2097152]{0:T(1024)(128)(4,1)S(1)}, s32[]{:S(2)}) async-start(s8[6291456]{0:T(1024)(128)(4,1)} %bitcast.180), calls=%async_computation.4 | async-start | bytes 4194304
  232.0 17.1 %slice-start.5 = ((s8[6291456]{0:T(1024)(128)(4,1)}), s8[4194304]{0:T(1024)(128)(4,1)S(1)}, s32[]{:S(2)}) async-start(s8[6291456]{0:T(1024)(128)(4,1)} %bitcast.184), calls=%async_computation.5 | async-start | bytes 8388608
  237.5 11.5 %slice-start.6 = ((s8[6291456]{0:T(1024)(128)(4,1)}), s8[2097152]{0:T(1024)(128)(4,1)S(1)}, s32[]{:S(2)}) async-start(s8[6291456]{0:T(1024)(128)(4,1)} %bitcast.184), calls=%async_computation.6 | async-start | bytes 4194304
  248.4 5.2 copy-start.18
  255.1 6.7 %copy-start.17 = (bf16[4,512,768]{2,1,0:T(8,128)(2,1)S(1)}, bf16[4,512,768]{2,1,0:T(8,128)(2,1)}, u32[]{:S(2)}) copy-start(bf16[4,512,768]{2,1,0:T(8,128)(2,1)} %get-tuple-element.112.refs_5_) | copy-start | bytes 9437188
  261.8 6.8 %copy-start.5 = (bf16[8,64,1024]{2,1,0:T(8,128)(2,1)S(1)}, bf16[8,64,1024]{2,1,0:T(8,128)(2,1)}, u32[]{:S(2)}) copy-start(bf16[8,64,1024]{2,1,0:T(8,128)(2,1)} %get-tuple-element.67) | copy-start | bytes 3145732
  268.6 2.6 copy-start.14
  270.3 5.2 copy-start.7
  271.2 4.3 copy-start.6
  420.2 102.5 %copy-start = (f32[11,128,256]{2,1,0:T(8,128)S(1)}, f32[11,128,256]{2,1,0:T(8,128)}, u32[]{:S(2)}) copy-start(f32[11,128,256]{2,1,0:T(8,128)} %get-tuple-element.80.ffn_ref) | copy-start | bytes 4325380
  420.2 102.5 %copy-start.1 = (bf16[8,64,1024]{2,1,0:T(8,128)(2,1)S(1)}, bf16[8,64,1024]{2,1,0:T(8,128)(2,1)}, u32[]{:S(2)}) copy-start(bf16[8,64,1024]{2,1,0:T(8,128)(2,1)} %get-tuple-element.89.y_ref) | copy-start | bytes 3145732
  522.7 1.2 copy-start.2
  (2 other events, 2.0 us)

commit v5 on v4

--- a/solution.py
+++ b/solution.py
@@ -459,15 +459,13 @@
         swap.start()
 
     last = 2 * (heads + lag) - 1
-    for now in range(min(gather.moves(), last)):
-        @pl.when(step * 2 + pl.program_id(1) == now)
-        def _():
-            gather.move(now)
-
-    @pl.when(step * 2 + pl.program_id(1) == last)
-    def _():
-        for now in range(last, gather.moves()):
-            gather.move(now)
+    for spot in range(last + 1):
+        moves = [m for m in range(gather.moves()) if m * last // (gather.moves() - 1) == spot]
+        if moves:
+            @pl.when(step * 2 + pl.program_id(1) == spot)
+            def _():
+                for m in moves:
+                    gather.move(m)
 
     def hop(h):
         return pltpu.make_async_remote_copy(
@@ -781,7 +779,7 @@
                             mine_a = self.ra[k - 1][t_k, j, own_a]
                             mine_b = self.rb[k - 1][t_k, j, own_b]
                         for buf, mine in ((self.ra[k], mine_a), (self.rb[k], mine_b)):
-                            buf[t_k, j, m] = (buf[t_k, j, m].astype(F32) + mine.astype(F32)).astype(BF16)
+                            buf[t_k, j, m] = buf[t_k, j, m] + mine
                 if k + 1 < planes:
                     self.a_hop(k + 1, t_k).start()
                     for copy in self.b_hops(k + 1, t_k):
@@ -801,9 +799,7 @@
             @pl.loop(0, parts)
             def _(j):
                 for m in range(half):
-                    self.r1[t_1, j, m] = (
-                        self.r1[t_1, j, m].astype(F32) + self.grad_s[slot, j, m, color].astype(F32)
-                    ).astype(BF16)
+                    self.r1[t_1, j, m] = self.r1[t_1, j, m] + self.grad_s[slot, j, m, color]
 
             self.a_hop(0, t_1).start()
             for copy in self.b_hops(0, t_1):
@@ -1308,8 +1304,9 @@
 
 
 def assemble_kernel(
-    per, base, ffn_ref, proj_ref, vec_ref, y_ref, g_ref,
+    per, starts, ffn_ref, proj_ref, vec_ref, y_ref, g_ref,
     query_ref, key_ref, value_ref, outgate_ref, out_ref, gate_ref, up_ref, down_ref, conv_ref, y_out, g_out,
+    mix_ref, gain_ref, hgain_ref, small_ref,
 ):
     y_out[...] = y_ref[...]
     g_out[...] = g_ref[...]
@@ -1332,25 +1329,40 @@
     heads = width // HEADW
     for h in range(heads):
         for tap in range(TAPS):
-            row = base + (h * TAPS + tap) * HEADW // 128
+            row = starts[3] + (h * TAPS + tap) * HEADW // 128
             spots = [h * DK, (heads + h) * DK, 2 * heads * DK + h * DV, 2 * heads * DK + h * DV + 128]
             for i, spot in enumerate(spots):
                 conv_ref[tap : tap + 1, spot : spot + 128] = vec_ref[row + i : row + i + 1]
-
-
-def assemble(ffn, proj, vec, y, g, per, hidden, base, conv_shape):
+    mix_ref[...] = vec_ref[starts[0] : starts[1]]
+    gain_ref[...] = vec_ref[starts[1] : starts[2]]
+    hgain_ref[...] = vec_ref[starts[2] : starts[3]]
+    smalls, rows = small_ref.shape
+    lines = starts[1] - starts[0]
+    first = lax.axis_index("dp") * rows
+    share = lax.axis_index("mp")
+    shift = lax.rem(first, 128)
+    pick = lax.broadcasted_iota(jnp.int32, (128, rows), 0) == lax.broadcasted_iota(jnp.int32, (128, rows), 1) + shift
+    for c in range(smalls):
+        row = vec_ref[pl.ds(starts[5] + (share * smalls + c) * lines + lax.div(first, 128), 1)]
+        if rows != 128:
+            row = jnp.sum(jnp.where(pick, row.T, 0.0), axis=0, keepdims=True)
+        small_ref[c : c + 1] = row
+
+
+def assemble(ffn, proj, vec, y, g, per, hidden, starts, conv_shape):
     rows = ffn.shape[1]
     f32 = lambda *shape: jax.ShapeDtypeStruct(shape, F32)
     vmem_spec = pl.BlockSpec(memory_space=pltpu.VMEM)
     return pl.pallas_call(
-        partial(assemble_kernel, per, base),
+        partial(assemble_kernel, per, starts),
         out_shape=(
             f32(rows, per * DK), f32(rows, per * DK), f32(rows, per * DV), f32(rows, per * DV), f32(rows, per * DV),
             f32(hidden, rows), f32(hidden, rows), f32(hidden, rows), f32(*conv_shape),
             jax.ShapeDtypeStruct(y.shape, BF16), jax.ShapeDtypeStruct(g.shape, BF16),
+            *[f32(starts[i + 1] - starts[i], 128) for i in range(3)], f32(2 * per, rows),
         ),
         in_specs=[vmem_spec] * 5,
-        out_specs=(vmem_spec,) * 11,
+        out_specs=(vmem_spec,) * 15,
         compiler_params=pltpu.CompilerParams(vmem_limit_bytes=40 * 2**20),
         cost_estimate=pl.CostEstimate(flops=0, bytes_accessed=10 * 2**20, transcendentals=0),
         name="assemble",
@@ -1626,28 +1638,26 @@
     )
     starts, _ = small_rows(heads, width, 2 * heads)
     part = lambda i: sums[starts[i] : starts[i + 1]].reshape(-1)
-    (s_query, s_key, s_value, s_outgate, s_out, s_gate, s_up, s_down, s_conv, final_out, final_grad) = assemble(
-        sums_ffn, sums_proj, sums, final_out, final_grad, per, hidden, starts[3], conv_weight.shape
+    (s_query, s_key, s_value, s_outgate, s_out, s_gate, s_up, s_down, s_conv, final_out, final_grad,
+     s_mix, s_gain, s_hgain, s_small) = assemble(
+        sums_ffn, sums_proj, sums, final_out, final_grad, per, hidden, starts, conv_weight.shape
     )
-    small_sum = part(5).reshape(parts, 2 * per, width)
-    mine = lax.dynamic_slice(small_sum, (share, 0, group * local_rows), (1, 2 * per, local_rows))[0].T
-
     return (
         final_out,
         final_grad,
-        part(0),
+        s_mix.reshape(-1),
         s_query,
         s_key,
         s_value,
         s_outgate,
-        mine[:, :per],
-        mine[:, per:],
+        s_small[:per].T,
+        s_small[per:].T,
         s_conv,
         part(4)[:heads],
         part(4)[heads : 2 * heads],
-        part(2),
+        s_hgain.reshape(-1),
         s_out,
-        part(1),
+        s_gain.reshape(-1),
         s_gate.T,
         s_up.T,
         s_down.T,

time: 543 us -> 538 us (level)
  no operation moved by 1% of the time
where the time goes in v5:
time: 538 us; the launch traced here: 528 us
  Pallas kernels  453 us (84%)
  matrix products  51.3 us (10%)
  local copies, waits for them, and re-layouts  14.6 us (3%)
  other arithmetic  7.53 us (1%)
    pallas_call x1, Pallas kernels, backward_core(): pl.pallas_call(partial(backward_kernel, heads, parts, bits, plan, rows),...  137 us
    pallas_call x1, Pallas kernels, forward_core(): pl.pallas_call(partial(forward_kernel, heads, parts, bits, pieces), grid=...  123 us
    pallas_call x1, Pallas kernels, scatter_sum(): pl.pallas_call(partial(scatter_kernel, bits, parts, plan, rows), out_shap...  102 us
    pallas_call x1, Pallas kernels, prologue(): pl.pallas_call(partial(prologue_kernel, bits, parts, pieces), out_shape=(...  89.4 us
    dot_general x9, matrix products, dot(): return jnp.einsum(spec, a, b, preferred_element_type=F32)  51.3 us

profile of v5, /device:TPU:0, one launch (start us, length us, event | category | flops | bytes accessed | tf_op | source)
XLA Modules:
  0.0 527.9 jit_solution(1429423572839305921)
XLA Ops:
  1.9 89.4 %prologue.1 = (bf16[8,64,1024]{2,1,0:T(8,128)(2,1)}, bf16[4,8,128,1536]{3,2,1,0:T(8,128)(2,1)}, bf16[4,8,16,128]{3,2,1,0:T(8,128)(2,1)}, f32[4,512,1536]{2,1,0:T...) custom-call(bf16[8,64,1024]{2,1,0:T(8,128)(2,1)} %refs_0_.2, ...), custom_call_target="tpu_custom_call" | custom-call | flops 6442450944 | bytes 41943040 | tf_op jit(solution)/shard_map/prologue/pallas_call | solution.py:399
  91.4 1.7 fusion.20
  94.8 122.8 %delta_forward.1 = (bf16[4,512,512]{2,1,0:T(8,128)(2,1)}, f32[8,512,256]{2,1,0:T(8,128)}, f32[8,4,128,256]{3,2,1,0:T(8,128)}, f32[8,4,128,128]{3,2,1,0:T(8,128)}...) custom-call(f32[4,512,1536]{2,1,0:T(8,128)} %get-tuple-element.64.ra, ...), custom_call_target="tpu_custom_call" | custom-call | flops 20000000000 | bytes 41943040 | tf_op jit(solution)/shard_map/delta_forward/pallas_call | solution.py:1388
  219.0 1.6 multiply_convert_fusion.1
  220.6 8.6 %fusion.37 = f32[4,768,512]{1,2,0:T(8,128)} fusion(bf16[512,1024,1]{1,0,2:T(8,128)(2,1)S(1)} %bitcast.157, bf16[4,1024,768]{2,1,0:T(8,128)(2,1)} %bitcast.183), kind=kOutput, calls=%fused_computation.80 | convolution fusion | flops 3221225472 | bytes 13631488 | tf_op jit(solution)/shard_map/td,gdf->gtf/dot_general | solution.py:1530
  229.2 2.4 multiply_reduce_fusion.2
  231.8 5.5 %fusion.15 = f32[4,768,512]{1,2,0:T(8,128)} fusion(bf16[4,1024,768]{2,1,0:T(8,128)(2,1)S(1)} %bitcast.178, f32[512,1024]{1,0:T(8,128)S(1)} %get-tuple-element.132, f32[1024]{0:T(1024)S(1)} %copy-done.9, f32[512]{0:T(512)S(1)} %add_rsqrt_fusion), kind=kOutput, calls=%fused_computation.31 | convolution fusion | flops 3222798336 | bytes 14686208 | tf_op jit(solution)/shard_map/td,gdf->gtf/dot_general | solution.py:1530
  237.3 10.9 %fusion.9 = (bf16[4,512,768]{2,1,0:T(8,128)(2,1)S(1)}, bf16[4,512,768]{2,1,0:T(8,128)(2,1)}, bf16[4,512,768]{2,1,0:T(8,128)(2,1)}) fusion(f32[4,768,512]{1,2,0:T(8,128)} %fusion.15, f32[4,768,512]{1,2,0:T(8,128)} %fusion.37, bf16[4,1024,768]{2,1,0:T(8,128)(2,1)S(1)} %bitcast.182, f32[512,1024]{1,0:T(8,128)S(1)} %get-tuple-element.132, ...), kind=kOutput, calls=%fused_computation.13 | convolution fusion | flops 3247964160 | bytes 30414848 | tf_op jit(solution)/shard_map/td,gdf->gtf/dot_general | solution.py:1530
  248.8 4.5 fusion.12
  253.5 1.3 copy.58.refs_1_
  254.9 6.6 %fusion.36 = f32[512,1024,1]{1,0,2:T(8,128)S(1)} fusion(bf16[4,512,768]{2,1,0:T(8,128)(2,1)} %get-tuple-element.119.refs_4_, bf16[4,1024,768]{2,1,0:T(8,128)(2,1)} %bitcast.179), kind=kOutput, calls=%fused_computation.79 | convolution fusion | flops 3221225472 | bytes 11534336 | tf_op jit(solution)/shard_map/gtf,gdf->td/dot_general | solution.py:1530
  261.5 6.8 %multiply_reduce_fusion = (f32[1024]{0:T(1024)}, f32[512]{0:T(512)S(1)}, f32[512,1024]{1,0:T(8,128)S(1)}) fusion(f32[512,1024]{1,0:T(8,128)S(1)} %get-tuple-element.132, f32[512]{0:T(512)S(1)} %add_rsqrt_fusion, f32[1024]{0:T(1024)S(1)} %copy-done.9, bf16[4,512,768]{2,1,0:T(8,128)(2,1)S(1)} %copy-done.17, bf16[4,1024,768]{2,1,0:T(8,128)(2,1)} %bitcast.175, ...), kind=kOutput, calls=%fused_computation.23 | convolution fusion | flops 3224893952 | bytes 15740928 | tf_op jit(solution)/shard_map/gtf,gdf->td/dot_general | solution.py:1530
  268.3 1.7 convert_bitcast_fusion
  270.0 0.9 copy-done.14
  270.9 4.3 convolution_bitcast_fusion.dhead_ref
  275.2 1.3 copy.57.refs_0_
  276.5 1.3 copy.59.refs_2_
  277.8 137.0 %delta_backward.1 = (bf16[4,512,1536]{2,1,0:T(8,128)(2,1)}, f32[8,8,512]{2,1,0:T(8,128)}, f32[8,4,512]{2,1,0:T(4,128)}, f32[1,256]{1,0:T(1,128)}, f32[11,128,256]{2,1,0:T(8,128)}, /*index=5*/bf16[8,64,1024]{2,1,0:T(8,128)(2,1)}) custom-call(f32[4,512,512]{2,1,0:T(8,128)} %convolution_bitcast_fusion.dhead_ref, f32[8,512,256]{2,1,0:T(8,128)} %get-tuple-element.77.o_ref, ...), custom_call_target="tpu_custom_call" | custom-call | flops 40000000000 | bytes 62914560 | tf_op jit(solution)/shard_map/delta_backward/pallas_call | solution.py:1464
  414.9 1.1 slice_reduce_fusion.1
  419.3 101.7 %scatter_sum.1 = (f32[6,128,256]{2,1,0:T(8,128)}, f32[280,128]{1,0:T(8,128)}, bf16[8,64,1024]{2,1,0:T(8,128)(2,1)}) custom-call(bf16[1024,512]{1,0:T(8,128)(2,1)} %get-tuple-element.85.lhs_ref, bf16[4,512,1536]{2,1,0:T(8,128)(2,1)} %get-tuple-element.86.refs_0_, f32[1,1024]{1,0:T(1,128)} %bitcast.191, f32[1,256]{1,0:T(1,128)} %get-tuple-element.87.refs_2_, ...), custom_call_target="tpu_custom_call" | custom-call | flops 12884901888 | bytes 12582912 | tf_op jit(solution)/shard_map/scatter_sum/pallas_call | solution.py:1007
  521.0 1.2 copy-done.2
  522.2 1.1 copy-done.3
  523.4 0.9 copy-done.4
  524.3 2.2 assemble.1
  (85 shorter events, 9.6 us)
Async XLA Ops:
  1.9 91.2 %copy-start.11 = (f32[8]{0:T(128)S(1)}, f32[8]{0:T(128)}, u32[]{:S(2)}) copy-start(f32[8]{0:T(128)} %param.30) | copy-start | bytes 100
  1.9 91.2 %copy-start.10 = (f32[8]{0:T(128)S(1)}, f32[8]{0:T(128)}, u32[]{:S(2)}) copy-start(f32[8]{0:T(128)} %param.31) | copy-start | bytes 100
  1.9 92.2 %copy-start.8 = (f32[4,4096]{1,0:T(4,128)S(1)}, f32[4,4096]{1,0:T(4,128)}, u32[]{:S(2)}) copy-start(f32[4,4096]{1,0:T(4,128)} %param.29) | copy-start | bytes 196612
  1.9 92.2 %slice-start = ((f32[4,4096]{1,0:T(4,128)}), f32[4,2048]{1,0:T(4,128)S(1)}, s32[]{:S(2)}) async-start(f32[4,4096]{1,0:T(4,128)} %param.29), calls=%async_computation | async-start | bytes 65536 | tf_op jit(solution)/shard_map/slice | solution.py:1587
  94.8 122.9 %copy-start.12 = (s32[8]{0:T(128)S(1)}, s32[8]{0:T(128)}, u32[]{:S(2)}) copy-start(s32[8]{0:T(128)} %param.21) | copy-start | bytes 100
  218.9 12.8 %slice-start.1 = ((s8[6291456]{0:T(1024)(128)(4,1)}), s8[4194304]{0:T(1024)(128)(4,1)S(1)}, s32[]{:S(2)}) async-start(s8[6291456]{0:T(1024)(128)(4,1)} %bitcast.176), calls=%async_computation.1 | async-start | bytes 8388608
  220.6 8.6 %copy-start.13 = (bf16[4,8,128,512]{3,2,1,0:T(8,128)(2,1)S(1)}, bf16[4,8,128,512]{3,2,1,0:T(8,128)(2,1)}, u32[]{:S(2)}) copy-start(bf16[4,8,128,512]{3,2,1,0:T(8,128)(2,1)} %get-tuple-element.70) | copy-start | bytes 12582916
  220.6 8.6 %copy-start.15 = (bf16[8,64,1024]{2,1,0:T(8,128)(2,1)S(1)}, bf16[8,64,1024]{2,1,0:T(8,128)(2,1)}, u32[]{:S(2)}) copy-start(bf16[8,64,1024]{2,1,0:T(8,128)(2,1)} %get-tuple-element.72.refs_8_) | copy-start | bytes 3145732
  220.6 8.6 %copy-start.16 = (bf16[4,512,512]{2,1,0:T(8,128)(2,1)S(1)}, bf16[4,512,512]{2,1,0:T(8,128)(2,1)}, u32[]{:S(2)}) copy-start(bf16[4,512,512]{2,1,0:T(8,128)(2,1)} %get-tuple-element.73.refs_6_) | copy-start | bytes 6291460
  220.6 11.1 %slice-start.2 = ((s8[6291456]{0:T(1024)(128)(4,1)}), s8[2097152]{0:T(1024)(128)(4,1)S(1)}, s32[]{:S(2)}) async-start(s8[6291456]{0:T(1024)(128)(4,1)} %bitcast.176), calls=%async_computation.2 | async-start | bytes 4194304
  229.2 2.5 copy-start.9
  229.2 8.0 %slice-start.3 = ((s8[6291456]{0:T(1024)(128)(4,1)}), s8[4194304]{0:T(1024)(128)(4,1)S(1)}, s32[]{:S(2)}) async-start(s8[6291456]{0:T(1024)(128)(4,1)} %bitcast.180), calls=%async_computation.3 | async-start | bytes 8388608
  231.7 5.5 %slice-start.4 = ((s8[6291456]{0:T(1024)(128)(4,1)}), s8[2097152]{0:T(1024)(128)(4,1)S(1)}, s32[]{:S(2)}) async-start(s8[6291456]{0:T(1024)(128)(4,1)} %bitcast.180), calls=%async_computation.4 | async-start | bytes 4194304
  231.7 17.0 %slice-start.5 = ((s8[6291456]{0:T(1024)(128)(4,1)}), s8[4194304]{0:T(1024)(128)(4,1)S(1)}, s32[]{:S(2)}) async-start(s8[6291456]{0:T(1024)(128)(4,1)} %bitcast.184), calls=%async_computation.5 | async-start | bytes 8388608
  237.3 11.5 %slice-start.6 = ((s8[6291456]{0:T(1024)(128)(4,1)}), s8[2097152]{0:T(1024)(128)(4,1)S(1)}, s32[]{:S(2)}) async-start(s8[6291456]{0:T(1024)(128)(4,1)} %bitcast.184), calls=%async_computation.6 | async-start | bytes 4194304
  248.1 5.2 copy-start.18
  254.9 6.7 %copy-start.17 = (bf16[4,512,768]{2,1,0:T(8,128)(2,1)S(1)}, bf16[4,512,768]{2,1,0:T(8,128)(2,1)}, u32[]{:S(2)}) copy-start(bf16[4,512,768]{2,1,0:T(8,128)(2,1)} %get-tuple-element.120.refs_5_) | copy-start | bytes 9437188
  261.5 6.8 %copy-start.5 = (bf16[8,64,1024]{2,1,0:T(8,128)(2,1)S(1)}, bf16[8,64,1024]{2,1,0:T(8,128)(2,1)}, u32[]{:S(2)}) copy-start(bf16[8,64,1024]{2,1,0:T(8,128)(2,1)} %get-tuple-element.71) | copy-start | bytes 3145732
  268.3 2.6 copy-start.14
  270.0 5.2 copy-start.7
  270.9 4.3 copy-start.6
  419.3 101.7 %copy-start = (f32[11,128,256]{2,1,0:T(8,128)S(1)}, f32[11,128,256]{2,1,0:T(8,128)}, u32[]{:S(2)}) copy-start(f32[11,128,256]{2,1,0:T(8,128)} %get-tuple-element.84.ffn_ref) | copy-start | bytes 4325380
  419.3 101.7 %copy-start.1 = (bf16[8,64,1024]{2,1,0:T(8,128)(2,1)S(1)}, bf16[8,64,1024]{2,1,0:T(8,128)(2,1)}, u32[]{:S(2)}) copy-start(bf16[8,64,1024]{2,1,0:T(8,128)(2,1)} %get-tuple-element.93.y_ref) | copy-start | bytes 3145732
  521.0 1.2 copy-start.2
  (2 other events, 2.0 us)

commit v6 on v5

--- a/solution.py
+++ b/solution.py
@@ -952,10 +952,10 @@
     for copy in fetch(0, 0):
         copy.start()
 
-    @pl.loop(0, max(scatter.ticks, 2 + parts + bits + 2))
+    @pl.loop(0, max(scatter.ticks, 1 + parts + bits + 2))
     def _(now):
         scatter.tick(now)
-        tick = now - 2
+        tick = now - 1
 
         @pl.when((tick >= 0) & (tick < parts))
         def _():

time: 538 us -> 541 us (level)
  no operation moved by 1% of the time
where the time goes in v6:
time: 541 us; the launch traced here: 531 us
  Pallas kernels  456 us (84%)
  matrix products  51.3 us (9%)
  local copies, waits for them, and re-layouts  14.6 us (3%)
  other arithmetic  7.53 us (1%)
    pallas_call x1, Pallas kernels, backward_core(): pl.pallas_call(partial(backward_kernel, heads, parts, bits, plan, rows),...  137 us
    pallas_call x1, Pallas kernels, forward_core(): pl.pallas_call(partial(forward_kernel, heads, parts, bits, pieces), grid=...  123 us
    pallas_call x1, Pallas kernels, scatter_sum(): pl.pallas_call(partial(scatter_kernel, bits, parts, plan, rows), out_shap...  105 us
    pallas_call x1, Pallas kernels, prologue(): pl.pallas_call(partial(prologue_kernel, bits, parts, pieces), out_shape=(...  89.4 us
    dot_general x9, matrix products, dot(): return jnp.einsum(spec, a, b, preferred_element_type=F32)  51.3 us

profile of v6, /device:TPU:0, one launch (start us, length us, event | category | flops | bytes accessed | tf_op | source)
XLA Modules:
  0.0 530.7 jit_solution(10303491896253574961)
XLA Ops:
  1.9 89.4 %prologue.1 = (bf16[8,64,1024]{2,1,0:T(8,128)(2,1)}, bf16[4,8,128,1536]{3,2,1,0:T(8,128)(2,1)}, bf16[4,8,16,128]{3,2,1,0:T(8,128)(2,1)}, f32[4,512,1536]{2,1,0:T...) custom-call(bf16[8,64,1024]{2,1,0:T(8,128)(2,1)} %refs_0_.2, ...), custom_call_target="tpu_custom_call" | custom-call | flops 6442450944 | bytes 41943040 | tf_op jit(solution)/shard_map/prologue/pallas_call | solution.py:399
  91.4 1.7 fusion.20
  94.8 122.8 %delta_forward.1 = (bf16[4,512,512]{2,1,0:T(8,128)(2,1)}, f32[8,512,256]{2,1,0:T(8,128)}, f32[8,4,128,256]{3,2,1,0:T(8,128)}, f32[8,4,128,128]{3,2,1,0:T(8,128)}...) custom-call(f32[4,512,1536]{2,1,0:T(8,128)} %get-tuple-element.64.ra, ...), custom_call_target="tpu_custom_call" | custom-call | flops 20000000000 | bytes 41943040 | tf_op jit(solution)/shard_map/delta_forward/pallas_call | solution.py:1388
  219.0 1.6 multiply_convert_fusion.1
  220.6 8.6 %fusion.37 = f32[4,768,512]{1,2,0:T(8,128)} fusion(bf16[512,1024,1]{1,0,2:T(8,128)(2,1)S(1)} %bitcast.157, bf16[4,1024,768]{2,1,0:T(8,128)(2,1)} %bitcast.183), kind=kOutput, calls=%fused_computation.80 | convolution fusion | flops 3221225472 | bytes 13631488 | tf_op jit(solution)/shard_map/td,gdf->gtf/dot_general | solution.py:1530
  229.2 2.4 multiply_reduce_fusion.2
  231.8 5.5 %fusion.15 = f32[4,768,512]{1,2,0:T(8,128)} fusion(bf16[4,1024,768]{2,1,0:T(8,128)(2,1)S(1)} %bitcast.178, f32[512,1024]{1,0:T(8,128)S(1)} %get-tuple-element.132, f32[1024]{0:T(1024)S(1)} %copy-done.9, f32[512]{0:T(512)S(1)} %add_rsqrt_fusion), kind=kOutput, calls=%fused_computation.31 | convolution fusion | flops 3222798336 | bytes 14686208 | tf_op jit(solution)/shard_map/td,gdf->gtf/dot_general | solution.py:1530
  237.3 10.9 %fusion.9 = (bf16[4,512,768]{2,1,0:T(8,128)(2,1)S(1)}, bf16[4,512,768]{2,1,0:T(8,128)(2,1)}, bf16[4,512,768]{2,1,0:T(8,128)(2,1)}) fusion(f32[4,768,512]{1,2,0:T(8,128)} %fusion.15, f32[4,768,512]{1,2,0:T(8,128)} %fusion.37, bf16[4,1024,768]{2,1,0:T(8,128)(2,1)S(1)} %bitcast.182, f32[512,1024]{1,0:T(8,128)S(1)} %get-tuple-element.132, ...), kind=kOutput, calls=%fused_computation.13 | convolution fusion | flops 3247964160 | bytes 30414848 | tf_op jit(solution)/shard_map/td,gdf->gtf/dot_general | solution.py:1530
  248.8 4.5 fusion.12
  253.5 1.3 copy.58.refs_1_
  254.9 6.6 %fusion.36 = f32[512,1024,1]{1,0,2:T(8,128)S(1)} fusion(bf16[4,512,768]{2,1,0:T(8,128)(2,1)} %get-tuple-element.119.refs_4_, bf16[4,1024,768]{2,1,0:T(8,128)(2,1)} %bitcast.179), kind=kOutput, calls=%fused_computation.79 | convolution fusion | flops 3221225472 | bytes 11534336 | tf_op jit(solution)/shard_map/gtf,gdf->td/dot_general | solution.py:1530
  261.5 6.8 %multiply_reduce_fusion = (f32[1024]{0:T(1024)}, f32[512]{0:T(512)S(1)}, f32[512,1024]{1,0:T(8,128)S(1)}) fusion(f32[512,1024]{1,0:T(8,128)S(1)} %get-tuple-element.132, f32[512]{0:T(512)S(1)} %add_rsqrt_fusion, f32[1024]{0:T(1024)S(1)} %copy-done.9, bf16[4,512,768]{2,1,0:T(8,128)(2,1)S(1)} %copy-done.17, bf16[4,1024,768]{2,1,0:T(8,128)(2,1)} %bitcast.175, ...), kind=kOutput, calls=%fused_computation.23 | convolution fusion | flops 3224893952 | bytes 15740928 | tf_op jit(solution)/shard_map/gtf,gdf->td/dot_general | solution.py:1530
  268.3 1.7 convert_bitcast_fusion
  270.0 0.9 copy-done.14
  270.9 4.3 convolution_bitcast_fusion.dhead_ref
  275.2 1.3 copy.57.refs_0_
  276.5 1.3 copy.59.refs_2_
  277.8 137.0 %delta_backward.1 = (bf16[4,512,1536]{2,1,0:T(8,128)(2,1)}, f32[8,8,512]{2,1,0:T(8,128)}, f32[8,4,512]{2,1,0:T(4,128)}, f32[1,256]{1,0:T(1,128)}, f32[11,128,256]{2,1,0:T(8,128)}, /*index=5*/bf16[8,64,1024]{2,1,0:T(8,128)(2,1)}) custom-call(f32[4,512,512]{2,1,0:T(8,128)} %convolution_bitcast_fusion.dhead_ref, f32[8,512,256]{2,1,0:T(8,128)} %get-tuple-element.77.o_ref, ...), custom_call_target="tpu_custom_call" | custom-call | flops 40000000000 | bytes 62914560 | tf_op jit(solution)/shard_map/delta_backward/pallas_call | solution.py:1464
  414.9 1.1 slice_reduce_fusion.1
  419.3 104.5 %scatter_sum.1 = (f32[6,128,256]{2,1,0:T(8,128)}, f32[280,128]{1,0:T(8,128)}, bf16[8,64,1024]{2,1,0:T(8,128)(2,1)}) custom-call(bf16[1024,512]{1,0:T(8,128)(2,1)} %get-tuple-element.85.lhs_ref, bf16[4,512,1536]{2,1,0:T(8,128)(2,1)} %get-tuple-element.86.refs_0_, f32[1,1024]{1,0:T(1,128)} %bitcast.191, f32[1,256]{1,0:T(1,128)} %get-tuple-element.87.refs_2_, ...), custom_call_target="tpu_custom_call" | custom-call | flops 12884901888 | bytes 12582912 | tf_op jit(solution)/shard_map/scatter_sum/pallas_call | solution.py:1007
  523.8 1.2 copy-done.2
  525.0 1.1 copy-done.3
  526.2 0.9 copy-done.4
  527.1 2.2 assemble.1
  (85 shorter events, 9.6 us)
Async XLA Ops:
  1.9 91.2 %copy-start.11 = (f32[8]{0:T(128)S(1)}, f32[8]{0:T(128)}, u32[]{:S(2)}) copy-start(f32[8]{0:T(128)} %param.30) | copy-start | bytes 100
  1.9 91.2 %copy-start.10 = (f32[8]{0:T(128)S(1)}, f32[8]{0:T(128)}, u32[]{:S(2)}) copy-start(f32[8]{0:T(128)} %param.31) | copy-start | bytes 100
  1.9 92.2 %copy-start.8 = (f32[4,4096]{1,0:T(4,128)S(1)}, f32[4,4096]{1,0:T(4,128)}, u32[]{:S(2)}) copy-start(f32[4,4096]{1,0:T(4,128)} %param.29) | copy-start | bytes 196612
  1.9 92.2 %slice-start = ((f32[4,4096]{1,0:T(4,128)}), f32[4,2048]{1,0:T(4,128)S(1)}, s32[]{:S(2)}) async-start(f32[4,4096]{1,0:T(4,128)} %param.29), calls=%async_computation | async-start | bytes 65536 | tf_op jit(solution)/shard_map/slice | solution.py:1587
  94.8 122.9 %copy-start.12 = (s32[8]{0:T(128)S(1)}, s32[8]{0:T(128)}, u32[]{:S(2)}) copy-start(s32[8]{0:T(128)} %param.21) | copy-start | bytes 100
  218.9 12.8 %slice-start.1 = ((s8[6291456]{0:T(1024)(128)(4,1)}), s8[4194304]{0:T(1024)(128)(4,1)S(1)}, s32[]{:S(2)}) async-start(s8[6291456]{0:T(1024)(128)(4,1)} %bitcast.176), calls=%async_computation.1 | async-start | bytes 8388608
  220.6 8.6 %copy-start.13 = (bf16[4,8,128,512]{3,2,1,0:T(8,128)(2,1)S(1)}, bf16[4,8,128,512]{3,2,1,0:T(8,128)(2,1)}, u32[]{:S(2)}) copy-start(bf16[4,8,128,512]{3,2,1,0:T(8,128)(2,1)} %get-tuple-element.70) | copy-start | bytes 12582916
  220.6 8.6 %copy-start.15 = (bf16[8,64,1024]{2,1,0:T(8,128)(2,1)S(1)}, bf16[8,64,1024]{2,1,0:T(8,128)(2,1)}, u32[]{:S(2)}) copy-start(bf16[8,64,1024]{2,1,0:T(8,128)(2,1)} %get-tuple-element.72.refs_8_) | copy-start | bytes 3145732
  220.6 8.6 %copy-start.16 = (bf16[4,512,512]{2,1,0:T(8,128)(2,1)S(1)}, bf16[4,512,512]{2,1,0:T(8,128)(2,1)}, u32[]{:S(2)}) copy-start(bf16[4,512,512]{2,1,0:T(8,128)(2,1)} %get-tuple-element.73.refs_6_) | copy-start | bytes 6291460
  220.6 11.1 %slice-start.2 = ((s8[6291456]{0:T(1024)(128)(4,1)}), s8[2097152]{0:T(1024)(128)(4,1)S(1)}, s32[]{:S(2)}) async-start(s8[6291456]{0:T(1024)(128)(4,1)} %bitcast.176), calls=%async_computation.2 | async-start | bytes 4194304
  229.2 2.5 copy-start.9
  229.2 8.0 %slice-start.3 = ((s8[6291456]{0:T(1024)(128)(4,1)}), s8[4194304]{0:T(1024)(128)(4,1)S(1)}, s32[]{:S(2)}) async-start(s8[6291456]{0:T(1024)(128)(4,1)} %bitcast.180), calls=%async_computation.3 | async-start | bytes 8388608
  231.7 5.5 %slice-start.4 = ((s8[6291456]{0:T(1024)(128)(4,1)}), s8[2097152]{0:T(1024)(128)(4,1)S(1)}, s32[]{:S(2)}) async-start(s8[6291456]{0:T(1024)(128)(4,1)} %bitcast.180), calls=%async_computation.4 | async-start | bytes 4194304
  231.7 17.0 %slice-start.5 = ((s8[6291456]{0:T(1024)(128)(4,1)}), s8[4194304]{0:T(1024)(128)(4,1)S(1)}, s32[]{:S(2)}) async-start(s8[6291456]{0:T(1024)(128)(4,1)} %bitcast.184), calls=%async_computation.5 | async-start | bytes 8388608
  237.3 11.5 %slice-start.6 = ((s8[6291456]{0:T(1024)(128)(4,1)}), s8[2097152]{0:T(1024)(128)(4,1)S(1)}, s32[]{:S(2)}) async-start(s8[6291456]{0:T(1024)(128)(4,1)} %bitcast.184), calls=%async_computation.6 | async-start | bytes 4194304
  248.1 5.2 copy-start.18
  254.9 6.7 %copy-start.17 = (bf16[4,512,768]{2,1,0:T(8,128)(2,1)S(1)}, bf16[4,512,768]{2,1,0:T(8,128)(2,1)}, u32[]{:S(2)}) copy-start(bf16[4,512,768]{2,1,0:T(8,128)(2,1)} %get-tuple-element.120.refs_5_) | copy-start | bytes 9437188
  261.5 6.8 %copy-start.5 = (bf16[8,64,1024]{2,1,0:T(8,128)(2,1)S(1)}, bf16[8,64,1024]{2,1,0:T(8,128)(2,1)}, u32[]{:S(2)}) copy-start(bf16[8,64,1024]{2,1,0:T(8,128)(2,1)} %get-tuple-element.71) | copy-start | bytes 3145732
  268.3 2.6 copy-start.14
  270.0 5.2 copy-start.7
  270.9 4.3 copy-start.6
  419.3 104.5 %copy-start = (f32[11,128,256]{2,1,0:T(8,128)S(1)}, f32[11,128,256]{2,1,0:T(8,128)}, u32[]{:S(2)}) copy-start(f32[11,128,256]{2,1,0:T(8,128)} %get-tuple-element.84.ffn_ref) | copy-start | bytes 4325380
  419.3 104.5 %copy-start.1 = (bf16[8,64,1024]{2,1,0:T(8,128)(2,1)S(1)}, bf16[8,64,1024]{2,1,0:T(8,128)(2,1)}, u32[]{:S(2)}) copy-start(bf16[8,64,1024]{2,1,0:T(8,128)(2,1)} %get-tuple-element.93.y_ref) | copy-start | bytes 3145732
  523.8 1.2 copy-start.2
  (2 other events, 2.0 us)
